TPU v7x, 32 devices: a whole 2x2x4 slice. The times are simulated.
32 devices in a mesh: delay: 8 (over z, x), src: 2 (over y), tgt: 2 (over core).
Axes of the slice: x: 2, y: 2, z: 4, core: 2. Of those that a mesh axis runs over, the one named last changes fastest.
Arguments:
- blocks: bfloat16 [8, 2, 2, 32, 128, 128], P('delay', 'src', 'tgt'), may hold values from -0.15625 to 0.15625
- coords: int32 [8, 2, 2, 32, 2], P('delay', 'src', 'tgt'), may hold values from 0 to 31, as said below
- counts: int32 [8, 2, 2], P('delay', 'src', 'tgt'), may hold values from 16 to 32, as said below
- history: bfloat16 [8, 2, 4096, 128], P('delay', None, 'src'), may hold values from -6 to 6
- excitation: bfloat16 [2, 2, 4096, 128], P(None, 'tgt', 'src'), may hold values from -6 to 6
- inverse: bfloat16 [2, 32, 128, 128], P('tgt', 'src'), may hold values from -0.5 to 0.5
Outputs:
- currents: bfloat16 [2, 2, 4096, 128], P(None, 'tgt', 'src')
Inputs may be any that keep to these rules, and one draw needn't show every extreme that they name: `counts`: at most 32 used slots in a tile; in every draw some tile has exactly 32. `coords`: within one tile the 32 slots name distinct (row block, column block) pairs, row blocks below 32 and column blocks below 32; slots at or past the tile's count are not used.
All inputs are finite; a program needn't handle non-finite values.
Results may differ from a plain program's by a relative error of at most 0.017.
Values may be sent and summed in bfloat16 or wider, within the bound.
No kernel may reach another device: no remote copies, remote signals or barrier semaphores. Data moves between devices by JAX's collectives and lax.ppermute only.
A program may use at most 64 MiB of HBM per device.

v0:
```python
import jax
import jax.numpy as jnp
from jax import lax
from jax.sharding import PartitionSpec as P


def from_behind(array, axis, by):
    peers = lax.axis_size(axis)
    pairs = [(i, i + by) for i in range(peers) if 0 <= i + by < peers]
    return lax.ppermute(array, axis, pairs)


def shards(blocks, coords, counts, history, excitation, inverse):
    block_edge = blocks.shape[-1]
    slot_count = blocks.shape[3]
    halves = history.shape[1]
    owned_rows = history.shape[2]
    excite_cols = history.shape[3]
    tile_rows = owned_rows * lax.axis_size("src")
    row_count = tile_rows // block_edge
    col_count = halves * owned_rows // block_edge
    slot_blocks = blocks[0, 0, 0]
    slot_places = coords[0, 0, 0]
    live_slots = lax.iota(jnp.int32, slot_count) < counts[0, 0, 0]
    masked = jnp.where(live_slots[:, None, None], slot_blocks, jnp.zeros_like(slot_blocks))
    selector = (slot_places[:, 0][None, :] == lax.iota(jnp.int32, row_count)[:, None]).astype(
        jnp.float32
    )
    lagged = history[0]
    first_bin = lax.axis_index("delay") == 0
    step_count = excitation.shape[0]
    results = []
    for moment in range(step_count):
        pieces = lagged.reshape(col_count, block_edge, excite_cols)[slot_places[:, 1]]
        products = jnp.einsum("cij,cjw->ciw", masked, pieces, preferred_element_type=jnp.float32)
        summed = jnp.einsum("rc,ciw->riw", selector, products, precision=lax.Precision.HIGHEST)
        partial_value = summed.reshape(tile_rows, excite_cols)
        over_bins = lax.psum(partial_value.astype(jnp.bfloat16), "delay").astype(jnp.float32)
        field_rows = lax.psum_scatter(over_bins, "src", scatter_dimension=0, tiled=True)
        drive_rows = (excitation[moment, 0].astype(jnp.float32) - field_rows).astype(jnp.bfloat16)
        drive_rows = drive_rows.reshape(owned_rows // block_edge, block_edge, excite_cols)
        current = jnp.einsum(
            "bij,bjw->biw", inverse[0], drive_rows, preferred_element_type=jnp.float32
        )
        current = current.reshape(owned_rows, excite_cols).astype(jnp.bfloat16)
        results.append(current)
        if moment + 1 < step_count:
            newest = lax.all_gather(current[None], "tgt", axis=0, tiled=True)
            shifted = from_behind(lagged, "delay", 1)
            lagged = jnp.where(first_bin, newest, shifted)
    return jnp.stack(results)[:, None]


def solution(mesh):
    placed = (
        P("delay", "src", "tgt", None, None, None),
        P("delay", "src", "tgt", None, None),
        P("delay", "src", "tgt"),
        P("delay", None, "src", None),
        P(None, "tgt", "src", None),
        P("tgt", "src", None, None),
    )
    return jax.shard_map(
        shards, mesh=mesh, in_specs=placed, out_specs=P(None, "tgt", "src", None), check_vma=False
    )
```

profile of v0, /device:TPU:0, one launch (start us, length us, event | category | flops | bytes accessed | tf_op | source)
XLA Modules:
  0.0 273.0 jit_solution(8578539657994806504)
XLA Ops:
  6.5 0.0 copy-start
  6.5 0.0 copy-start.2
  6.5 0.0 all-reduce.3.cloned.1.call-start
  7.3 0.8 slice_bitcast_fusion
  8.1 2.0 gather_fusion
  10.1 0.0 copy-done.2
  10.1 0.5 fusion.15
  10.6 2.4 fusion.4
  13.0 1.4 copy.10
  14.4 0.0 all-reduce.3.cloned.1.call-update
  14.4 0.0 copy-start.3
  14.5 0.0 reduce-scatter.3.cloned.1.call-start
  14.5 81.0 %all-reduce.3.cloned.1.call-done = bf16[4096,128]{1,0:T(8,128)(2,1)} async-done(((bf16[4096,128]{1,0:T(8,128)(2,1)}), bf16[4096,128]{1,0:T(8,128)(2,1)}) %all-reduce.3.cloned.1.call-update) | async-done | bytes 1048592 | tf_op jit(solution)/shard_map/psum | solution.py:38
  95.5 2.7 convert_element_type.73
  98.2 0.0 reduce-scatter.3.cloned.1.call-update
  98.2 0.0 all-gather.2.cloned.1.call-start
  98.3 0.0 copy-done.3
  98.3 4.2 %collective-permute-start = (bf16[2,2048,128]{2,1,0:T(8,128)(2,1)S(1)}, bf16[2,2048,128]{2,1,0:T(8,128)(2,1)}, u32[]{:S(2)}, u32[]{:S(2)}) collective-permute-start(bf16[2,2048,128]{2,1,0:T(8,128)(2,1)S(1)} %bitcast.56), channel_id=1, source_target_pairs={{0,4},{4,8},{8,12},{12,16},{16,20},{20,24},{24,28},{1,5},{5,9},{9,... | collective-permute-start | bytes 3145736 | tf_op jit(solution)/shard_map/ppermute | solution.py:10
  102.4 27.4 %reduce-scatter.3.cloned.1.call-done = f32[2048,128]{1,0:T(8,128)} async-done(((f32[4096,128]{1,0:T(8,128)}), f32[2048,128]{1,0:T(8,128)}) %reduce-scatter.3.cloned.1.call-update) | async-done | bytes 1048592 | tf_op jit(solution)/shard_map/reduce_scatter | solution.py:39
  129.8 1.5 fusion.11
  131.3 0.0 copy-done
  131.3 1.1 convolution_convert_fusion.1
  132.4 0.0 all-gather.2.cloned.1.call-update
  132.4 0.0 all-reduce.5.cloned.1.call-start
  132.5 0.0 collective-permute-done
  132.5 9.1 %all-gather.2.cloned.1.call-done = bf16[2,2048,128]{2,1,0:T(8,128)(2,1)} async-done(((bf16[1,2048,128]{2,1,0:T(8,128)(2,1)}), bf16[2,2048,128]{2,1,0:T(8,128)(2,1)}) %all-gather.2.cloned.1.call-update) | async-done | bytes 1048592 | tf_op jit(solution)/shard_map/all_gather | solution.py:48
  141.6 2.3 broadcast_select_fusion
  143.9 2.0 gather_fusion.1
  145.9 0.5 fusion.14
  146.4 2.4 fusion.7
  148.8 1.4 copy.12
  150.2 0.0 all-reduce.5.cloned.1.call-update
  150.2 0.0 copy-start.4
  150.3 0.0 reduce-scatter.5.cloned.1.call-start
  150.3 79.2 %all-reduce.5.cloned.1.call-done = bf16[4096,128]{1,0:T(8,128)(2,1)} async-done(((bf16[4096,128]{1,0:T(8,128)(2,1)}), bf16[4096,128]{1,0:T(8,128)(2,1)}) %all-reduce.5.cloned.1.call-update) | async-done | bytes 1048592 | tf_op jit(solution)/shard_map/psum | solution.py:38
  229.5 2.7 convert_element_type.82
  232.2 0.0 reduce-scatter.5.cloned.1.call-update
  232.2 0.0 copy-start.1
  232.2 31.6 %reduce-scatter.5.cloned.1.call-done = f32[2048,128]{1,0:T(8,128)} async-done(((f32[4096,128]{1,0:T(8,128)}), f32[2048,128]{1,0:T(8,128)}) %reduce-scatter.5.cloned.1.call-update) | async-done | bytes 1048592 | tf_op jit(solution)/shard_map/reduce_scatter | solution.py:39
  263.8 0.0 copy-done.4
  263.8 1.3 fusion.10
  265.1 0.3 convolution_convert_fusion
  265.4 0.0 copy-done.1
  265.5 1.1 maximum_bitcast_fusion
  (2 shorter events, 0.0 us)
Async XLA Ops:
  6.5 124.7 %copy-start = (bf16[1,16,128,128]{3,2,1,0:T(8,128)(2,1)S(1)}, bf16[1,16,128,128]{3,2,1,0:T(8,128)(2,1)}, u32[]{:S(2)}) copy-start(bf16[1,16,128,128]{3,2,1,0:T(8,128)(2,1)} %param.11) | copy-start | bytes 1572868
  6.5 3.5 %copy-start.2 = (bf16[1,1,1,32,128,128]{5,4,3,2,1,0:T(8,128)(2,1)S(1)}, bf16[1,1,1,32,128,128]{5,4,3,2,1,0:T(8,128)(2,1)}, u32[]{:S(2)}) copy-start(bf16[1,1,1,32,128,128]{5,4,3,2,1,0:T(8,128)(2,1)} %param.6) | copy-start | bytes 3145732
  6.5 89.0 %all-reduce.3.cloned.1.call-start = ((), (), s32[]{:S(2)}) async-start(), calls=%async_computation.2 | async-start | bytes 2097152 | tf_op jit(solution)/shard_map/psum | solution.py:38
  14.4 83.8 %copy-start.3 = (bf16[1,2,2048,128]{3,2,1,0:T(8,128)(2,1)S(1)}, bf16[1,2,2048,128]{3,2,1,0:T(8,128)(2,1)}, u32[]{:S(2)}) copy-start(bf16[1,2,2048,128]{3,2,1,0:T(8,128)(2,1)} %param.9) | copy-start | bytes 3145732
  14.5 115.3 %reduce-scatter.3.cloned.1.call-start = ((), (), s32[]{:S(2)}) async-start(), calls=%async_computation.3 | async-start | bytes 3145728 | tf_op jit(solution)/shard_map/reduce_scatter | solution.py:39
  98.2 43.4 %all-gather.2.cloned.1.call-start = ((), (), s32[]{:S(2)}) async-start(), calls=%async_computation.4 | async-start | bytes 1572864 | tf_op jit(solution)/shard_map/all_gather | solution.py:48
  98.3 34.2 %collective-permute-start = (bf16[2,2048,128]{2,1,0:T(8,128)(2,1)S(1)}, bf16[2,2048,128]{2,1,0:T(8,128)(2,1)}, u32[]{:S(2)}, u32[]{:S(2)}) collective-permute-start(bf16[2,2048,128]{2,1,0:T(8,128)(2,1)S(1)} %bitcast.56), channel_id=1, source_target_pairs={{0,4},{4,8},{8,12},{12,16},{16,20},{20,24},{24,28},{1,5},{5,9},{9,... | collective-permute-start | bytes 3145736 | tf_op jit(solution)/shard_map/ppermute | solution.py:10
  132.4 97.1 %all-reduce.5.cloned.1.call-start = ((), (), s32[]{:S(2)}) async-start(), calls=%async_computation.5 | async-start | bytes 2097152 | tf_op jit(solution)/shard_map/psum | solution.py:38
  150.2 113.6 %copy-start.4 = (bf16[2,1,2048,128]{3,2,1,0:T(8,128)(2,1)S(1)}, bf16[2,1,2048,128]{3,2,1,0:T(8,128)(2,1)}, u32[]{:S(2)}) copy-start(bf16[2,1,2048,128]{3,2,1,0:T(8,128)(2,1)} %param.10) | copy-start | bytes 3145732
  150.3 113.6 %reduce-scatter.5.cloned.1.call-start = ((), (), s32[]{:S(2)}) async-start(), calls=%async_computation.6 | async-start | bytes 3145728 | tf_op jit(solution)/shard_map/reduce_scatter | solution.py:39
  232.2 33.2 %copy-start.1 = (bf16[16,128,128]{1,2,0:T(8,128)(2,1)S(1)}, bf16[16,128,128]{1,2,0:T(8,128)(2,1)}, u32[]{:S(2)}) copy-start(bf16[16,128,128]{1,2,0:T(8,128)(2,1)} %convolution_convert_fusion.1) | copy-start | bytes 1572868
Sparse Core Ops, SparseCore 0:
  14.6 80.8 all-reduce.2
  98.3 31.4 reduce-scatter.2
  132.5 9.0 all-gather.1
  150.4 79.1 all-reduce.4
  232.4 31.4 reduce-scatter.4
where the time goes:
time: 273 us
  waiting for transfers between devices  228 us (84%)
  between operations  14.1 us (5%)
  other arithmetic  12.3 us (5%)
  matrix products  7.27 us (3%)
  local copies, waits for them, and re-layouts  6.72 us (2%)
  starting transfers between devices  4.33 us (2%)
    psum x2, waiting for transfers between devices, shards(): lax.psum(partial_value.astype(jnp.bfloat16), 'delay').astype(jnp.float32)  160 us
    reduce_scatter x2, waiting for transfers between devices, shards(): lax.psum_scatter(over_bins, 'src', scatter_dimension=0, tiled=True)  58.9 us
    all_gather x1, waiting for transfers between devices, shards(): newest = lax.all_gather(current[None], 'tgt', axis=0, tiled=True)  9.13 us
  transfers between devices with their start and end apart: 6, of which 5 were waited for; matrix products, arithmetic and copies ran while one was open for 1% of the time, Pallas kernels for 0%

commit v1 on v0

v1 whole, which is shorter than its diff:
```python
import functools

import jax
import jax.numpy as jnp
from jax import lax
from jax.experimental import pallas as pl
from jax.experimental.pallas import tpu as pltpu
from jax.sharding import PartitionSpec as P

VMEM = pl.BlockSpec(memory_space=pltpu.VMEM)
SMEM = pl.BlockSpec(memory_space=pltpu.SMEM)
PARAMS = pltpu.CompilerParams(vmem_limit_bytes=48 * 1024 * 1024)
F32 = jnp.float32
BF16 = jnp.bfloat16


def exchange(array, axis, by):
    peers = lax.axis_size(axis)
    return lax.ppermute(array, axis, [(i, i ^ by) for i in range(peers)])


def call(kernel, outs, specs, scratch, *args):
    return pl.pallas_call(
        kernel,
        out_shape=outs,
        in_specs=specs,
        out_specs=[VMEM] * len(outs),
        scratch_shapes=scratch,
        compiler_params=PARAMS,
    )(*args)


class Plan:
    def __init__(self, blocks, history):
        self.edge = blocks.shape[-1]
        self.slots = blocks.shape[3]
        self.owned = history.shape[2]
        self.width = history.shape[3]
        self.srcs = lax.axis_size("src")
        self.bins = lax.axis_size("delay")
        self.halves = history.shape[1]
        owned_blocks = self.owned // self.edge
        self.groups = min(self.bins // 2, owned_blocks // 2)
        self.slice_rows = self.owned // (2 * self.groups)
        self.piece = self.slice_rows // 2
        self.tile_rows = self.owned * self.srcs
        self.slices = 2 * self.groups

    def x(self):
        return lax.axis_index("delay") & 1

    def g(self):
        return (lax.axis_index("delay") >> 1) & (self.groups - 1)

    def shape(self, *lead):
        return jax.ShapeDtypeStruct((*lead, self.piece, self.width), BF16)


def tile_product(p, acc, blocks, coords, counts, column):
    acc[...] = jnp.zeros_like(acc)

    def slot(c, carry):
        row = pl.multiple_of(coords[2 * c] * p.edge, p.edge)
        acc[pl.ds(row, p.edge)] += jnp.dot(
            blocks[c], column(coords[2 * c + 1]), preferred_element_type=F32
        )
        return carry

    lax.fori_loop(0, counts[0], slot, 0)


def split_first(p, acc, outs):
    src, x = lax.axis_index("src"), p.x()
    a_outs, b_send, b_keep = outs[: p.srcs], outs[p.srcs], outs[p.srcs + 1]
    unit = p.slice_rows

    def rows(s, xx, g, piece):
        start = ((s * 2 + xx) * p.groups + g) * unit + piece * p.piece
        return acc[pl.ds(pl.multiple_of(start, p.piece), p.piece)].astype(BF16)

    for k, ref in enumerate(a_outs):
        for xx in range(2):
            for g in range(p.groups):
                ref[xx, g] = rows(src ^ k, xx, g, 0)
    for s in range(p.srcs):
        for g in range(p.groups):
            b_send[s, g] = rows(s, x ^ 1, g, 1)
            b_keep[s, g] = rows(s, x, g, 1)


def first_kernel(p, blocks, coords, counts, history, *rest):
    *outs, own_half, acc = rest
    per_half = p.owned // p.edge
    own_half[...] = history[lax.axis_index("tgt")]

    def column(c):
        start = pl.multiple_of((c % per_half) * p.edge, p.edge)
        return history[c // per_half, pl.ds(start, p.edge)]

    tile_product(p, acc, blocks, coords, counts, column)
    split_first(p, acc, outs)


def later_kernel(p, blocks, coords, counts, own, other, *rest):
    *outs, acc = rest
    per_half = p.owned // p.edge
    half = lax.axis_index("tgt")

    def column(c):
        start = pl.multiple_of((c % per_half) * p.edge, p.edge)
        at = pl.ds(start, p.edge)
        return jnp.where(c // per_half == half, own[at], other[at])

    tile_product(p, acc, blocks, coords, counts, column)
    split_first(p, acc, outs)


def second_kernel(p, *refs):
    n = p.srcs
    a_keep, a_came = refs[0], refs[1:n]
    b_keep, b_came = refs[n], refs[n + 1]
    a_send, a_stay = refs[n + 2], refs[n + 3]
    b_outs = refs[n + 4 :]
    src, x = lax.axis_index("src"), p.x()

    def a_sum(xx):
        total = a_keep[xx].astype(F32)
        for came in a_came:
            total = total + came[xx].astype(F32)
        return total.astype(BF16)

    a_send[...] = a_sum(x ^ 1)
    a_stay[...] = a_sum(x)
    for k, ref in enumerate(b_outs):
        s = src ^ k
        ref[...] = (b_keep[s].astype(F32) + b_came[s].astype(F32)).astype(BF16)


def third_kernel(p, *refs):
    n = p.srcs
    a_keep, a_came, b_keep = refs[:3]
    b_came = refs[3 : n + 2]
    outs = refs[n + 2 :]
    mine = p.g()
    for k, ref in enumerate(outs):
        g = mine ^ k
        ref[0] = (a_keep[g].astype(F32) + a_came[g].astype(F32)).astype(BF16)
        total = b_keep[g].astype(F32)
        for came in b_came:
            total = total + came[g].astype(F32)
        ref[1] = total.astype(BF16)


def current_kernel(p, step, keep, *refs):
    *came, excitation, inverse, out = refs
    start = (p.x() * p.groups + p.g()) * p.slice_rows
    per_slice = p.slice_rows // p.edge
    field = keep[...].astype(F32)
    for ref in came:
        field = field + ref[...].astype(F32)
    field = field.reshape(p.slice_rows, p.width)
    at = pl.ds(pl.multiple_of(start, p.slice_rows), p.slice_rows)
    drive = (excitation[step, 0, at].astype(F32) - field).astype(BF16)
    first = (p.x() * p.groups + p.g()) * per_slice
    for b in range(per_slice):
        rows = slice(b * p.edge, (b + 1) * p.edge)
        out[rows] = jnp.dot(
            inverse[0, first + b], drive[rows], preferred_element_type=F32
        ).astype(BF16)


def place_of(p, k):
    low = (lax.axis_index("delay") & (p.slices - 1)) ^ k
    at = ((low & 1) * p.groups + (low >> 1)) * p.slice_rows
    return pl.ds(pl.multiple_of(at, p.slice_rows), p.slice_rows)


def join_kernel(p, *refs):
    *slices, shifted, out, lagged = refs
    for k, ref in enumerate(slices):
        out[place_of(p, k)] = ref[...]
    first_bin = lax.axis_index("delay") == 0

    @pl.when(first_bin)
    def _():
        lagged[...] = out[...]

    @pl.when(jnp.logical_not(first_bin))
    def _():
        lagged[...] = shifted[...]


def last_kernel(p, before, *refs):
    *slices, out = refs
    out[: before.shape[0], 0] = before[...]
    for k, ref in enumerate(slices):
        out[before.shape[0], 0, place_of(p, k)] = ref[...]


def field_sum(p, firsts):
    n = p.srcs
    a_keep, a_sends = firsts[0], firsts[1:n]
    b_send, b_keep = firsts[n], firsts[n + 1]
    a_came = [exchange(v, "src", k) for k, v in enumerate(a_sends, 1)]
    b_came = exchange(b_send, "delay", 1)
    one = p.shape(p.groups)
    a_send, a_stay, b_stay, *b_sends = call(
        functools.partial(second_kernel, p),
        [one] * (2 + n),
        [VMEM] * (n + 2),
        [],
        a_keep,
        *a_came,
        b_keep,
        b_came,
    )
    a_came = exchange(a_send, "delay", 1)
    b_came = [exchange(v, "src", k) for k, v in enumerate(b_sends, 1)]
    terms = call(
        functools.partial(third_kernel, p),
        [p.shape(2)] * p.groups,
        [VMEM] * (n + 2),
        [],
        a_stay,
        a_came,
        b_stay,
        *b_came,
    )
    by = 2 * p.groups
    while by < p.bins:
        terms = [
            (v.astype(F32) + exchange(v, "delay", by).astype(F32)).astype(BF16)
            for v in terms
        ]
        by *= 2
    keep, *sends = terms
    return [keep] + [exchange(v, "delay", 2 * k) for k, v in enumerate(sends, 1)]


def shards(blocks, coords, counts, history, excitation, inverse):
    p = Plan(blocks, history)
    steps = excitation.shape[0]
    slot_blocks = blocks.reshape(blocks.shape[3:])
    places = coords.reshape(-1)
    used = counts.reshape(-1)
    first_outs = (
        [p.shape(2, p.groups)] * p.srcs
        + [p.shape(p.srcs, p.groups)] * 2
    )
    half = jax.ShapeDtypeStruct((p.owned, p.width), BF16)
    acc = [pltpu.VMEM((p.tile_rows, p.width), F32)]
    *firsts, lagged = call(
        functools.partial(first_kernel, p),
        first_outs + [half],
        [VMEM, SMEM, SMEM, VMEM],
        acc,
        slot_blocks,
        places,
        used,
        history[0],
    )
    done = []
    for step in range(steps):
        terms = field_sum(p, firsts)
        piece = call(
            functools.partial(current_kernel, p, step),
            [jax.ShapeDtypeStruct((p.slice_rows, p.width), BF16)],
            [VMEM] * (len(terms) + 2),
            [],
            *terms,
            excitation,
            inverse,
        )[0]
        if step + 1 < steps:
            shifted = lax.ppermute(
                lagged, "delay", [(i, i + 1) for i in range(p.bins - 1)]
            )
        slices = [piece] + [exchange(piece, "delay", k) for k in range(1, p.slices)]
        if step + 1 == steps:
            return call(
                functools.partial(last_kernel, p),
                [jax.ShapeDtypeStruct((steps, 1, p.owned, p.width), BF16)],
                [VMEM] * (1 + len(slices)),
                [],
                jnp.stack(done),
                *slices,
            )[0]
        current, lagged = call(
            functools.partial(join_kernel, p),
            [half, half],
            [VMEM] * (len(slices) + 1),
            [],
            *slices,
            shifted,
        )
        done.append(current)
        other = exchange(lagged, "tgt", 1)
        firsts = call(
            functools.partial(later_kernel, p),
            first_outs,
            [VMEM, SMEM, SMEM, VMEM, VMEM],
            acc,
            slot_blocks,
            places,
            used,
            lagged,
            other,
        )


def solution(mesh):
    placed = (
        P("delay", "src", "tgt", None, None, None),
        P("delay", "src", "tgt", None, None),
        P("delay", "src", "tgt"),
        P("delay", None, "src", None),
        P(None, "tgt", "src", None),
        P("tgt", "src", None, None),
    )
    return jax.shard_map(
        shards, mesh=mesh, in_specs=placed, out_specs=P(None, "tgt", "src", None), check_vma=False
    )
```

time: 273 us -> 109 us (0.40)
  waiting for transfers between devices: 228 us -> 45.5 us
  starting transfers between devices: 4.33 us -> 47.7 us
  between operations: 14.1 us -> 0.81 us
  Pallas kernels: 0 us -> 12.3 us
  other arithmetic: 12.3 us -> 0 us
  matrix products: 7.27 us -> 0 us
  local copies, waits for them, and re-layouts: 6.72 us -> 2.66 us
    psum x2 -> x0, waiting for transfers between devices: 160 us -> none  [shards(): lax.psum(partial_value.astype(jnp.bfloat16), 'delay').astype(jnp.float32)]
    reduce_scatter x2 -> x0, waiting for transfers between devices: 58.9 us -> none  [shards(): lax.psum_scatter(over_bins, 'src', scatter_dimension=0, tiled=True)]
    ppermute x1 -> x30, waiting for transfers between devices: 0.01 us -> 45.5 us  [the longest x29 45.5 us: exchange(): return lax.ppermute(array, axis, [(i, i ^ by) for i in range(peers)])]
    ppermute x1 -> x30, starting transfers between devices: 4.16 us -> 47.7 us  [the longest x29 45.8 us: exchange(): return lax.ppermute(array, axis, [(i, i ^ by) for i in range(peers)])]
    pallas_call x0 -> x10, Pallas kernels: none -> 12.3 us  [call(): pl.pallas_call(kernel, out_shape=outs, in_specs=specs, out_specs=[VMEM] *...]
    all_gather x1 -> x0, waiting for transfers between devices: 9.13 us -> none  [shards(): newest = lax.all_gather(current[None], 'tgt', axis=0, tiled=True)]
    convert_element_type x4 -> x0, other arithmetic: 8.18 us -> none  [the longest x2 5.39 us: shards(): lax.psum(partial_value.astype(jnp.bfloat16), 'delay').astype(jnp.float32)]
    dot_general x6 -> x0, matrix products: 7.27 us -> none  [the longest x2 4.89 us: shards(): jnp.einsum('rc,ciw->riw', selector, products, precision=lax.Precision.HIG...]
  transfers between devices with their start and end apart: 6 -> 30, of which waited for: 5 -> 18; matrix products, arithmetic and copies ran while one was open for 1% -> 0% of each run, Pallas kernels for 0% -> 0%
where the time goes in v1:
time: 109 us
  starting transfers between devices  47.7 us (44%)
  waiting for transfers between devices  45.5 us (42%)
  Pallas kernels  12.3 us (11%)
  local copies, waits for them, and re-layouts  2.66 us (2%)
    ppermute x29, starting transfers between devices, exchange(): return lax.ppermute(array, axis, [(i, i ^ by) for i in range(peers)])  45.8 us
    ppermute x29, waiting for transfers between devices, exchange(): return lax.ppermute(array, axis, [(i, i ^ by) for i in range(peers)])  45.5 us
    pallas_call x10, Pallas kernels, call(): pl.pallas_call(kernel, out_shape=outs, in_specs=specs, out_specs=[VMEM] *...  12.3 us
    unnamed x13, local copies, waits for them, and re-layouts  2.56 us
  transfers between devices with their start and end apart: 30, of which 18 were waited for; matrix products, arithmetic and copies ran while one was open for 0% of the time, Pallas kernels for 0%

profile of v1, /device:TPU:0, one launch (start us, length us, event | category | flops | bytes accessed | tf_op | source)
XLA Modules:
  0.0 109.0 jit_solution(2912477021045228964)
XLA Ops:
  0.9 1.2 %copy-done.1 = bf16[1,1,1,32,128,128]{5,4,3,2,1,0:T(8,128)(2,1)S(1)} copy-done((bf16[1,1,1,32,128,128]{5,4,3,2,1,0:T(8,128)(2,1)S(1)}, bf16[1,1,1,32,128,128]{5,4,3,2,1,0:T(8,128)(2,1)}, u32[]{:S(2)}) %copy-start.1) | copy-done | bytes 1048600
  2.1 1.2 %copy-done.4 = bf16[1,2,2048,128]{3,2,1,0:T(8,128)(2,1)S(1)} copy-done((bf16[1,2,2048,128]{3,2,1,0:T(8,128)(2,1)S(1)}, bf16[1,2,2048,128]{3,2,1,0:T(8,128)(2,1)}, u32[]{:S(2)}) %copy-start.4) | copy-done | bytes 1048600
  3.3 5.2 %shard_map.64 = (bf16[2,4,128,128]{3,2,1,0:T(8,128)(2,1)S(1)}, bf16[2,4,128,128]{3,2,1,0:T(8,128)(2,1)S(1)}, bf16[2,4,128,128]{3,2,1,0:T(8,128)(2,1)S(1)}, bf16[...) custom-call(bf16[32,128,128]{2,1,0:T(8,128)(2,1)S(1)} %bitcast.8, s32[64]{0:T(128)S(1)} %reshape.10.coords, ...), custom_call_target="tpu_custom_call" | custom-call | tf_op jit(solution)/shard_map/pallas_call | solution.py:23
  8.5 1.3 %collective-permute-start = (bf16[2,4,128,128]{3,2,1,0:T(8,128)(2,1)S(1)}, bf16[2,4,128,128]{3,2,1,0:T(8,128)(2,1)S(1)}, u32[]{:S(2)}, u32[]{:S(2)}) collective-permute-start(bf16[2,4,128,128]{3,2,1,0:T(8,128)(2,1)S(1)} %get-tuple-element.33), channel_id=1, source_target_pairs={{0,2},{2,0},{1,3},{3,1},{4,6},{6,4},{5,7},{7,5},{8,10},{10,8},{9,1... | collective-permute-start | bytes 786440 | tf_op jit(solution)/shard_map/ppermute | solution.py:19
  9.9 2.1 %collective-permute-start.1 = (bf16[2,4,128,128]{3,2,1,0:T(8,128)(2,1)S(1)}, bf16[2,4,128,128]{3,2,1,0:T(8,128)(2,1)S(1)}, u32[]{:S(2)}, u32[]{:S(2)}) collective-permute-start(bf16[2,4,128,128]{3,2,1,0:T(8,128)(2,1)S(1)} %get-tuple-element.35), channel_id=1, source_target_pairs={{0,4},{4,0},{8,12},{12,8},{16,20},{20,16},{24,28},{28,24},{1,5},{5... | collective-permute-start | bytes 786440 | tf_op jit(solution)/shard_map/ppermute | solution.py:19
  11.9 1.9 %collective-permute-start.14 = (bf16[2048,128]{1,0:T(8,128)(2,1)S(1)}, bf16[2048,128]{1,0:T(8,128)(2,1)S(1)}, u32[]{:S(2)}, u32[]{:S(2)}) collective-permute-start(bf16[2048,128]{1,0:T(8,128)(2,1)S(1)} %get-tuple-element.44), channel_id=1, source_target_pairs={{0,4},{4,8},{8,12},{12,16},{16,20},{20,24},{24,28},{1,5},{5,9},{9,... | collective-permute-start | bytes 1572872 | tf_op jit(solution)/shard_map/ppermute | solution.py:275
  13.9 2.9 %collective-permute-done.refs_1_ = bf16[2,4,128,128]{3,2,1,0:T(8,128)(2,1)S(1)} collective-permute-done((bf16[2,4,128,128]{3,2,1,0:T(8,128)(2,1)S(1)}, bf16[2,4,128,128]{3,2,1,0:T(8,128)(2,1)S(1)}, u32[]{:S(2)}, u32[]{:S(2)}) %collective-permute-start) | collective-permute-done | bytes 262176 | tf_op jit(solution)/shard_map/ppermute | solution.py:19
  16.7 1.9 %collective-permute-done.1.refs_3_ = bf16[2,4,128,128]{3,2,1,0:T(8,128)(2,1)S(1)} collective-permute-done((bf16[2,4,128,128]{3,2,1,0:T(8,128)(2,1)S(1)}, bf16[2,4,128,128]{3,2,1,0:T(8,128)(2,1)S(1)}, u32[]{:S(2)}, u32[]{:S(2)}) %collective-permute-start.1) | collective-permute-done | bytes 262176 | tf_op jit(solution)/shard_map/ppermute | solution.py:19
  18.8 2.5 %collective-permute-start.2 = (bf16[4,128,128]{2,1,0:T(8,128)(2,1)S(1)}, bf16[4,128,128]{2,1,0:T(8,128)(2,1)S(1)}, u32[]{:S(2)}, u32[]{:S(2)}) collective-permute-start(bf16[4,128,128]{2,1,0:T(8,128)(2,1)S(1)} %get-tuple-element.37), channel_id=1, source_target_pairs={{0,4},{4,0},{8,12},{12,8},{16,20},{20,16},{24,28},{28,24},{1,5},{5... | collective-permute-start | bytes 393224 | tf_op jit(solution)/shard_map/ppermute | solution.py:19
  21.4 9.7 %collective-permute-done.2.refs_1_ = bf16[4,128,128]{2,1,0:T(8,128)(2,1)S(1)} collective-permute-done((bf16[4,128,128]{2,1,0:T(8,128)(2,1)S(1)}, bf16[4,128,128]{2,1,0:T(8,128)(2,1)S(1)}, u32[]{:S(2)}, u32[]{:S(2)}) %collective-permute-start.2) | collective-permute-done | bytes 131104 | tf_op jit(solution)/shard_map/ppermute | solution.py:19
  31.2 5.2 %collective-permute-start.4 = (bf16[2,128,128]{2,1,0:T(8,128)(2,1)S(1)}, bf16[2,128,128]{2,1,0:T(8,128)(2,1)S(1)}, u32[]{:S(2)}, u32[]{:S(2)}) collective-permute-start(bf16[2,128,128]{2,1,0:T(8,128)(2,1)S(1)} %get-tuple-element.41), channel_id=1, source_target_pairs={{0,8},{4,12},{8,0},{12,4},{16,24},{20,28},{24,16},{28,20},{1,9},{5... | collective-permute-start | bytes 196616 | tf_op jit(solution)/shard_map/ppermute | solution.py:19
  36.4 3.2 %collective-permute-start.5 = (bf16[2,128,128]{2,1,0:T(8,128)(2,1)S(1)}, bf16[2,128,128]{2,1,0:T(8,128)(2,1)S(1)}, u32[]{:S(2)}, u32[]{:S(2)}) collective-permute-start(bf16[2,128,128]{2,1,0:T(8,128)(2,1)S(1)} %get-tuple-element.42), channel_id=1, source_target_pairs={{0,16},{4,20},{8,24},{12,28},{16,0},{20,4},{24,8},{28,12},{1,17},{... | collective-permute-start | bytes 196616 | tf_op jit(solution)/shard_map/ppermute | solution.py:19
  39.5 0.6 collective-permute-start.6
  40.1 1.6 %collective-permute-done.5.refs_1_ = bf16[2,128,128]{2,1,0:T(8,128)(2,1)S(1)} collective-permute-done((bf16[2,128,128]{2,1,0:T(8,128)(2,1)S(1)}, bf16[2,128,128]{2,1,0:T(8,128)(2,1)S(1)}, u32[]{:S(2)}, u32[]{:S(2)}) %collective-permute-start.5) | collective-permute-done | bytes 65568 | tf_op jit(solution)/shard_map/ppermute | solution.py:19
  41.8 3.9 %collective-permute-done.6.refs_2_ = bf16[2,128,128]{2,1,0:T(8,128)(2,1)S(1)} collective-permute-done((bf16[2,128,128]{2,1,0:T(8,128)(2,1)S(1)}, bf16[2,128,128]{2,1,0:T(8,128)(2,1)S(1)}, u32[]{:S(2)}, u32[]{:S(2)}) %collective-permute-start.6) | collective-permute-done | bytes 65568 | tf_op jit(solution)/shard_map/ppermute | solution.py:19
  45.7 0.2 shard_map.67.refs_0_
  45.9 2.7 %collective-permute-start.13 = (bf16[256,128]{1,0:T(8,128)(2,1)S(1)}, bf16[256,128]{1,0:T(8,128)(2,1)S(1)}, u32[]{:S(2)}, u32[]{:S(2)}) collective-permute-start(bf16[256,128]{1,0:T(8,128)(2,1)S(1)} %shard_map.67.refs_0_), channel_id=1, source_target_pairs={{0,28},{4,24},{8,20},{12,16},{16,12},{20,8},{24,4},{28,0},{1,29},{... | collective-permute-start | bytes 196616 | tf_op jit(solution)/shard_map/ppermute | solution.py:19
  48.6 3.1 %collective-permute-start.12 = (bf16[256,128]{1,0:T(8,128)(2,1)S(1)}, bf16[256,128]{1,0:T(8,128)(2,1)S(1)}, u32[]{:S(2)}, u32[]{:S(2)}) collective-permute-start(bf16[256,128]{1,0:T(8,128)(2,1)S(1)} %shard_map.67.refs_0_), channel_id=1, source_target_pairs={{0,24},{4,28},{8,16},{12,20},{16,8},{20,12},{24,0},{28,4},{1,25},{... | collective-permute-start | bytes 196616 | tf_op jit(solution)/shard_map/ppermute | solution.py:19
  51.7 1.9 %collective-permute-start.10 = (bf16[256,128]{1,0:T(8,128)(2,1)S(1)}, bf16[256,128]{1,0:T(8,128)(2,1)S(1)}, u32[]{:S(2)}, u32[]{:S(2)}) collective-permute-start(bf16[256,128]{1,0:T(8,128)(2,1)S(1)} %shard_map.67.refs_0_), channel_id=1, source_target_pairs={{0,16},{4,20},{8,24},{12,28},{16,0},{20,4},{24,8},{28,12},{1,17},{... | collective-permute-start | bytes 196616 | tf_op jit(solution)/shard_map/ppermute | solution.py:19
  53.6 2.0 %collective-permute-start.9 = (bf16[256,128]{1,0:T(8,128)(2,1)S(1)}, bf16[256,128]{1,0:T(8,128)(2,1)S(1)}, u32[]{:S(2)}, u32[]{:S(2)}) collective-permute-start(bf16[256,128]{1,0:T(8,128)(2,1)S(1)} %shard_map.67.refs_0_), channel_id=1, source_target_pairs={{0,12},{4,8},{8,4},{12,0},{16,28},{20,24},{24,20},{28,16},{1,13},{... | collective-permute-start | bytes 196616 | tf_op jit(solution)/shard_map/ppermute | solution.py:19
  55.6 2.4 %collective-permute-start.8 = (bf16[256,128]{1,0:T(8,128)(2,1)S(1)}, bf16[256,128]{1,0:T(8,128)(2,1)S(1)}, u32[]{:S(2)}, u32[]{:S(2)}) collective-permute-start(bf16[256,128]{1,0:T(8,128)(2,1)S(1)} %shard_map.67.refs_0_), channel_id=1, source_target_pairs={{0,8},{4,12},{8,0},{12,4},{16,24},{20,28},{24,16},{28,20},{1,9},{5... | collective-permute-start | bytes 196616 | tf_op jit(solution)/shard_map/ppermute | solution.py:19
  57.9 0.8 collective-permute-done.11.refs_5_
  58.8 0.8 collective-permute-start.7
  59.6 0.9 collective-permute-done.8.refs_2_
  60.5 2.5 %collective-permute-done.7.refs_1_ = bf16[256,128]{1,0:T(8,128)(2,1)S(1)} collective-permute-done((bf16[256,128]{1,0:T(8,128)(2,1)S(1)}, bf16[256,128]{1,0:T(8,128)(2,1)S(1)}, u32[]{:S(2)}, u32[]{:S(2)}) %collective-permute-start.7) | collective-permute-done | bytes 65568 | tf_op jit(solution)/shard_map/ppermute | solution.py:19
  63.2 1.9 %collective-permute-done.15.other = bf16[2048,128]{1,0:T(8,128)(2,1)S(1)} collective-permute-done((bf16[2048,128]{1,0:T(8,128)(2,1)S(1)}, bf16[2048,128]{1,0:T(8,128)(2,1)S(1)}, u32[]{:S(2)}, u32[]{:S(2)}) %collective-permute-start.15) | collective-permute-done | bytes 524320 | tf_op jit(solution)/shard_map/ppermute | solution.py:19
  65.1 5.2 %shard_map.69 = (bf16[2,4,128,128]{3,2,1,0:T(8,128)(2,1)S(1)}, bf16[2,4,128,128]{3,2,1,0:T(8,128)(2,1)S(1)}, bf16[2,4,128,128]{3,2,1,0:T(8,128)(2,1)S(1)}, bf16[2,4,128,128]{3,2,1,0:T(8,128)(2,1)S(1)}) custom-call(bf16[32,128,128]{2,1,0:T(8,128)(2,1)S(1)} %bitcast.9, s32[64]{0:T(128)S(1)} %reshape.10.coords, s32[1]{0:T(128)} %bitcast.7.counts, ...), custom_call_target="tpu_custom_call" | custom-call | tf_op jit(solution)/shard_map/pallas_call | solution.py:23
  70.4 0.3 collective-permute-start.17
  70.8 6.1 %collective-permute-done.16.refs_1_ = bf16[2,4,128,128]{3,2,1,0:T(8,128)(2,1)S(1)} collective-permute-done((bf16[2,4,128,128]{3,2,1,0:T(8,128)(2,1)S(1)}, bf16[2,4,128,128]{3,2,1,0:T(8,128)(2,1)S(1)}, u32[]{:S(2)}, u32[]{:S(2)}) %collective-permute-start.16) | collective-permute-done | bytes 262176 | tf_op jit(solution)/shard_map/ppermute | solution.py:19
  76.9 1.2 %collective-permute-done.17.refs_3_ = bf16[2,4,128,128]{3,2,1,0:T(8,128)(2,1)S(1)} collective-permute-done((bf16[2,4,128,128]{3,2,1,0:T(8,128)(2,1)S(1)}, bf16[2,4,128,128]{3,2,1,0:T(8,128)(2,1)S(1)}, u32[]{:S(2)}, u32[]{:S(2)}) %collective-permute-start.17) | collective-permute-done | bytes 262176 | tf_op jit(solution)/shard_map/ppermute | solution.py:19
  78.2 0.7 collective-permute-start.18
  78.9 1.3 %collective-permute-start.19 = (bf16[4,128,128]{2,1,0:T(8,128)(2,1)S(1)}, bf16[4,128,128]{2,1,0:T(8,128)(2,1)S(1)}, u32[]{:S(2)}, u32[]{:S(2)}) collective-permute-start(bf16[4,128,128]{2,1,0:T(8,128)(2,1)S(1)} %get-tuple-element.54), channel_id=1, source_target_pairs={{0,2},{2,0},{1,3},{3,1},{4,6},{6,4},{5,7},{7,5},{8,10},{10,8},{9,1... | collective-permute-start | bytes 393224 | tf_op jit(solution)/shard_map/ppermute | solution.py:19
  80.2 3.1 %collective-permute-done.18.refs_1_ = bf16[4,128,128]{2,1,0:T(8,128)(2,1)S(1)} collective-permute-done((bf16[4,128,128]{2,1,0:T(8,128)(2,1)S(1)}, bf16[4,128,128]{2,1,0:T(8,128)(2,1)S(1)}, u32[]{:S(2)}, u32[]{:S(2)}) %collective-permute-start.18) | collective-permute-done | bytes 131104 | tf_op jit(solution)/shard_map/ppermute | solution.py:19
  83.2 0.6 collective-permute-done.19.refs_3_
  84.0 3.3 %collective-permute-start.21 = (bf16[2,128,128]{2,1,0:T(8,128)(2,1)S(1)}, bf16[2,128,128]{2,1,0:T(8,128)(2,1)S(1)}, u32[]{:S(2)}, u32[]{:S(2)}) collective-permute-start(bf16[2,128,128]{2,1,0:T(8,128)(2,1)S(1)} %get-tuple-element.57), channel_id=1, source_target_pairs={{0,16},{4,20},{8,24},{12,28},{16,0},{20,4},{24,8},{28,12},{1,17},{... | collective-permute-start | bytes 196616 | tf_op jit(solution)/shard_map/ppermute | solution.py:19
  87.3 1.1 collective-permute-start.22
  88.4 1.1 %collective-permute-done.21.refs_1_ = bf16[2,128,128]{2,1,0:T(8,128)(2,1)S(1)} collective-permute-done((bf16[2,128,128]{2,1,0:T(8,128)(2,1)S(1)}, bf16[2,128,128]{2,1,0:T(8,128)(2,1)S(1)}, u32[]{:S(2)}, u32[]{:S(2)}) %collective-permute-start.21) | collective-permute-done | bytes 65568 | tf_op jit(solution)/shard_map/ppermute | solution.py:19
  89.5 3.9 %collective-permute-done.22.refs_2_ = bf16[2,128,128]{2,1,0:T(8,128)(2,1)S(1)} collective-permute-done((bf16[2,128,128]{2,1,0:T(8,128)(2,1)S(1)}, bf16[2,128,128]{2,1,0:T(8,128)(2,1)S(1)}, u32[]{:S(2)}, u32[]{:S(2)}) %collective-permute-start.22) | collective-permute-done | bytes 65568 | tf_op jit(solution)/shard_map/ppermute | solution.py:19
  93.5 0.2 shard_map.72.refs_0_
  93.6 1.9 %collective-permute-start.29 = (bf16[256,128]{1,0:T(8,128)(2,1)S(1)}, bf16[256,128]{1,0:T(8,128)(2,1)S(1)}, u32[]{:S(2)}, u32[]{:S(2)}) collective-permute-start(bf16[256,128]{1,0:T(8,128)(2,1)S(1)} %shard_map.72.refs_0_), channel_id=1, source_target_pairs={{0,28},{4,24},{8,20},{12,16},{16,12},{20,8},{24,4},{28,0},{1,29},{... | collective-permute-start | bytes 196616 | tf_op jit(solution)/shard_map/ppermute | solution.py:19
  95.5 1.8 %collective-permute-start.28 = (bf16[256,128]{1,0:T(8,128)(2,1)S(1)}, bf16[256,128]{1,0:T(8,128)(2,1)S(1)}, u32[]{:S(2)}, u32[]{:S(2)}) collective-permute-start(bf16[256,128]{1,0:T(8,128)(2,1)S(1)} %shard_map.72.refs_0_), channel_id=1, source_target_pairs={{0,24},{4,28},{8,16},{12,20},{16,8},{20,12},{24,0},{28,4},{1,25},{... | collective-permute-start | bytes 196616 | tf_op jit(solution)/shard_map/ppermute | solution.py:19
  97.3 4.0 %collective-permute-start.26 = (bf16[256,128]{1,0:T(8,128)(2,1)S(1)}, bf16[256,128]{1,0:T(8,128)(2,1)S(1)}, u32[]{:S(2)}, u32[]{:S(2)}) collective-permute-start(bf16[256,128]{1,0:T(8,128)(2,1)S(1)} %shard_map.72.refs_0_), channel_id=1, source_target_pairs={{0,16},{4,20},{8,24},{12,28},{16,0},{20,4},{24,8},{28,12},{1,17},{... | collective-permute-start | bytes 196616 | tf_op jit(solution)/shard_map/ppermute | solution.py:19
  101.4 1.8 %collective-permute-start.24 = (bf16[256,128]{1,0:T(8,128)(2,1)S(1)}, bf16[256,128]{1,0:T(8,128)(2,1)S(1)}, u32[]{:S(2)}, u32[]{:S(2)}) collective-permute-start(bf16[256,128]{1,0:T(8,128)(2,1)S(1)} %shard_map.72.refs_0_), channel_id=1, source_target_pairs={{0,8},{4,12},{8,0},{12,4},{16,24},{20,28},{24,16},{28,20},{1,9},{5... | collective-permute-start | bytes 196616 | tf_op jit(solution)/shard_map/ppermute | solution.py:19
  103.2 1.7 %collective-permute-start.23 = (bf16[256,128]{1,0:T(8,128)(2,1)S(1)}, bf16[256,128]{1,0:T(8,128)(2,1)S(1)}, u32[]{:S(2)}, u32[]{:S(2)}) collective-permute-start(bf16[256,128]{1,0:T(8,128)(2,1)S(1)} %shard_map.72.refs_0_), channel_id=1, source_target_pairs={{0,4},{4,0},{8,12},{12,8},{16,20},{20,16},{24,28},{28,24},{1,5},{5... | collective-permute-start | bytes 196616 | tf_op jit(solution)/shard_map/ppermute | solution.py:19
  104.9 1.0 collective-permute-done.27.refs_5_
  105.9 1.4 %collective-permute-done.25.refs_3_ = bf16[256,128]{1,0:T(8,128)(2,1)S(1)} collective-permute-done((bf16[256,128]{1,0:T(8,128)(2,1)S(1)}, bf16[256,128]{1,0:T(8,128)(2,1)S(1)}, u32[]{:S(2)}, u32[]{:S(2)}) %collective-permute-start.25) | collective-permute-done | bytes 65568 | tf_op jit(solution)/shard_map/ppermute | solution.py:19
  107.3 0.6 collective-permute-done.23.refs_1_
  108.0 1.0 shard_map.73
  (36 shorter events, 1.0 us)
Async XLA Ops:
  0.0 0.7 copy-start.5
  0.9 1.2 %copy-start.1 = (bf16[1,1,1,32,128,128]{5,4,3,2,1,0:T(8,128)(2,1)S(1)}, bf16[1,1,1,32,128,128]{5,4,3,2,1,0:T(8,128)(2,1)}, u32[]{:S(2)}) copy-start(bf16[1,1,1,32,128,128]{5,4,3,2,1,0:T(8,128)(2,1)} %param.6) | copy-start | bytes 3145732
  2.1 1.2 %copy-start.4 = (bf16[1,2,2048,128]{3,2,1,0:T(8,128)(2,1)S(1)}, bf16[1,2,2048,128]{3,2,1,0:T(8,128)(2,1)}, u32[]{:S(2)}) copy-start(bf16[1,2,2048,128]{3,2,1,0:T(8,128)(2,1)} %param.9) | copy-start | bytes 3145732
  8.5 37.2 %copy-start = (bf16[2,1,2048,128]{3,2,1,0:T(8,128)(2,1)S(1)}, bf16[2,1,2048,128]{3,2,1,0:T(8,128)(2,1)}, u32[]{:S(2)}) copy-start(bf16[2,1,2048,128]{3,2,1,0:T(8,128)(2,1)} %refs_3_.3) | copy-start | bytes 3145732
  8.5 8.2 %collective-permute-start = (bf16[2,4,128,128]{3,2,1,0:T(8,128)(2,1)S(1)}, bf16[2,4,128,128]{3,2,1,0:T(8,128)(2,1)S(1)}, u32[]{:S(2)}, u32[]{:S(2)}) collective-permute-start(bf16[2,4,128,128]{3,2,1,0:T(8,128)(2,1)S(1)} %get-tuple-element.33), channel_id=1, source_target_pairs={{0,2},{2,0},{1,3},{3,1},{4,6},{6,4},{5,7},{7,5},{8,10},{10,8},{9,1... | collective-permute-start | bytes 786440 | tf_op jit(solution)/shard_map/ppermute | solution.py:19
  9.9 8.8 %collective-permute-start.1 = (bf16[2,4,128,128]{3,2,1,0:T(8,128)(2,1)S(1)}, bf16[2,4,128,128]{3,2,1,0:T(8,128)(2,1)S(1)}, u32[]{:S(2)}, u32[]{:S(2)}) collective-permute-start(bf16[2,4,128,128]{3,2,1,0:T(8,128)(2,1)S(1)} %get-tuple-element.35), channel_id=1, source_target_pairs={{0,4},{4,0},{8,12},{12,8},{16,20},{20,16},{24,28},{28,24},{1,5},{5... | collective-permute-start | bytes 786440 | tf_op jit(solution)/shard_map/ppermute | solution.py:19
  11.9 51.1 %collective-permute-start.14 = (bf16[2048,128]{1,0:T(8,128)(2,1)S(1)}, bf16[2048,128]{1,0:T(8,128)(2,1)S(1)}, u32[]{:S(2)}, u32[]{:S(2)}) collective-permute-start(bf16[2048,128]{1,0:T(8,128)(2,1)S(1)} %get-tuple-element.44), channel_id=1, source_target_pairs={{0,4},{4,8},{8,12},{12,16},{16,20},{20,24},{24,28},{1,5},{5,9},{9,... | collective-permute-start | bytes 1572872 | tf_op jit(solution)/shard_map/ppermute | solution.py:275
  18.8 26.9 %copy-start.3 = (bf16[1,16,128,128]{3,2,1,0:T(8,128)(2,1)S(1)}, bf16[1,16,128,128]{3,2,1,0:T(8,128)(2,1)}, u32[]{:S(2)}) copy-start(bf16[1,16,128,128]{3,2,1,0:T(8,128)(2,1)} %refs_4_.3) | copy-start | bytes 1572868
  18.8 12.3 %collective-permute-start.2 = (bf16[4,128,128]{2,1,0:T(8,128)(2,1)S(1)}, bf16[4,128,128]{2,1,0:T(8,128)(2,1)S(1)}, u32[]{:S(2)}, u32[]{:S(2)}) collective-permute-start(bf16[4,128,128]{2,1,0:T(8,128)(2,1)S(1)} %get-tuple-element.37), channel_id=1, source_target_pairs={{0,4},{4,0},{8,12},{12,8},{16,20},{20,16},{24,28},{28,24},{1,5},{5... | collective-permute-start | bytes 393224 | tf_op jit(solution)/shard_map/ppermute | solution.py:19
  21.4 9.7 %collective-permute-start.3 = (bf16[4,128,128]{2,1,0:T(8,128)(2,1)S(1)}, bf16[4,128,128]{2,1,0:T(8,128)(2,1)S(1)}, u32[]{:S(2)}, u32[]{:S(2)}) collective-permute-start(bf16[4,128,128]{2,1,0:T(8,128)(2,1)S(1)} %get-tuple-element.39), channel_id=1, source_target_pairs={{0,2},{2,0},{1,3},{3,1},{4,6},{6,4},{5,7},{7,5},{8,10},{10,8},{9,1... | collective-permute-start | bytes 393224 | tf_op jit(solution)/shard_map/ppermute | solution.py:19
  31.2 9.0 %collective-permute-start.4 = (bf16[2,128,128]{2,1,0:T(8,128)(2,1)S(1)}, bf16[2,128,128]{2,1,0:T(8,128)(2,1)S(1)}, u32[]{:S(2)}, u32[]{:S(2)}) collective-permute-start(bf16[2,128,128]{2,1,0:T(8,128)(2,1)S(1)} %get-tuple-element.41), channel_id=1, source_target_pairs={{0,8},{4,12},{8,0},{12,4},{16,24},{20,28},{24,16},{28,20},{1,9},{5... | collective-permute-start | bytes 196616 | tf_op jit(solution)/shard_map/ppermute | solution.py:19
  36.4 5.4 %collective-permute-start.5 = (bf16[2,128,128]{2,1,0:T(8,128)(2,1)S(1)}, bf16[2,128,128]{2,1,0:T(8,128)(2,1)S(1)}, u32[]{:S(2)}, u32[]{:S(2)}) collective-permute-start(bf16[2,128,128]{2,1,0:T(8,128)(2,1)S(1)} %get-tuple-element.42), channel_id=1, source_target_pairs={{0,16},{4,20},{8,24},{12,28},{16,0},{20,4},{24,8},{28,12},{1,17},{... | collective-permute-start | bytes 196616 | tf_op jit(solution)/shard_map/ppermute | solution.py:19
  39.5 6.2 %collective-permute-start.6 = (bf16[2,128,128]{2,1,0:T(8,128)(2,1)S(1)}, bf16[2,128,128]{2,1,0:T(8,128)(2,1)S(1)}, u32[]{:S(2)}, u32[]{:S(2)}) collective-permute-start(bf16[2,128,128]{2,1,0:T(8,128)(2,1)S(1)} %get-tuple-element.43), channel_id=1, source_target_pairs={{0,24},{4,28},{8,16},{12,20},{16,8},{20,12},{24,0},{28,4},{1,25},{... | collective-permute-start | bytes 196616 | tf_op jit(solution)/shard_map/ppermute | solution.py:19
  45.7 19.4 %copy-start.2 = (bf16[1,1,1,32,128,128]{5,4,3,2,1,0:T(8,128)(2,1)S(1)}, bf16[1,1,1,32,128,128]{5,4,3,2,1,0:T(8,128)(2,1)}, u32[]{:S(2)}) copy-start(bf16[1,1,1,32,128,128]{5,4,3,2,1,0:T(8,128)(2,1)} %param.6) | copy-start | bytes 3145732
  45.9 7.7 %collective-permute-start.13 = (bf16[256,128]{1,0:T(8,128)(2,1)S(1)}, bf16[256,128]{1,0:T(8,128)(2,1)S(1)}, u32[]{:S(2)}, u32[]{:S(2)}) collective-permute-start(bf16[256,128]{1,0:T(8,128)(2,1)S(1)} %shard_map.67.refs_0_), channel_id=1, source_target_pairs={{0,28},{4,24},{8,20},{12,16},{16,12},{20,8},{24,4},{28,0},{1,29},{... | collective-permute-start | bytes 196616 | tf_op jit(solution)/shard_map/ppermute | solution.py:19
  48.6 7.0 %collective-permute-start.12 = (bf16[256,128]{1,0:T(8,128)(2,1)S(1)}, bf16[256,128]{1,0:T(8,128)(2,1)S(1)}, u32[]{:S(2)}, u32[]{:S(2)}) collective-permute-start(bf16[256,128]{1,0:T(8,128)(2,1)S(1)} %shard_map.67.refs_0_), channel_id=1, source_target_pairs={{0,24},{4,28},{8,16},{12,20},{16,8},{20,12},{24,0},{28,4},{1,25},{... | collective-permute-start | bytes 196616 | tf_op jit(solution)/shard_map/ppermute | solution.py:19
  51.7 7.0 %collective-permute-start.11 = (bf16[256,128]{1,0:T(8,128)(2,1)S(1)}, bf16[256,128]{1,0:T(8,128)(2,1)S(1)}, u32[]{:S(2)}, u32[]{:S(2)}) collective-permute-start(bf16[256,128]{1,0:T(8,128)(2,1)S(1)} %shard_map.67.refs_0_), channel_id=1, source_target_pairs={{0,20},{4,16},{8,28},{12,24},{16,4},{20,0},{24,12},{28,8},{1,21},{... | collective-permute-start | bytes 196616 | tf_op jit(solution)/shard_map/ppermute | solution.py:19
  51.7 7.8 %collective-permute-start.10 = (bf16[256,128]{1,0:T(8,128)(2,1)S(1)}, bf16[256,128]{1,0:T(8,128)(2,1)S(1)}, u32[]{:S(2)}, u32[]{:S(2)}) collective-permute-start(bf16[256,128]{1,0:T(8,128)(2,1)S(1)} %shard_map.67.refs_0_), channel_id=1, source_target_pairs={{0,16},{4,20},{8,24},{12,28},{16,0},{20,4},{24,8},{28,12},{1,17},{... | collective-permute-start | bytes 196616 | tf_op jit(solution)/shard_map/ppermute | solution.py:19
  53.6 5.9 %collective-permute-start.9 = (bf16[256,128]{1,0:T(8,128)(2,1)S(1)}, bf16[256,128]{1,0:T(8,128)(2,1)S(1)}, u32[]{:S(2)}, u32[]{:S(2)}) collective-permute-start(bf16[256,128]{1,0:T(8,128)(2,1)S(1)} %shard_map.67.refs_0_), channel_id=1, source_target_pairs={{0,12},{4,8},{8,4},{12,0},{16,28},{20,24},{24,20},{28,16},{1,13},{... | collective-permute-start | bytes 196616 | tf_op jit(solution)/shard_map/ppermute | solution.py:19
  55.6 4.9 %collective-permute-start.8 = (bf16[256,128]{1,0:T(8,128)(2,1)S(1)}, bf16[256,128]{1,0:T(8,128)(2,1)S(1)}, u32[]{:S(2)}, u32[]{:S(2)}) collective-permute-start(bf16[256,128]{1,0:T(8,128)(2,1)S(1)} %shard_map.67.refs_0_), channel_id=1, source_target_pairs={{0,8},{4,12},{8,0},{12,4},{16,24},{20,28},{24,16},{28,20},{1,9},{5... | collective-permute-start | bytes 196616 | tf_op jit(solution)/shard_map/ppermute | solution.py:19
  58.8 4.3 %collective-permute-start.7 = (bf16[256,128]{1,0:T(8,128)(2,1)S(1)}, bf16[256,128]{1,0:T(8,128)(2,1)S(1)}, u32[]{:S(2)}, u32[]{:S(2)}) collective-permute-start(bf16[256,128]{1,0:T(8,128)(2,1)S(1)} %shard_map.67.refs_0_), channel_id=1, source_target_pairs={{0,4},{4,0},{8,12},{12,8},{16,20},{20,16},{24,28},{28,24},{1,5},{5... | collective-permute-start | bytes 196616 | tf_op jit(solution)/shard_map/ppermute | solution.py:19
  63.1 2.0 %collective-permute-start.15 = (bf16[2048,128]{1,0:T(8,128)(2,1)S(1)}, bf16[2048,128]{1,0:T(8,128)(2,1)S(1)}, u32[]{:S(2)}, u32[]{:S(2)}) collective-permute-start(bf16[2048,128]{1,0:T(8,128)(2,1)S(1)} %get-tuple-element.46.own), channel_id=1, source_target_pairs={{0,1},{1,0},{2,3},{3,2},{4,5},{5,4},{6,7},{7,6},{8,9},{9,8},{10,11... | collective-permute-start | bytes 1572872 | tf_op jit(solution)/shard_map/ppermute | solution.py:19
  70.4 6.5 %collective-permute-start.16 = (bf16[2,4,128,128]{3,2,1,0:T(8,128)(2,1)S(1)}, bf16[2,4,128,128]{3,2,1,0:T(8,128)(2,1)S(1)}, u32[]{:S(2)}, u32[]{:S(2)}) collective-permute-start(bf16[2,4,128,128]{3,2,1,0:T(8,128)(2,1)S(1)} %get-tuple-element.48), channel_id=1, source_target_pairs={{0,2},{2,0},{1,3},{3,1},{4,6},{6,4},{5,7},{7,5},{8,10},{10,8},{9,1... | collective-permute-start | bytes 786440 | tf_op jit(solution)/shard_map/ppermute | solution.py:19
  70.4 7.6 %collective-permute-start.17 = (bf16[2,4,128,128]{3,2,1,0:T(8,128)(2,1)S(1)}, bf16[2,4,128,128]{3,2,1,0:T(8,128)(2,1)S(1)}, u32[]{:S(2)}, u32[]{:S(2)}) collective-permute-start(bf16[2,4,128,128]{3,2,1,0:T(8,128)(2,1)S(1)} %get-tuple-element.50), channel_id=1, source_target_pairs={{0,4},{4,0},{8,12},{12,8},{16,20},{20,16},{24,28},{28,24},{1,5},{5... | collective-permute-start | bytes 786440 | tf_op jit(solution)/shard_map/ppermute | solution.py:19
  78.2 5.0 %collective-permute-start.18 = (bf16[4,128,128]{2,1,0:T(8,128)(2,1)S(1)}, bf16[4,128,128]{2,1,0:T(8,128)(2,1)S(1)}, u32[]{:S(2)}, u32[]{:S(2)}) collective-permute-start(bf16[4,128,128]{2,1,0:T(8,128)(2,1)S(1)} %get-tuple-element.52), channel_id=1, source_target_pairs={{0,4},{4,0},{8,12},{12,8},{16,20},{20,16},{24,28},{28,24},{1,5},{5... | collective-permute-start | bytes 393224 | tf_op jit(solution)/shard_map/ppermute | solution.py:19
  78.9 5.0 %collective-permute-start.19 = (bf16[4,128,128]{2,1,0:T(8,128)(2,1)S(1)}, bf16[4,128,128]{2,1,0:T(8,128)(2,1)S(1)}, u32[]{:S(2)}, u32[]{:S(2)}) collective-permute-start(bf16[4,128,128]{2,1,0:T(8,128)(2,1)S(1)} %get-tuple-element.54), channel_id=1, source_target_pairs={{0,2},{2,0},{1,3},{3,1},{4,6},{6,4},{5,7},{7,5},{8,10},{10,8},{9,1... | collective-permute-start | bytes 393224 | tf_op jit(solution)/shard_map/ppermute | solution.py:19
  83.9 4.5 %collective-permute-start.20 = (bf16[2,128,128]{2,1,0:T(8,128)(2,1)S(1)}, bf16[2,128,128]{2,1,0:T(8,128)(2,1)S(1)}, u32[]{:S(2)}, u32[]{:S(2)}) collective-permute-start(bf16[2,128,128]{2,1,0:T(8,128)(2,1)S(1)} %get-tuple-element.56), channel_id=1, source_target_pairs={{0,8},{4,12},{8,0},{12,4},{16,24},{20,28},{24,16},{28,20},{1,9},{5... | collective-permute-start | bytes 196616 | tf_op jit(solution)/shard_map/ppermute | solution.py:19
  84.0 5.5 %collective-permute-start.21 = (bf16[2,128,128]{2,1,0:T(8,128)(2,1)S(1)}, bf16[2,128,128]{2,1,0:T(8,128)(2,1)S(1)}, u32[]{:S(2)}, u32[]{:S(2)}) collective-permute-start(bf16[2,128,128]{2,1,0:T(8,128)(2,1)S(1)} %get-tuple-element.57), channel_id=1, source_target_pairs={{0,16},{4,20},{8,24},{12,28},{16,0},{20,4},{24,8},{28,12},{1,17},{... | collective-permute-start | bytes 196616 | tf_op jit(solution)/shard_map/ppermute | solution.py:19
  87.3 6.2 %collective-permute-start.22 = (bf16[2,128,128]{2,1,0:T(8,128)(2,1)S(1)}, bf16[2,128,128]{2,1,0:T(8,128)(2,1)S(1)}, u32[]{:S(2)}, u32[]{:S(2)}) collective-permute-start(bf16[2,128,128]{2,1,0:T(8,128)(2,1)S(1)} %get-tuple-element.58), channel_id=1, source_target_pairs={{0,24},{4,28},{8,16},{12,20},{16,8},{20,12},{24,0},{28,4},{1,25},{... | collective-permute-start | bytes 196616 | tf_op jit(solution)/shard_map/ppermute | solution.py:19
  93.6 7.7 %collective-permute-start.29 = (bf16[256,128]{1,0:T(8,128)(2,1)S(1)}, bf16[256,128]{1,0:T(8,128)(2,1)S(1)}, u32[]{:S(2)}, u32[]{:S(2)}) collective-permute-start(bf16[256,128]{1,0:T(8,128)(2,1)S(1)} %shard_map.72.refs_0_), channel_id=1, source_target_pairs={{0,28},{4,24},{8,20},{12,16},{16,12},{20,8},{24,4},{28,0},{1,29},{... | collective-permute-start | bytes 196616 | tf_op jit(solution)/shard_map/ppermute | solution.py:19
  95.5 7.7 %collective-permute-start.28 = (bf16[256,128]{1,0:T(8,128)(2,1)S(1)}, bf16[256,128]{1,0:T(8,128)(2,1)S(1)}, u32[]{:S(2)}, u32[]{:S(2)}) collective-permute-start(bf16[256,128]{1,0:T(8,128)(2,1)S(1)} %shard_map.72.refs_0_), channel_id=1, source_target_pairs={{0,24},{4,28},{8,16},{12,20},{16,8},{20,12},{24,0},{28,4},{1,25},{... | collective-permute-start | bytes 196616 | tf_op jit(solution)/shard_map/ppermute | solution.py:19
  97.3 8.5 %collective-permute-start.27 = (bf16[256,128]{1,0:T(8,128)(2,1)S(1)}, bf16[256,128]{1,0:T(8,128)(2,1)S(1)}, u32[]{:S(2)}, u32[]{:S(2)}) collective-permute-start(bf16[256,128]{1,0:T(8,128)(2,1)S(1)} %shard_map.72.refs_0_), channel_id=1, source_target_pairs={{0,20},{4,16},{8,28},{12,24},{16,4},{20,0},{24,12},{28,8},{1,21},{... | collective-permute-start | bytes 196616 | tf_op jit(solution)/shard_map/ppermute | solution.py:19
  97.3 8.5 %collective-permute-start.26 = (bf16[256,128]{1,0:T(8,128)(2,1)S(1)}, bf16[256,128]{1,0:T(8,128)(2,1)S(1)}, u32[]{:S(2)}, u32[]{:S(2)}) collective-permute-start(bf16[256,128]{1,0:T(8,128)(2,1)S(1)} %shard_map.72.refs_0_), channel_id=1, source_target_pairs={{0,16},{4,20},{8,24},{12,28},{16,0},{20,4},{24,8},{28,12},{1,17},{... | collective-permute-start | bytes 196616 | tf_op jit(solution)/shard_map/ppermute | solution.py:19
  101.4 5.9 %collective-permute-start.25 = (bf16[256,128]{1,0:T(8,128)(2,1)S(1)}, bf16[256,128]{1,0:T(8,128)(2,1)S(1)}, u32[]{:S(2)}, u32[]{:S(2)}) collective-permute-start(bf16[256,128]{1,0:T(8,128)(2,1)S(1)} %shard_map.72.refs_0_), channel_id=1, source_target_pairs={{0,12},{4,8},{8,4},{12,0},{16,28},{20,24},{24,20},{28,16},{1,13},{... | collective-permute-start | bytes 196616 | tf_op jit(solution)/shard_map/ppermute | solution.py:19
  101.4 5.9 %collective-permute-start.24 = (bf16[256,128]{1,0:T(8,128)(2,1)S(1)}, bf16[256,128]{1,0:T(8,128)(2,1)S(1)}, u32[]{:S(2)}, u32[]{:S(2)}) collective-permute-start(bf16[256,128]{1,0:T(8,128)(2,1)S(1)} %shard_map.72.refs_0_), channel_id=1, source_target_pairs={{0,8},{4,12},{8,0},{12,4},{16,24},{20,28},{24,16},{28,20},{1,9},{5... | collective-permute-start | bytes 196616 | tf_op jit(solution)/shard_map/ppermute | solution.py:19
  103.2 4.8 %collective-permute-start.23 = (bf16[256,128]{1,0:T(8,128)(2,1)S(1)}, bf16[256,128]{1,0:T(8,128)(2,1)S(1)}, u32[]{:S(2)}, u32[]{:S(2)}) collective-permute-start(bf16[256,128]{1,0:T(8,128)(2,1)S(1)} %shard_map.72.refs_0_), channel_id=1, source_target_pairs={{0,4},{4,0},{8,12},{12,8},{16,20},{20,16},{24,28},{28,24},{1,5},{5... | collective-permute-start | bytes 196616 | tf_op jit(solution)/shard_map/ppermute | solution.py:19

commit v2 on v1

--- a/solution.py
+++ b/solution.py
@@ -8,8 +8,9 @@
 from jax.sharding import PartitionSpec as P
 
 VMEM = pl.BlockSpec(memory_space=pltpu.VMEM)
+HBM = pl.BlockSpec(memory_space=pltpu.HBM)
 SMEM = pl.BlockSpec(memory_space=pltpu.SMEM)
-PARAMS = pltpu.CompilerParams(vmem_limit_bytes=48 * 1024 * 1024)
+MIB = 1024 * 1024
 F32 = jnp.float32
 BF16 = jnp.bfloat16
 
@@ -19,15 +20,15 @@
     return lax.ppermute(array, axis, [(i, i ^ by) for i in range(peers)])
 
 
-def call(kernel, outs, specs, scratch, *args):
-    return pl.pallas_call(
+def call(kernel, outs, specs, scratch, *args, grant=32 * MIB):
+    return list(pl.pallas_call(
         kernel,
         out_shape=outs,
         in_specs=specs,
         out_specs=[VMEM] * len(outs),
         scratch_shapes=scratch,
-        compiler_params=PARAMS,
-    )(*args)
+        compiler_params=pltpu.CompilerParams(vmem_limit_bytes=grant),
+    )(*args))
 
 
 class Plan:
@@ -56,17 +57,28 @@
         return jax.ShapeDtypeStruct((*lead, self.piece, self.width), BF16)
 
 
-def tile_product(p, acc, blocks, coords, counts, column):
-    acc[...] = jnp.zeros_like(acc)
-
-    def slot(c, carry):
-        row = pl.multiple_of(coords[2 * c] * p.edge, p.edge)
-        acc[pl.ds(row, p.edge)] += jnp.dot(
-            blocks[c], column(coords[2 * c + 1]), preferred_element_type=F32
-        )
+GROUP = 4
+
+
+def tile_product(p, acc, blocks, coords, counts, column, ready=None):
+    def group(i, carry):
+        if ready is not None:
+            ready(i)
+        slots = [i * GROUP + j for j in range(GROUP)]
+
+        @pl.when(slots[0] < counts[0])
+        def _():
+            products = [
+                jnp.dot(blocks[c], column(coords[1, c]), preferred_element_type=F32)
+                for c in slots
+            ]
+            for c, product in zip(slots, products):
+                at = pl.ds(pl.multiple_of(coords[0, c] * p.edge, p.edge), p.edge)
+                acc[at] += jnp.where(c < counts[0], product, 0.0)
+
         return carry
 
-    lax.fori_loop(0, counts[0], slot, 0)
+    lax.fori_loop(0, p.slots // GROUP, group, 0)
 
 
 def split_first(p, acc, outs):
@@ -88,16 +100,38 @@
             b_keep[s, g] = rows(s, x, g, 1)
 
 
-def first_kernel(p, blocks, coords, counts, history, *rest):
-    *outs, own_half, acc = rest
+def first_kernel(p, blocks_hbm, coords, counts, history_hbm, *rest):
+    *outs, own_half, acc, blocks, history, block_sem, history_sem = rest
     per_half = p.owned // p.edge
-    own_half[...] = history[lax.axis_index("tgt")]
+    rows = p.owned // 2
+    copies = [
+        pltpu.make_async_copy(
+            history_hbm.at[h, pl.ds(i * rows, rows)],
+            history.at[h, pl.ds(i * rows, rows)],
+            history_sem.at[h, i],
+        )
+        for h in range(p.halves)
+        for i in range(2)
+    ]
+
+    def block_copy(i):
+        at = pl.ds(i * GROUP, GROUP)
+        return pltpu.make_async_copy(blocks_hbm.at[at], blocks.at[at], block_sem.at[i])
+
+    for copy in copies:
+        copy.start()
+    for i in range(p.slots // GROUP):
+        block_copy(i).start()
+    acc[...] = jnp.zeros_like(acc)
+    for copy in copies:
+        copy.wait()
 
     def column(c):
         start = pl.multiple_of((c % per_half) * p.edge, p.edge)
         return history[c // per_half, pl.ds(start, p.edge)]
 
-    tile_product(p, acc, blocks, coords, counts, column)
+    tile_product(p, acc, blocks, coords, counts, column, lambda i: block_copy(i).wait())
+    own_half[...] = history[lax.axis_index("tgt")]
     split_first(p, acc, outs)
 
 
@@ -111,6 +145,7 @@
         at = pl.ds(start, p.edge)
         return jnp.where(c // per_half == half, own[at], other[at])
 
+    acc[...] = jnp.zeros_like(acc)
     tile_product(p, acc, blocks, coords, counts, column)
     split_first(p, acc, outs)
 
@@ -141,6 +176,17 @@
     a_keep, a_came, b_keep = refs[:3]
     b_came = refs[3 : n + 2]
     outs = refs[n + 2 :]
+    if len(outs) > p.groups:
+        mine, behind, *outs, onward = outs
+
+        @pl.when(p.x() == 0)
+        def _():
+            onward[...] = mine[...]
+
+        @pl.when(p.x() == 1)
+        def _():
+            onward[...] = behind[...]
+
     mine = p.g()
     for k, ref in enumerate(outs):
         g = mine ^ k
@@ -197,8 +243,14 @@
         out[before.shape[0], 0, place_of(p, k)] = ref[...]
 
 
-def field_sum(p, firsts):
+def field_sum(p, firsts, lagged):
     n = p.srcs
+    moved = []
+    if lagged is not None:
+        behind = lax.ppermute(
+            lagged, "delay", [(i, i + 2) for i in range(1, p.bins - 2, 2)]
+        )
+        moved = [lagged, behind]
     a_keep, a_sends = firsts[0], firsts[1:n]
     b_send, b_keep = firsts[n], firsts[n + 1]
     a_came = [exchange(v, "src", k) for k, v in enumerate(a_sends, 1)]
@@ -218,14 +270,19 @@
     b_came = [exchange(v, "src", k) for k, v in enumerate(b_sends, 1)]
     terms = call(
         functools.partial(third_kernel, p),
-        [p.shape(2)] * p.groups,
-        [VMEM] * (n + 2),
+        [p.shape(2)] * p.groups
+        + [jax.ShapeDtypeStruct(v.shape, BF16) for v in moved[:1]],
+        [VMEM] * (n + 2 + len(moved)),
         [],
         a_stay,
         a_came,
         b_stay,
         *b_came,
-    )
+        *moved,
+    )
+    shifted = None
+    if moved:
+        shifted = exchange(terms.pop(), "delay", 1)
     by = 2 * p.groups
     while by < p.bins:
         terms = [
@@ -234,14 +291,15 @@
         ]
         by *= 2
     keep, *sends = terms
-    return [keep] + [exchange(v, "delay", 2 * k) for k, v in enumerate(sends, 1)]
+    came = [exchange(v, "delay", 2 * k) for k, v in enumerate(sends, 1)]
+    return [keep, *came], shifted
 
 
 def shards(blocks, coords, counts, history, excitation, inverse):
     p = Plan(blocks, history)
     steps = excitation.shape[0]
     slot_blocks = blocks.reshape(blocks.shape[3:])
-    places = coords.reshape(-1)
+    places = coords.reshape(-1, 2).T
     used = counts.reshape(-1)
     first_outs = (
         [p.shape(2, p.groups)] * p.srcs
@@ -252,16 +310,24 @@
     *firsts, lagged = call(
         functools.partial(first_kernel, p),
         first_outs + [half],
-        [VMEM, SMEM, SMEM, VMEM],
-        acc,
+        [HBM, SMEM, SMEM, HBM],
+        acc
+        + [
+            pltpu.VMEM(slot_blocks.shape, BF16),
+            pltpu.VMEM(history.shape[1:], BF16),
+            pltpu.SemaphoreType.DMA((p.slots // GROUP,)),
+            pltpu.SemaphoreType.DMA((p.halves, 2)),
+        ],
         slot_blocks,
         places,
         used,
         history[0],
+        grant=52 * MIB,
     )
     done = []
     for step in range(steps):
-        terms = field_sum(p, firsts)
+        more = step + 1 < steps
+        terms, shifted = field_sum(p, firsts, lagged if more else None)
         piece = call(
             functools.partial(current_kernel, p, step),
             [jax.ShapeDtypeStruct((p.slice_rows, p.width), BF16)],
@@ -271,12 +337,8 @@
             excitation,
             inverse,
         )[0]
-        if step + 1 < steps:
-            shifted = lax.ppermute(
-                lagged, "delay", [(i, i + 1) for i in range(p.bins - 1)]
-            )
         slices = [piece] + [exchange(piece, "delay", k) for k in range(1, p.slices)]
-        if step + 1 == steps:
+        if not more:
             return call(
                 functools.partial(last_kernel, p),
                 [jax.ShapeDtypeStruct((steps, 1, p.owned, p.width), BF16)],

time: 109 us -> 96.3 us (0.88)
  waiting for transfers between devices: 45.5 us -> 40.6 us
  Pallas kernels: 12.3 us -> 7.58 us
  local copies, waits for them, and re-layouts: 2.66 us -> 0.69 us
    ppermute x29 -> x30, waiting for transfers between devices: 45.5 us -> 40.6 us  [exchange(): return lax.ppermute(array, axis, [(i, i ^ by) for i in range(peers)])]
    pallas_call x10, Pallas kernels: 12.3 us -> 7.58 us  [call(): pl.pallas_call(kernel, out_shape=outs, in_specs=specs, out_specs=[VMEM] *...]
    unnamed x13 -> x8, local copies, waits for them, and re-layouts: 2.56 us -> 0.69 us
    ppermute x1, starting transfers between devices: 1.93 us -> 0.69 us  [field_sum(): lax.ppermute(lagged, 'delay', [(i, i + 2) for i in range(1, p.bins - 2, 2)])]
    ppermute x29 -> x30, starting transfers between devices: 45.8 us -> 46.4 us  [exchange(): return lax.ppermute(array, axis, [(i, i ^ by) for i in range(peers)])]
  transfers between devices with their start and end apart: 30 -> 31, of which waited for: 18 -> 24; matrix products, arithmetic and copies ran while one was open for 0% -> 0% of each run, Pallas kernels for 0% -> 0%
where the time goes in v2:
time: 96.3 us; the launch traced here: 96.7 us
  starting transfers between devices  47.1 us (49%)
  waiting for transfers between devices  40.6 us (42%)
  Pallas kernels  7.58 us (8%)
    ppermute x30, starting transfers between devices, exchange(): return lax.ppermute(array, axis, [(i, i ^ by) for i in range(peers)])  46.4 us
    ppermute x30, waiting for transfers between devices, exchange(): return lax.ppermute(array, axis, [(i, i ^ by) for i in range(peers)])  40.6 us
    pallas_call x10, Pallas kernels, call(): pl.pallas_call(kernel, out_shape=outs, in_specs=specs, out_specs=[VMEM] *...  7.58 us
  transfers between devices with their start and end apart: 31, of which 24 were waited for; matrix products, arithmetic and copies ran while one was open for 0% of the time, Pallas kernels for 0%

profile of v2, /device:TPU:0, one launch (start us, length us, event | category | flops | bytes accessed | tf_op | source)
XLA Modules:
  0.0 96.7 jit_solution(6610843717300792837)
XLA Ops:
  0.7 0.7 copy-done.3
  1.3 3.6 %shard_map.64 = (bf16[2,4,128,128]{3,2,1,0:T(8,128)(2,1)S(1)}, bf16[2,4,128,128]{3,2,1,0:T(8,128)(2,1)S(1)}, bf16[2,4,128,128]{3,2,1,0:T(8,128)(2,1)S(1)}, bf16[...) custom-call(bf16[32,128,128]{2,1,0:T(8,128)(2,1)} %bitcast.9, s32[2,32]{1,0:T(2,128)S(1)} %bitcast.12, ...), custom_call_target="tpu_custom_call" | custom-call | tf_op jit(solution)/shard_map/pallas_call | solution.py:24
  4.9 0.7 collective-permute-start.4
  5.6 2.8 %collective-permute-start = (bf16[2,4,128,128]{3,2,1,0:T(8,128)(2,1)S(1)}, bf16[2,4,128,128]{3,2,1,0:T(8,128)(2,1)S(1)}, u32[]{:S(2)}, u32[]{:S(2)}) collective-permute-start(bf16[2,4,128,128]{3,2,1,0:T(8,128)(2,1)S(1)} %get-tuple-element.34), channel_id=1, source_target_pairs={{0,2},{2,0},{1,3},{3,1},{4,6},{6,4},{5,7},{7,5},{8,10},{10,8},{9,1... | collective-permute-start | bytes 786440 | tf_op jit(solution)/shard_map/ppermute | solution.py:20
  8.5 4.7 %collective-permute-start.1 = (bf16[2,4,128,128]{3,2,1,0:T(8,128)(2,1)S(1)}, bf16[2,4,128,128]{3,2,1,0:T(8,128)(2,1)S(1)}, u32[]{:S(2)}, u32[]{:S(2)}) collective-permute-start(bf16[2,4,128,128]{3,2,1,0:T(8,128)(2,1)S(1)} %get-tuple-element.36), channel_id=1, source_target_pairs={{0,4},{4,0},{8,12},{12,8},{16,20},{20,16},{24,28},{28,24},{1,5},{5... | collective-permute-start | bytes 786440 | tf_op jit(solution)/shard_map/ppermute | solution.py:20
  13.2 1.8 %collective-permute-done.refs_1_ = bf16[2,4,128,128]{3,2,1,0:T(8,128)(2,1)S(1)} collective-permute-done((bf16[2,4,128,128]{3,2,1,0:T(8,128)(2,1)S(1)}, bf16[2,4,128,128]{3,2,1,0:T(8,128)(2,1)S(1)}, u32[]{:S(2)}, u32[]{:S(2)}) %collective-permute-start) | collective-permute-done | bytes 262176 | tf_op jit(solution)/shard_map/ppermute | solution.py:20
  15.0 4.1 %collective-permute-done.1.refs_3_ = bf16[2,4,128,128]{3,2,1,0:T(8,128)(2,1)S(1)} collective-permute-done((bf16[2,4,128,128]{3,2,1,0:T(8,128)(2,1)S(1)}, bf16[2,4,128,128]{3,2,1,0:T(8,128)(2,1)S(1)}, u32[]{:S(2)}, u32[]{:S(2)}) %collective-permute-start.1) | collective-permute-done | bytes 262176 | tf_op jit(solution)/shard_map/ppermute | solution.py:20
  19.2 1.8 %collective-permute-start.2 = (bf16[4,128,128]{2,1,0:T(8,128)(2,1)S(1)}, bf16[4,128,128]{2,1,0:T(8,128)(2,1)S(1)}, u32[]{:S(2)}, u32[]{:S(2)}) collective-permute-start(bf16[4,128,128]{2,1,0:T(8,128)(2,1)S(1)} %get-tuple-element.38), channel_id=1, source_target_pairs={{0,4},{4,0},{8,12},{12,8},{16,20},{20,16},{24,28},{28,24},{1,5},{5... | collective-permute-start | bytes 393224 | tf_op jit(solution)/shard_map/ppermute | solution.py:20
  21.1 0.4 collective-permute-start.3
  21.4 2.9 %collective-permute-done.2.refs_1_ = bf16[4,128,128]{2,1,0:T(8,128)(2,1)S(1)} collective-permute-done((bf16[4,128,128]{2,1,0:T(8,128)(2,1)S(1)}, bf16[4,128,128]{2,1,0:T(8,128)(2,1)S(1)}, u32[]{:S(2)}, u32[]{:S(2)}) %collective-permute-start.2) | collective-permute-done | bytes 131104 | tf_op jit(solution)/shard_map/ppermute | solution.py:20
  24.3 1.7 %collective-permute-done.3.refs_3_ = bf16[4,128,128]{2,1,0:T(8,128)(2,1)S(1)} collective-permute-done((bf16[4,128,128]{2,1,0:T(8,128)(2,1)S(1)}, bf16[4,128,128]{2,1,0:T(8,128)(2,1)S(1)}, u32[]{:S(2)}, u32[]{:S(2)}) %collective-permute-start.3) | collective-permute-done | bytes 131104 | tf_op jit(solution)/shard_map/ppermute | solution.py:20
  26.5 1.4 %collective-permute-start.5 = (bf16[2,128,128]{2,1,0:T(8,128)(2,1)S(1)}, bf16[2,128,128]{2,1,0:T(8,128)(2,1)S(1)}, u32[]{:S(2)}, u32[]{:S(2)}) collective-permute-start(bf16[2,128,128]{2,1,0:T(8,128)(2,1)S(1)} %get-tuple-element.43), channel_id=1, source_target_pairs={{0,8},{4,12},{8,0},{12,4},{16,24},{20,28},{24,16},{28,20},{1,9},{5... | collective-permute-start | bytes 196616 | tf_op jit(solution)/shard_map/ppermute | solution.py:20
  27.8 1.2 %collective-permute-start.6 = (bf16[2,128,128]{2,1,0:T(8,128)(2,1)S(1)}, bf16[2,128,128]{2,1,0:T(8,128)(2,1)S(1)}, u32[]{:S(2)}, u32[]{:S(2)}) collective-permute-start(bf16[2,128,128]{2,1,0:T(8,128)(2,1)S(1)} %get-tuple-element.44), channel_id=1, source_target_pairs={{0,16},{4,20},{8,24},{12,28},{16,0},{20,4},{24,8},{28,12},{1,17},{... | collective-permute-start | bytes 196616 | tf_op jit(solution)/shard_map/ppermute | solution.py:20
  29.0 1.8 %collective-permute-start.7 = (bf16[2,128,128]{2,1,0:T(8,128)(2,1)S(1)}, bf16[2,128,128]{2,1,0:T(8,128)(2,1)S(1)}, u32[]{:S(2)}, u32[]{:S(2)}) collective-permute-start(bf16[2,128,128]{2,1,0:T(8,128)(2,1)S(1)} %get-tuple-element.45), channel_id=1, source_target_pairs={{0,24},{4,28},{8,16},{12,20},{16,8},{20,12},{24,0},{28,4},{1,25},{... | collective-permute-start | bytes 196616 | tf_op jit(solution)/shard_map/ppermute | solution.py:20
  30.9 2.8 %collective-permute-done.6.refs_1_ = bf16[2,128,128]{2,1,0:T(8,128)(2,1)S(1)} collective-permute-done((bf16[2,128,128]{2,1,0:T(8,128)(2,1)S(1)}, bf16[2,128,128]{2,1,0:T(8,128)(2,1)S(1)}, u32[]{:S(2)}, u32[]{:S(2)}) %collective-permute-start.6) | collective-permute-done | bytes 65568 | tf_op jit(solution)/shard_map/ppermute | solution.py:20
  33.7 1.5 %collective-permute-done.7.refs_2_ = bf16[2,128,128]{2,1,0:T(8,128)(2,1)S(1)} collective-permute-done((bf16[2,128,128]{2,1,0:T(8,128)(2,1)S(1)}, bf16[2,128,128]{2,1,0:T(8,128)(2,1)S(1)}, u32[]{:S(2)}, u32[]{:S(2)}) %collective-permute-start.7) | collective-permute-done | bytes 65568 | tf_op jit(solution)/shard_map/ppermute | solution.py:20
  35.4 3.1 %collective-permute-start.14 = (bf16[256,128]{1,0:T(8,128)(2,1)S(1)}, bf16[256,128]{1,0:T(8,128)(2,1)S(1)}, u32[]{:S(2)}, u32[]{:S(2)}) collective-permute-start(bf16[256,128]{1,0:T(8,128)(2,1)S(1)} %shard_map.67.refs_0_), channel_id=1, source_target_pairs={{0,28},{4,24},{8,20},{12,16},{16,12},{20,8},{24,4},{28,0},{1,29},{... | collective-permute-start | bytes 196616 | tf_op jit(solution)/shard_map/ppermute | solution.py:20
  38.5 2.0 %collective-permute-start.13 = (bf16[256,128]{1,0:T(8,128)(2,1)S(1)}, bf16[256,128]{1,0:T(8,128)(2,1)S(1)}, u32[]{:S(2)}, u32[]{:S(2)}) collective-permute-start(bf16[256,128]{1,0:T(8,128)(2,1)S(1)} %shard_map.67.refs_0_), channel_id=1, source_target_pairs={{0,24},{4,28},{8,16},{12,20},{16,8},{20,12},{24,0},{28,4},{1,25},{... | collective-permute-start | bytes 196616 | tf_op jit(solution)/shard_map/ppermute | solution.py:20
  40.5 2.6 %collective-permute-start.11 = (bf16[256,128]{1,0:T(8,128)(2,1)S(1)}, bf16[256,128]{1,0:T(8,128)(2,1)S(1)}, u32[]{:S(2)}, u32[]{:S(2)}) collective-permute-start(bf16[256,128]{1,0:T(8,128)(2,1)S(1)} %shard_map.67.refs_0_), channel_id=1, source_target_pairs={{0,16},{4,20},{8,24},{12,28},{16,0},{20,4},{24,8},{28,12},{1,17},{... | collective-permute-start | bytes 196616 | tf_op jit(solution)/shard_map/ppermute | solution.py:20
  43.2 1.6 %collective-permute-start.10 = (bf16[256,128]{1,0:T(8,128)(2,1)S(1)}, bf16[256,128]{1,0:T(8,128)(2,1)S(1)}, u32[]{:S(2)}, u32[]{:S(2)}) collective-permute-start(bf16[256,128]{1,0:T(8,128)(2,1)S(1)} %shard_map.67.refs_0_), channel_id=1, source_target_pairs={{0,12},{4,8},{8,4},{12,0},{16,28},{20,24},{24,20},{28,16},{1,13},{... | collective-permute-start | bytes 196616 | tf_op jit(solution)/shard_map/ppermute | solution.py:20
  44.8 1.5 %collective-permute-start.9 = (bf16[256,128]{1,0:T(8,128)(2,1)S(1)}, bf16[256,128]{1,0:T(8,128)(2,1)S(1)}, u32[]{:S(2)}, u32[]{:S(2)}) collective-permute-start(bf16[256,128]{1,0:T(8,128)(2,1)S(1)} %shard_map.67.refs_0_), channel_id=1, source_target_pairs={{0,8},{4,12},{8,0},{12,4},{16,24},{20,28},{24,16},{28,20},{1,9},{5... | collective-permute-start | bytes 196616 | tf_op jit(solution)/shard_map/ppermute | solution.py:20
  46.3 0.8 collective-permute-done.12.refs_5_
  47.1 0.4 collective-permute-start.8
  47.6 0.9 collective-permute-done.10.refs_3_
  48.5 0.8 collective-permute-done.9.refs_2_
  49.3 2.1 %collective-permute-done.8.refs_1_ = bf16[256,128]{1,0:T(8,128)(2,1)S(1)} collective-permute-done((bf16[256,128]{1,0:T(8,128)(2,1)S(1)}, bf16[256,128]{1,0:T(8,128)(2,1)S(1)}, u32[]{:S(2)}, u32[]{:S(2)}) %collective-permute-start.8) | collective-permute-done | bytes 65568 | tf_op jit(solution)/shard_map/ppermute | solution.py:20
  51.5 1.9 %collective-permute-done.16.other = bf16[2048,128]{1,0:T(8,128)(2,1)S(1)} collective-permute-done((bf16[2048,128]{1,0:T(8,128)(2,1)S(1)}, bf16[2048,128]{1,0:T(8,128)(2,1)S(1)}, u32[]{:S(2)}, u32[]{:S(2)}) %collective-permute-start.16) | collective-permute-done | bytes 524320 | tf_op jit(solution)/shard_map/ppermute | solution.py:20
  53.4 2.1 %shard_map.69 = (bf16[2,4,128,128]{3,2,1,0:T(8,128)(2,1)S(1)}, bf16[2,4,128,128]{3,2,1,0:T(8,128)(2,1)S(1)}, bf16[2,4,128,128]{3,2,1,0:T(8,128)(2,1)S(1)}, bf16[2,4,128,128]{3,2,1,0:T(8,128)(2,1)S(1)}) custom-call(bf16[32,128,128]{2,1,0:T(8,128)(2,1)S(1)} %bitcast.10, s32[2,32]{1,0:T(2,128)S(1)} %bitcast.13, s32[1]{0:T(128)} %bitcast.8.counts, ...), custom_call_target="tpu_custom_call" | custom-call | tf_op jit(solution)/shard_map/pallas_call | solution.py:24
  55.6 0.7 collective-permute-start.17
  56.3 2.1 %collective-permute-start.18 = (bf16[2,4,128,128]{3,2,1,0:T(8,128)(2,1)S(1)}, bf16[2,4,128,128]{3,2,1,0:T(8,128)(2,1)S(1)}, u32[]{:S(2)}, u32[]{:S(2)}) collective-permute-start(bf16[2,4,128,128]{3,2,1,0:T(8,128)(2,1)S(1)} %get-tuple-element.52), channel_id=1, source_target_pairs={{0,4},{4,0},{8,12},{12,8},{16,20},{20,16},{24,28},{28,24},{1,5},{5... | collective-permute-start | bytes 786440 | tf_op jit(solution)/shard_map/ppermute | solution.py:20
  58.4 6.0 %collective-permute-done.17.refs_1_ = bf16[2,4,128,128]{3,2,1,0:T(8,128)(2,1)S(1)} collective-permute-done((bf16[2,4,128,128]{3,2,1,0:T(8,128)(2,1)S(1)}, bf16[2,4,128,128]{3,2,1,0:T(8,128)(2,1)S(1)}, u32[]{:S(2)}, u32[]{:S(2)}) %collective-permute-start.17) | collective-permute-done | bytes 262176 | tf_op jit(solution)/shard_map/ppermute | solution.py:20
  64.4 0.4 collective-permute-done.18.refs_3_
  64.9 1.8 %collective-permute-start.19 = (bf16[4,128,128]{2,1,0:T(8,128)(2,1)S(1)}, bf16[4,128,128]{2,1,0:T(8,128)(2,1)S(1)}, u32[]{:S(2)}, u32[]{:S(2)}) collective-permute-start(bf16[4,128,128]{2,1,0:T(8,128)(2,1)S(1)} %get-tuple-element.54), channel_id=1, source_target_pairs={{0,4},{4,0},{8,12},{12,8},{16,20},{20,16},{24,28},{28,24},{1,5},{5... | collective-permute-start | bytes 393224 | tf_op jit(solution)/shard_map/ppermute | solution.py:20
  67.0 2.9 %collective-permute-done.19.refs_1_ = bf16[4,128,128]{2,1,0:T(8,128)(2,1)S(1)} collective-permute-done((bf16[4,128,128]{2,1,0:T(8,128)(2,1)S(1)}, bf16[4,128,128]{2,1,0:T(8,128)(2,1)S(1)}, u32[]{:S(2)}, u32[]{:S(2)}) %collective-permute-start.19) | collective-permute-done | bytes 131104 | tf_op jit(solution)/shard_map/ppermute | solution.py:20
  69.9 1.7 %collective-permute-done.20.refs_3_ = bf16[4,128,128]{2,1,0:T(8,128)(2,1)S(1)} collective-permute-done((bf16[4,128,128]{2,1,0:T(8,128)(2,1)S(1)}, bf16[4,128,128]{2,1,0:T(8,128)(2,1)S(1)}, u32[]{:S(2)}, u32[]{:S(2)}) %collective-permute-start.20) | collective-permute-done | bytes 131104 | tf_op jit(solution)/shard_map/ppermute | solution.py:20
  71.8 2.4 %collective-permute-start.22 = (bf16[2,128,128]{2,1,0:T(8,128)(2,1)S(1)}, bf16[2,128,128]{2,1,0:T(8,128)(2,1)S(1)}, u32[]{:S(2)}, u32[]{:S(2)}) collective-permute-start(bf16[2,128,128]{2,1,0:T(8,128)(2,1)S(1)} %get-tuple-element.59), channel_id=1, source_target_pairs={{0,16},{4,20},{8,24},{12,28},{16,0},{20,4},{24,8},{28,12},{1,17},{... | collective-permute-start | bytes 196616 | tf_op jit(solution)/shard_map/ppermute | solution.py:20
  74.1 2.0 %collective-permute-start.23 = (bf16[2,128,128]{2,1,0:T(8,128)(2,1)S(1)}, bf16[2,128,128]{2,1,0:T(8,128)(2,1)S(1)}, u32[]{:S(2)}, u32[]{:S(2)}) collective-permute-start(bf16[2,128,128]{2,1,0:T(8,128)(2,1)S(1)} %get-tuple-element.60), channel_id=1, source_target_pairs={{0,24},{4,28},{8,16},{12,20},{16,8},{20,12},{24,0},{28,4},{1,25},{... | collective-permute-start | bytes 196616 | tf_op jit(solution)/shard_map/ppermute | solution.py:20
  76.2 1.3 %collective-permute-done.22.refs_1_ = bf16[2,128,128]{2,1,0:T(8,128)(2,1)S(1)} collective-permute-done((bf16[2,128,128]{2,1,0:T(8,128)(2,1)S(1)}, bf16[2,128,128]{2,1,0:T(8,128)(2,1)S(1)}, u32[]{:S(2)}, u32[]{:S(2)}) %collective-permute-start.22) | collective-permute-done | bytes 65568 | tf_op jit(solution)/shard_map/ppermute | solution.py:20
  77.5 2.8 %collective-permute-done.23.refs_2_ = bf16[2,128,128]{2,1,0:T(8,128)(2,1)S(1)} collective-permute-done((bf16[2,128,128]{2,1,0:T(8,128)(2,1)S(1)}, bf16[2,128,128]{2,1,0:T(8,128)(2,1)S(1)}, u32[]{:S(2)}, u32[]{:S(2)}) %collective-permute-start.23) | collective-permute-done | bytes 65568 | tf_op jit(solution)/shard_map/ppermute | solution.py:20
  80.5 1.9 %collective-permute-start.30 = (bf16[256,128]{1,0:T(8,128)(2,1)S(1)}, bf16[256,128]{1,0:T(8,128)(2,1)S(1)}, u32[]{:S(2)}, u32[]{:S(2)}) collective-permute-start(bf16[256,128]{1,0:T(8,128)(2,1)S(1)} %shard_map.72.refs_0_), channel_id=1, source_target_pairs={{0,28},{4,24},{8,20},{12,16},{16,12},{20,8},{24,4},{28,0},{1,29},{... | collective-permute-start | bytes 196616 | tf_op jit(solution)/shard_map/ppermute | solution.py:20
  82.4 3.1 %collective-permute-start.29 = (bf16[256,128]{1,0:T(8,128)(2,1)S(1)}, bf16[256,128]{1,0:T(8,128)(2,1)S(1)}, u32[]{:S(2)}, u32[]{:S(2)}) collective-permute-start(bf16[256,128]{1,0:T(8,128)(2,1)S(1)} %shard_map.72.refs_0_), channel_id=1, source_target_pairs={{0,24},{4,28},{8,16},{12,20},{16,8},{20,12},{24,0},{28,4},{1,25},{... | collective-permute-start | bytes 196616 | tf_op jit(solution)/shard_map/ppermute | solution.py:20
  85.6 2.6 %collective-permute-start.27 = (bf16[256,128]{1,0:T(8,128)(2,1)S(1)}, bf16[256,128]{1,0:T(8,128)(2,1)S(1)}, u32[]{:S(2)}, u32[]{:S(2)}) collective-permute-start(bf16[256,128]{1,0:T(8,128)(2,1)S(1)} %shard_map.72.refs_0_), channel_id=1, source_target_pairs={{0,16},{4,20},{8,24},{12,28},{16,0},{20,4},{24,8},{28,12},{1,17},{... | collective-permute-start | bytes 196616 | tf_op jit(solution)/shard_map/ppermute | solution.py:20
  88.3 3.2 %collective-permute-start.25 = (bf16[256,128]{1,0:T(8,128)(2,1)S(1)}, bf16[256,128]{1,0:T(8,128)(2,1)S(1)}, u32[]{:S(2)}, u32[]{:S(2)}) collective-permute-start(bf16[256,128]{1,0:T(8,128)(2,1)S(1)} %shard_map.72.refs_0_), channel_id=1, source_target_pairs={{0,8},{4,12},{8,0},{12,4},{16,24},{20,28},{24,16},{28,20},{1,9},{5... | collective-permute-start | bytes 196616 | tf_op jit(solution)/shard_map/ppermute | solution.py:20
  91.7 1.0 %collective-permute-done.27.refs_4_ = bf16[256,128]{1,0:T(8,128)(2,1)S(1)} collective-permute-done((bf16[256,128]{1,0:T(8,128)(2,1)S(1)}, bf16[256,128]{1,0:T(8,128)(2,1)S(1)}, u32[]{:S(2)}, u32[]{:S(2)}) %collective-permute-start.27) | collective-permute-done | bytes 65568 | tf_op jit(solution)/shard_map/ppermute | solution.py:20
  92.7 1.1 %collective-permute-done.26.refs_3_ = bf16[256,128]{1,0:T(8,128)(2,1)S(1)} collective-permute-done((bf16[256,128]{1,0:T(8,128)(2,1)S(1)}, bf16[256,128]{1,0:T(8,128)(2,1)S(1)}, u32[]{:S(2)}, u32[]{:S(2)}) %collective-permute-start.26) | collective-permute-done | bytes 65568 | tf_op jit(solution)/shard_map/ppermute | solution.py:20
  93.7 0.6 collective-permute-done.25.refs_2_
  94.4 1.3 %collective-permute-done.24.refs_1_ = bf16[256,128]{1,0:T(8,128)(2,1)S(1)} collective-permute-done((bf16[256,128]{1,0:T(8,128)(2,1)S(1)}, bf16[256,128]{1,0:T(8,128)(2,1)S(1)}, u32[]{:S(2)}, u32[]{:S(2)}) %collective-permute-start.24) | collective-permute-done | bytes 65568 | tf_op jit(solution)/shard_map/ppermute | solution.py:20
  95.7 1.0 %shard_map.73 = bf16[2,1,2048,128]{3,2,1,0:T(8,128)(2,1)} custom-call(bf16[1,2048,128]{2,1,0:T(8,128)(2,1)S(1)} %bitcast.11, bf16[256,128]{1,0:T(8,128)(2,1)S(1)} %shard_map.72.refs_0_, bf16[256,128]{1,0:T(8,128)(2,1)S(1)} %collective-permute-done.24.refs_1_, bf16[256,128]{1,0:T(8,128)(2,1)S(1)} %collective-permute-done.25.refs_2_, ...), custom_call_target="tpu_custom_call" | custom-call | tf_op jit(solution)/shard_map/pallas_call | solution.py:24
  (32 shorter events, 2.3 us)
Async XLA Ops:
  0.7 0.7 copy-start.3
  4.9 21.1 %collective-permute-start.4 = (bf16[2048,128]{1,0:T(8,128)(2,1)S(1)}, bf16[2048,128]{1,0:T(8,128)(2,1)S(1)}, u32[]{:S(2)}, u32[]{:S(2)}) collective-permute-start(bf16[2048,128]{1,0:T(8,128)(2,1)S(1)} %get-tuple-element.41.refs_4_), channel_id=1, source_target_pairs={{4,12},{12,20},{20,28},{5,13},{13,21},{21,29},{6,14},{14,22},{22,3... | collective-permute-start | bytes 1572872 | tf_op jit(solution)/shard_map/ppermute | solution.py:250
  5.6 9.3 %collective-permute-start = (bf16[2,4,128,128]{3,2,1,0:T(8,128)(2,1)S(1)}, bf16[2,4,128,128]{3,2,1,0:T(8,128)(2,1)S(1)}, u32[]{:S(2)}, u32[]{:S(2)}) collective-permute-start(bf16[2,4,128,128]{3,2,1,0:T(8,128)(2,1)S(1)} %get-tuple-element.34), channel_id=1, source_target_pairs={{0,2},{2,0},{1,3},{3,1},{4,6},{6,4},{5,7},{7,5},{8,10},{10,8},{9,1... | collective-permute-start | bytes 786440 | tf_op jit(solution)/shard_map/ppermute | solution.py:20
  8.5 10.6 %collective-permute-start.1 = (bf16[2,4,128,128]{3,2,1,0:T(8,128)(2,1)S(1)}, bf16[2,4,128,128]{3,2,1,0:T(8,128)(2,1)S(1)}, u32[]{:S(2)}, u32[]{:S(2)}) collective-permute-start(bf16[2,4,128,128]{3,2,1,0:T(8,128)(2,1)S(1)} %get-tuple-element.36), channel_id=1, source_target_pairs={{0,4},{4,0},{8,12},{12,8},{16,20},{20,16},{24,28},{28,24},{1,5},{5... | collective-permute-start | bytes 786440 | tf_op jit(solution)/shard_map/ppermute | solution.py:20
  19.2 16.0 %copy-start.1 = (bf16[2,1,2048,128]{3,2,1,0:T(8,128)(2,1)S(1)}, bf16[2,1,2048,128]{3,2,1,0:T(8,128)(2,1)}, u32[]{:S(2)}) copy-start(bf16[2,1,2048,128]{3,2,1,0:T(8,128)(2,1)} %refs_3_.3) | copy-start | bytes 3145732
  19.2 5.0 %collective-permute-start.2 = (bf16[4,128,128]{2,1,0:T(8,128)(2,1)S(1)}, bf16[4,128,128]{2,1,0:T(8,128)(2,1)S(1)}, u32[]{:S(2)}, u32[]{:S(2)}) collective-permute-start(bf16[4,128,128]{2,1,0:T(8,128)(2,1)S(1)} %get-tuple-element.38), channel_id=1, source_target_pairs={{0,4},{4,0},{8,12},{12,8},{16,20},{20,16},{24,28},{28,24},{1,5},{5... | collective-permute-start | bytes 393224 | tf_op jit(solution)/shard_map/ppermute | solution.py:20
  21.1 5.0 %collective-permute-start.3 = (bf16[4,128,128]{2,1,0:T(8,128)(2,1)S(1)}, bf16[4,128,128]{2,1,0:T(8,128)(2,1)S(1)}, u32[]{:S(2)}, u32[]{:S(2)}) collective-permute-start(bf16[4,128,128]{2,1,0:T(8,128)(2,1)S(1)} %get-tuple-element.40), channel_id=1, source_target_pairs={{0,2},{2,0},{1,3},{3,1},{4,6},{6,4},{5,7},{7,5},{8,10},{10,8},{9,1... | collective-permute-start | bytes 393224 | tf_op jit(solution)/shard_map/ppermute | solution.py:20
  26.0 9.2 %copy-start.2 = (bf16[1,16,128,128]{3,2,1,0:T(8,128)(2,1)S(1)}, bf16[1,16,128,128]{3,2,1,0:T(8,128)(2,1)}, u32[]{:S(2)}) copy-start(bf16[1,16,128,128]{3,2,1,0:T(8,128)(2,1)} %refs_4_.3) | copy-start | bytes 1572868
  26.1 25.2 %collective-permute-start.15 = (bf16[2048,128]{1,0:T(8,128)(2,1)S(1)}, bf16[2048,128]{1,0:T(8,128)(2,1)S(1)}, u32[]{:S(2)}, u32[]{:S(2)}) collective-permute-start(bf16[2048,128]{1,0:T(8,128)(2,1)S(1)} %get-tuple-element.46), channel_id=1, source_target_pairs={{0,4},{4,0},{8,12},{12,8},{16,20},{20,16},{24,28},{28,24},{1,5},{5... | collective-permute-start | bytes 1572872 | tf_op jit(solution)/shard_map/ppermute | solution.py:20
  26.5 4.4 %collective-permute-start.5 = (bf16[2,128,128]{2,1,0:T(8,128)(2,1)S(1)}, bf16[2,128,128]{2,1,0:T(8,128)(2,1)S(1)}, u32[]{:S(2)}, u32[]{:S(2)}) collective-permute-start(bf16[2,128,128]{2,1,0:T(8,128)(2,1)S(1)} %get-tuple-element.43), channel_id=1, source_target_pairs={{0,8},{4,12},{8,0},{12,4},{16,24},{20,28},{24,16},{28,20},{1,9},{5... | collective-permute-start | bytes 196616 | tf_op jit(solution)/shard_map/ppermute | solution.py:20
  27.8 5.9 %collective-permute-start.6 = (bf16[2,128,128]{2,1,0:T(8,128)(2,1)S(1)}, bf16[2,128,128]{2,1,0:T(8,128)(2,1)S(1)}, u32[]{:S(2)}, u32[]{:S(2)}) collective-permute-start(bf16[2,128,128]{2,1,0:T(8,128)(2,1)S(1)} %get-tuple-element.44), channel_id=1, source_target_pairs={{0,16},{4,20},{8,24},{12,28},{16,0},{20,4},{24,8},{28,12},{1,17},{... | collective-permute-start | bytes 196616 | tf_op jit(solution)/shard_map/ppermute | solution.py:20
  29.0 6.2 %collective-permute-start.7 = (bf16[2,128,128]{2,1,0:T(8,128)(2,1)S(1)}, bf16[2,128,128]{2,1,0:T(8,128)(2,1)S(1)}, u32[]{:S(2)}, u32[]{:S(2)}) collective-permute-start(bf16[2,128,128]{2,1,0:T(8,128)(2,1)S(1)} %get-tuple-element.45), channel_id=1, source_target_pairs={{0,24},{4,28},{8,16},{12,20},{16,8},{20,12},{24,0},{28,4},{1,25},{... | collective-permute-start | bytes 196616 | tf_op jit(solution)/shard_map/ppermute | solution.py:20
  35.2 18.2 %copy-start = (bf16[1,1,1,32,128,128]{5,4,3,2,1,0:T(8,128)(2,1)S(1)}, bf16[1,1,1,32,128,128]{5,4,3,2,1,0:T(8,128)(2,1)}, u32[]{:S(2)}) copy-start(bf16[1,1,1,32,128,128]{5,4,3,2,1,0:T(8,128)(2,1)} %param.6) | copy-start | bytes 3145732
  35.4 7.9 %collective-permute-start.14 = (bf16[256,128]{1,0:T(8,128)(2,1)S(1)}, bf16[256,128]{1,0:T(8,128)(2,1)S(1)}, u32[]{:S(2)}, u32[]{:S(2)}) collective-permute-start(bf16[256,128]{1,0:T(8,128)(2,1)S(1)} %shard_map.67.refs_0_), channel_id=1, source_target_pairs={{0,28},{4,24},{8,20},{12,16},{16,12},{20,8},{24,4},{28,0},{1,29},{... | collective-permute-start | bytes 196616 | tf_op jit(solution)/shard_map/ppermute | solution.py:20
  38.5 6.4 %collective-permute-start.13 = (bf16[256,128]{1,0:T(8,128)(2,1)S(1)}, bf16[256,128]{1,0:T(8,128)(2,1)S(1)}, u32[]{:S(2)}, u32[]{:S(2)}) collective-permute-start(bf16[256,128]{1,0:T(8,128)(2,1)S(1)} %shard_map.67.refs_0_), channel_id=1, source_target_pairs={{0,24},{4,28},{8,16},{12,20},{16,8},{20,12},{24,0},{28,4},{1,25},{... | collective-permute-start | bytes 196616 | tf_op jit(solution)/shard_map/ppermute | solution.py:20
  40.5 6.6 %collective-permute-start.12 = (bf16[256,128]{1,0:T(8,128)(2,1)S(1)}, bf16[256,128]{1,0:T(8,128)(2,1)S(1)}, u32[]{:S(2)}, u32[]{:S(2)}) collective-permute-start(bf16[256,128]{1,0:T(8,128)(2,1)S(1)} %shard_map.67.refs_0_), channel_id=1, source_target_pairs={{0,20},{4,16},{8,28},{12,24},{16,4},{20,0},{24,12},{28,8},{1,21},{... | collective-permute-start | bytes 196616 | tf_op jit(solution)/shard_map/ppermute | solution.py:20
  40.5 7.1 %collective-permute-start.11 = (bf16[256,128]{1,0:T(8,128)(2,1)S(1)}, bf16[256,128]{1,0:T(8,128)(2,1)S(1)}, u32[]{:S(2)}, u32[]{:S(2)}) collective-permute-start(bf16[256,128]{1,0:T(8,128)(2,1)S(1)} %shard_map.67.refs_0_), channel_id=1, source_target_pairs={{0,16},{4,20},{8,24},{12,28},{16,0},{20,4},{24,8},{28,12},{1,17},{... | collective-permute-start | bytes 196616 | tf_op jit(solution)/shard_map/ppermute | solution.py:20
  43.2 5.2 %collective-permute-start.10 = (bf16[256,128]{1,0:T(8,128)(2,1)S(1)}, bf16[256,128]{1,0:T(8,128)(2,1)S(1)}, u32[]{:S(2)}, u32[]{:S(2)}) collective-permute-start(bf16[256,128]{1,0:T(8,128)(2,1)S(1)} %shard_map.67.refs_0_), channel_id=1, source_target_pairs={{0,12},{4,8},{8,4},{12,0},{16,28},{20,24},{24,20},{28,16},{1,13},{... | collective-permute-start | bytes 196616 | tf_op jit(solution)/shard_map/ppermute | solution.py:20
  44.8 4.4 %collective-permute-start.9 = (bf16[256,128]{1,0:T(8,128)(2,1)S(1)}, bf16[256,128]{1,0:T(8,128)(2,1)S(1)}, u32[]{:S(2)}, u32[]{:S(2)}) collective-permute-start(bf16[256,128]{1,0:T(8,128)(2,1)S(1)} %shard_map.67.refs_0_), channel_id=1, source_target_pairs={{0,8},{4,12},{8,0},{12,4},{16,24},{20,28},{24,16},{28,20},{1,9},{5... | collective-permute-start | bytes 196616 | tf_op jit(solution)/shard_map/ppermute | solution.py:20
  47.1 4.3 %collective-permute-start.8 = (bf16[256,128]{1,0:T(8,128)(2,1)S(1)}, bf16[256,128]{1,0:T(8,128)(2,1)S(1)}, u32[]{:S(2)}, u32[]{:S(2)}) collective-permute-start(bf16[256,128]{1,0:T(8,128)(2,1)S(1)} %shard_map.67.refs_0_), channel_id=1, source_target_pairs={{0,4},{4,0},{8,12},{12,8},{16,20},{20,16},{24,28},{28,24},{1,5},{5... | collective-permute-start | bytes 196616 | tf_op jit(solution)/shard_map/ppermute | solution.py:20
  51.5 2.0 %collective-permute-start.16 = (bf16[2048,128]{1,0:T(8,128)(2,1)S(1)}, bf16[2048,128]{1,0:T(8,128)(2,1)S(1)}, u32[]{:S(2)}, u32[]{:S(2)}) collective-permute-start(bf16[2048,128]{1,0:T(8,128)(2,1)S(1)} %get-tuple-element.48.own), channel_id=1, source_target_pairs={{0,1},{1,0},{2,3},{3,2},{4,5},{5,4},{6,7},{7,6},{8,9},{9,8},{10,11... | collective-permute-start | bytes 1572872 | tf_op jit(solution)/shard_map/ppermute | solution.py:20
  55.6 8.8 %collective-permute-start.17 = (bf16[2,4,128,128]{3,2,1,0:T(8,128)(2,1)S(1)}, bf16[2,4,128,128]{3,2,1,0:T(8,128)(2,1)S(1)}, u32[]{:S(2)}, u32[]{:S(2)}) collective-permute-start(bf16[2,4,128,128]{3,2,1,0:T(8,128)(2,1)S(1)} %get-tuple-element.50), channel_id=1, source_target_pairs={{0,2},{2,0},{1,3},{3,1},{4,6},{6,4},{5,7},{7,5},{8,10},{10,8},{9,1... | collective-permute-start | bytes 786440 | tf_op jit(solution)/shard_map/ppermute | solution.py:20
  56.3 8.5 %collective-permute-start.18 = (bf16[2,4,128,128]{3,2,1,0:T(8,128)(2,1)S(1)}, bf16[2,4,128,128]{3,2,1,0:T(8,128)(2,1)S(1)}, u32[]{:S(2)}, u32[]{:S(2)}) collective-permute-start(bf16[2,4,128,128]{3,2,1,0:T(8,128)(2,1)S(1)} %get-tuple-element.52), channel_id=1, source_target_pairs={{0,4},{4,0},{8,12},{12,8},{16,20},{20,16},{24,28},{28,24},{1,5},{5... | collective-permute-start | bytes 786440 | tf_op jit(solution)/shard_map/ppermute | solution.py:20
  64.9 5.0 %collective-permute-start.19 = (bf16[4,128,128]{2,1,0:T(8,128)(2,1)S(1)}, bf16[4,128,128]{2,1,0:T(8,128)(2,1)S(1)}, u32[]{:S(2)}, u32[]{:S(2)}) collective-permute-start(bf16[4,128,128]{2,1,0:T(8,128)(2,1)S(1)} %get-tuple-element.54), channel_id=1, source_target_pairs={{0,4},{4,0},{8,12},{12,8},{16,20},{20,16},{24,28},{28,24},{1,5},{5... | collective-permute-start | bytes 393224 | tf_op jit(solution)/shard_map/ppermute | solution.py:20
  66.7 5.0 %collective-permute-start.20 = (bf16[4,128,128]{2,1,0:T(8,128)(2,1)S(1)}, bf16[4,128,128]{2,1,0:T(8,128)(2,1)S(1)}, u32[]{:S(2)}, u32[]{:S(2)}) collective-permute-start(bf16[4,128,128]{2,1,0:T(8,128)(2,1)S(1)} %get-tuple-element.56), channel_id=1, source_target_pairs={{0,2},{2,0},{1,3},{3,1},{4,6},{6,4},{5,7},{7,5},{8,10},{10,8},{9,1... | collective-permute-start | bytes 393224 | tf_op jit(solution)/shard_map/ppermute | solution.py:20
  71.7 4.5 %collective-permute-start.21 = (bf16[2,128,128]{2,1,0:T(8,128)(2,1)S(1)}, bf16[2,128,128]{2,1,0:T(8,128)(2,1)S(1)}, u32[]{:S(2)}, u32[]{:S(2)}) collective-permute-start(bf16[2,128,128]{2,1,0:T(8,128)(2,1)S(1)} %get-tuple-element.58), channel_id=1, source_target_pairs={{0,8},{4,12},{8,0},{12,4},{16,24},{20,28},{24,16},{28,20},{1,9},{5... | collective-permute-start | bytes 196616 | tf_op jit(solution)/shard_map/ppermute | solution.py:20
  71.8 5.7 %collective-permute-start.22 = (bf16[2,128,128]{2,1,0:T(8,128)(2,1)S(1)}, bf16[2,128,128]{2,1,0:T(8,128)(2,1)S(1)}, u32[]{:S(2)}, u32[]{:S(2)}) collective-permute-start(bf16[2,128,128]{2,1,0:T(8,128)(2,1)S(1)} %get-tuple-element.59), channel_id=1, source_target_pairs={{0,16},{4,20},{8,24},{12,28},{16,0},{20,4},{24,8},{28,12},{1,17},{... | collective-permute-start | bytes 196616 | tf_op jit(solution)/shard_map/ppermute | solution.py:20
  74.1 6.2 %collective-permute-start.23 = (bf16[2,128,128]{2,1,0:T(8,128)(2,1)S(1)}, bf16[2,128,128]{2,1,0:T(8,128)(2,1)S(1)}, u32[]{:S(2)}, u32[]{:S(2)}) collective-permute-start(bf16[2,128,128]{2,1,0:T(8,128)(2,1)S(1)} %get-tuple-element.60), channel_id=1, source_target_pairs={{0,24},{4,28},{8,16},{12,20},{16,8},{20,12},{24,0},{28,4},{1,25},{... | collective-permute-start | bytes 196616 | tf_op jit(solution)/shard_map/ppermute | solution.py:20
  80.5 7.8 %collective-permute-start.30 = (bf16[256,128]{1,0:T(8,128)(2,1)S(1)}, bf16[256,128]{1,0:T(8,128)(2,1)S(1)}, u32[]{:S(2)}, u32[]{:S(2)}) collective-permute-start(bf16[256,128]{1,0:T(8,128)(2,1)S(1)} %shard_map.72.refs_0_), channel_id=1, source_target_pairs={{0,28},{4,24},{8,20},{12,16},{16,12},{20,8},{24,4},{28,0},{1,29},{... | collective-permute-start | bytes 196616 | tf_op jit(solution)/shard_map/ppermute | solution.py:20
  82.4 9.0 %collective-permute-start.29 = (bf16[256,128]{1,0:T(8,128)(2,1)S(1)}, bf16[256,128]{1,0:T(8,128)(2,1)S(1)}, u32[]{:S(2)}, u32[]{:S(2)}) collective-permute-start(bf16[256,128]{1,0:T(8,128)(2,1)S(1)} %shard_map.72.refs_0_), channel_id=1, source_target_pairs={{0,24},{4,28},{8,16},{12,20},{16,8},{20,12},{24,0},{28,4},{1,25},{... | collective-permute-start | bytes 196616 | tf_op jit(solution)/shard_map/ppermute | solution.py:20
  85.6 6.1 %collective-permute-start.28 = (bf16[256,128]{1,0:T(8,128)(2,1)S(1)}, bf16[256,128]{1,0:T(8,128)(2,1)S(1)}, u32[]{:S(2)}, u32[]{:S(2)}) collective-permute-start(bf16[256,128]{1,0:T(8,128)(2,1)S(1)} %shard_map.72.refs_0_), channel_id=1, source_target_pairs={{0,20},{4,16},{8,28},{12,24},{16,4},{20,0},{24,12},{28,8},{1,21},{... | collective-permute-start | bytes 196616 | tf_op jit(solution)/shard_map/ppermute | solution.py:20
  85.6 7.1 %collective-permute-start.27 = (bf16[256,128]{1,0:T(8,128)(2,1)S(1)}, bf16[256,128]{1,0:T(8,128)(2,1)S(1)}, u32[]{:S(2)}, u32[]{:S(2)}) collective-permute-start(bf16[256,128]{1,0:T(8,128)(2,1)S(1)} %shard_map.72.refs_0_), channel_id=1, source_target_pairs={{0,16},{4,20},{8,24},{12,28},{16,0},{20,4},{24,8},{28,12},{1,17},{... | collective-permute-start | bytes 196616 | tf_op jit(solution)/shard_map/ppermute | solution.py:20
  88.2 5.5 %collective-permute-start.26 = (bf16[256,128]{1,0:T(8,128)(2,1)S(1)}, bf16[256,128]{1,0:T(8,128)(2,1)S(1)}, u32[]{:S(2)}, u32[]{:S(2)}) collective-permute-start(bf16[256,128]{1,0:T(8,128)(2,1)S(1)} %shard_map.72.refs_0_), channel_id=1, source_target_pairs={{0,12},{4,8},{8,4},{12,0},{16,28},{20,24},{24,20},{28,16},{1,13},{... | collective-permute-start | bytes 196616 | tf_op jit(solution)/shard_map/ppermute | solution.py:20
  88.3 6.1 %collective-permute-start.25 = (bf16[256,128]{1,0:T(8,128)(2,1)S(1)}, bf16[256,128]{1,0:T(8,128)(2,1)S(1)}, u32[]{:S(2)}, u32[]{:S(2)}) collective-permute-start(bf16[256,128]{1,0:T(8,128)(2,1)S(1)} %shard_map.72.refs_0_), channel_id=1, source_target_pairs={{0,8},{4,12},{8,0},{12,4},{16,24},{20,28},{24,16},{28,20},{1,9},{5... | collective-permute-start | bytes 196616 | tf_op jit(solution)/shard_map/ppermute | solution.py:20
  91.4 4.3 %collective-permute-start.24 = (bf16[256,128]{1,0:T(8,128)(2,1)S(1)}, bf16[256,128]{1,0:T(8,128)(2,1)S(1)}, u32[]{:S(2)}, u32[]{:S(2)}) collective-permute-start(bf16[256,128]{1,0:T(8,128)(2,1)S(1)} %shard_map.72.refs_0_), channel_id=1, source_target_pairs={{0,4},{4,0},{8,12},{12,8},{16,20},{20,16},{24,28},{28,24},{1,5},{5... | collective-permute-start | bytes 196616 | tf_op jit(solution)/shard_map/ppermute | solution.py:20

commit v3 on v2

--- a/solution.py
+++ b/solution.py
@@ -18,6 +18,20 @@
 def exchange(array, axis, by):
     peers = lax.axis_size(axis)
     return lax.ppermute(array, axis, [(i, i ^ by) for i in range(peers)])
+
+
+def hop(array, piece, stage):
+    bins, srcs, cores = (lax.axis_size(a) for a in ("delay", "src", "tgt"))
+    pairs = []
+    for d in range(bins):
+        for s in range(srcs):
+            for t in range(cores):
+                over_src = (piece + t + stage) % 2 == 0
+                to = (d, s ^ 1) if over_src else (d ^ 1, s)
+                pairs.append(
+                    ((d * srcs + s) * cores + t, (to[0] * srcs + to[1]) * cores + t)
+                )
+    return lax.ppermute(array, ("delay", "src", "tgt"), pairs)
 
 
 def call(kernel, outs, specs, scratch, *args, grant=32 * MIB):
@@ -81,23 +95,40 @@
     lax.fori_loop(0, p.slots // GROUP, group, 0)
 
 
-def split_first(p, acc, outs):
-    src, x = lax.axis_index("src"), p.x()
-    a_outs, b_send, b_keep = outs[: p.srcs], outs[p.srcs], outs[p.srcs + 1]
-    unit = p.slice_rows
+def over_src(piece):
+    return ((lax.axis_index("tgt") + piece) & 1) == 0
+
+
+def split_first(p, source, outs, high):
+    y, x = lax.axis_index("src") & 1, p.x()
 
     def rows(s, xx, g, piece):
-        start = ((s * 2 + xx) * p.groups + g) * unit + piece * p.piece
-        return acc[pl.ds(pl.multiple_of(start, p.piece), p.piece)].astype(BF16)
-
-    for k, ref in enumerate(a_outs):
-        for xx in range(2):
+        start = (((high * 2 + s) * 2 + xx) * p.groups + g) * p.slice_rows
+        start = pl.multiple_of(start + piece * p.piece, p.piece)
+        return source[pl.ds(start, p.piece)].astype(BF16)
+
+    for piece in range(2):
+        send, keep = outs[2 * piece], outs[2 * piece + 1]
+        by_src = over_src(piece)
+        for j in range(2):
             for g in range(p.groups):
-                ref[xx, g] = rows(src ^ k, xx, g, 0)
-    for s in range(p.srcs):
-        for g in range(p.groups):
-            b_send[s, g] = rows(s, x ^ 1, g, 1)
-            b_keep[s, g] = rows(s, x, g, 1)
+                send[j, g] = rows(
+                    jnp.where(by_src, y ^ 1, j), jnp.where(by_src, j, x ^ 1), g, piece
+                )
+                keep[j, g] = rows(
+                    jnp.where(by_src, y, j), jnp.where(by_src, j, x), g, piece
+                )
+
+
+def split_kernel(p, source, *outs):
+    split_first(p, source, outs, 0)
+
+
+def hand_over(p, acc, outs):
+    if p.srcs == 2:
+        split_first(p, acc, outs, 0)
+    else:
+        outs[0][...] = acc[...].astype(BF16)
 
 
 def first_kernel(p, blocks_hbm, coords, counts, history_hbm, *rest):
@@ -132,7 +163,7 @@
 
     tile_product(p, acc, blocks, coords, counts, column, lambda i: block_copy(i).wait())
     own_half[...] = history[lax.axis_index("tgt")]
-    split_first(p, acc, outs)
+    hand_over(p, acc, outs)
 
 
 def later_kernel(p, blocks, coords, counts, own, other, *rest):
@@ -147,35 +178,29 @@
 
     acc[...] = jnp.zeros_like(acc)
     tile_product(p, acc, blocks, coords, counts, column)
-    split_first(p, acc, outs)
+    hand_over(p, acc, outs)
+
+
+def total(*terms):
+    value = terms[0].astype(F32)
+    for term in terms[1:]:
+        value = value + term.astype(F32)
+    return value.astype(BF16)
 
 
 def second_kernel(p, *refs):
-    n = p.srcs
-    a_keep, a_came = refs[0], refs[1:n]
-    b_keep, b_came = refs[n], refs[n + 1]
-    a_send, a_stay = refs[n + 2], refs[n + 3]
-    b_outs = refs[n + 4 :]
-    src, x = lax.axis_index("src"), p.x()
-
-    def a_sum(xx):
-        total = a_keep[xx].astype(F32)
-        for came in a_came:
-            total = total + came[xx].astype(F32)
-        return total.astype(BF16)
-
-    a_send[...] = a_sum(x ^ 1)
-    a_stay[...] = a_sum(x)
-    for k, ref in enumerate(b_outs):
-        s = src ^ k
-        ref[...] = (b_keep[s].astype(F32) + b_came[s].astype(F32)).astype(BF16)
+    ins, outs = refs[:4], refs[4:]
+    y, x = lax.axis_index("src") & 1, p.x()
+    for piece in range(2):
+        keep, came = ins[2 * piece : 2 * piece + 2]
+        send, stay = outs[2 * piece : 2 * piece + 2]
+        own = jnp.where(over_src(piece), x, y)
+        send[...] = total(keep[own ^ 1], came[own ^ 1])
+        stay[...] = total(keep[own], came[own])
 
 
 def third_kernel(p, *refs):
-    n = p.srcs
-    a_keep, a_came, b_keep = refs[:3]
-    b_came = refs[3 : n + 2]
-    outs = refs[n + 2 :]
+    ins, outs = refs[:4], refs[4:]
     if len(outs) > p.groups:
         mine, behind, *outs, onward = outs
 
@@ -187,14 +212,12 @@
         def _():
             onward[...] = behind[...]
 
-    mine = p.g()
+    here = p.g()
     for k, ref in enumerate(outs):
-        g = mine ^ k
-        ref[0] = (a_keep[g].astype(F32) + a_came[g].astype(F32)).astype(BF16)
-        total = b_keep[g].astype(F32)
-        for came in b_came:
-            total = total + came[g].astype(F32)
-        ref[1] = total.astype(BF16)
+        g = here ^ k
+        for piece in range(2):
+            stay, came = ins[2 * piece : 2 * piece + 2]
+            ref[piece] = total(stay[g], came[g])
 
 
 def current_kernel(p, step, keep, *refs):
@@ -221,10 +244,18 @@
     return pl.ds(pl.multiple_of(at, p.slice_rows), p.slice_rows)
 
 
+def join_slices(p, slices, out):
+    k = 0
+    for ref in slices:
+        for i in range(ref.shape[0] // p.slice_rows):
+            by = 2 * (k % p.groups) + k // p.groups
+            out[place_of(p, by)] = ref[i * p.slice_rows : (i + 1) * p.slice_rows]
+            k += 1
+
+
 def join_kernel(p, *refs):
     *slices, shifted, out, lagged = refs
-    for k, ref in enumerate(slices):
-        out[place_of(p, k)] = ref[...]
+    join_slices(p, slices, out)
     first_bin = lax.axis_index("delay") == 0
 
     @pl.when(first_bin)
@@ -239,45 +270,55 @@
 def last_kernel(p, before, *refs):
     *slices, out = refs
     out[: before.shape[0], 0] = before[...]
-    for k, ref in enumerate(slices):
-        out[before.shape[0], 0, place_of(p, k)] = ref[...]
+    join_slices(p, slices, out.at[before.shape[0], 0])
+
+
+def narrow(p, firsts):
+    if p.srcs == 2:
+        return firsts
+    rest = firsts[0]
+    by = p.srcs // 2
+    while by > 1:
+        upper = (lax.axis_index("src") // by) & 1
+        size = rest.shape[0] // 2
+        keep = lax.dynamic_slice_in_dim(rest, upper * size, size)
+        send = lax.dynamic_slice_in_dim(rest, (1 - upper) * size, size)
+        rest = total(keep, exchange(send, "src", by))
+        by //= 2
+    return call(
+        functools.partial(split_kernel, p), [p.shape(2, p.groups)] * 4, [VMEM], [], rest
+    )
 
 
 def field_sum(p, firsts, lagged):
-    n = p.srcs
     moved = []
     if lagged is not None:
         behind = lax.ppermute(
             lagged, "delay", [(i, i + 2) for i in range(1, p.bins - 2, 2)]
         )
         moved = [lagged, behind]
-    a_keep, a_sends = firsts[0], firsts[1:n]
-    b_send, b_keep = firsts[n], firsts[n + 1]
-    a_came = [exchange(v, "src", k) for k, v in enumerate(a_sends, 1)]
-    b_came = exchange(b_send, "delay", 1)
+    send0, keep0, send1, keep1 = narrow(p, firsts)
     one = p.shape(p.groups)
-    a_send, a_stay, b_stay, *b_sends = call(
+    send0, stay0, send1, stay1 = call(
         functools.partial(second_kernel, p),
-        [one] * (2 + n),
-        [VMEM] * (n + 2),
+        [one] * 4,
+        [VMEM] * 4,
         [],
-        a_keep,
-        *a_came,
-        b_keep,
-        b_came,
-    )
-    a_came = exchange(a_send, "delay", 1)
-    b_came = [exchange(v, "src", k) for k, v in enumerate(b_sends, 1)]
+        keep0,
+        hop(send0, 0, 0),
+        keep1,
+        hop(send1, 1, 0),
+    )
     terms = call(
         functools.partial(third_kernel, p),
         [p.shape(2)] * p.groups
         + [jax.ShapeDtypeStruct(v.shape, BF16) for v in moved[:1]],
-        [VMEM] * (n + 2 + len(moved)),
+        [VMEM] * (4 + len(moved)),
         [],
-        a_stay,
-        a_came,
-        b_stay,
-        *b_came,
+        stay0,
+        hop(send0, 0, 1),
+        stay1,
+        hop(send1, 1, 1),
         *moved,
     )
     shifted = None
@@ -295,16 +336,38 @@
     return [keep, *came], shifted
 
 
+def pack_kernel(*refs):
+    *ins, out = refs
+    rows = ins[0].shape[0]
+    for i, ref in enumerate(ins):
+        out[i * rows : (i + 1) * rows] = ref[...]
+
+
+def pack(p, parts):
+    return call(
+        pack_kernel,
+        [jax.ShapeDtypeStruct((len(parts) * p.slice_rows, p.width), BF16)],
+        [VMEM] * len(parts),
+        [],
+        *parts,
+    )[0]
+
+
+def gather(p, piece):
+    along = [exchange(piece, "delay", 2 * k) for k in range(1, p.groups)]
+    beside = exchange(piece, "delay", 1)
+    return [piece, *along, beside, *(exchange(v, "delay", 1) for v in along)]
+
+
 def shards(blocks, coords, counts, history, excitation, inverse):
     p = Plan(blocks, history)
     steps = excitation.shape[0]
     slot_blocks = blocks.reshape(blocks.shape[3:])
     places = coords.reshape(-1, 2).T
     used = counts.reshape(-1)
-    first_outs = (
-        [p.shape(2, p.groups)] * p.srcs
-        + [p.shape(p.srcs, p.groups)] * 2
-    )
+    first_outs = [p.shape(2, p.groups)] * 4
+    if p.srcs > 2:
+        first_outs = [jax.ShapeDtypeStruct((p.tile_rows, p.width), BF16)]
     half = jax.ShapeDtypeStruct((p.owned, p.width), BF16)
     acc = [pltpu.VMEM((p.tile_rows, p.width), F32)]
     *firsts, lagged = call(
@@ -337,7 +400,7 @@
             excitation,
             inverse,
         )[0]
-        slices = [piece] + [exchange(piece, "delay", k) for k in range(1, p.slices)]
+        slices = gather(p, piece)
         if not more:
             return call(
                 functools.partial(last_kernel, p),

time: 96.3 us -> 91.5 us (0.950)
  starting transfers between devices: 47.1 us -> 41.9 us
    ppermute x30 -> x22, starting transfers between devices: 46.4 us -> 25.8 us  [exchange(): return lax.ppermute(array, axis, [(i, i ^ by) for i in range(peers)])]
    ppermute x0 -> x8, waiting for transfers between devices: none -> 19.3 us  [hop(): return lax.ppermute(array, ('delay', 'src', 'tgt'), pairs)]
    ppermute x30 -> x22, waiting for transfers between devices: 40.6 us -> 22.1 us  [exchange(): return lax.ppermute(array, axis, [(i, i ^ by) for i in range(peers)])]
    ppermute x0 -> x8, starting transfers between devices: none -> 15.4 us  [hop(): return lax.ppermute(array, ('delay', 'src', 'tgt'), pairs)]
  transfers between devices with their start and end apart: 31 -> 31, of which waited for: 24 -> 19; matrix products, arithmetic and copies ran while one was open for 0% -> 0% of each run, Pallas kernels for 0% -> 0%
where the time goes in v3:
time: 91.5 us; the launch traced here: 92.3 us
  starting transfers between devices  41.9 us (46%)
  waiting for transfers between devices  41.4 us (45%)
  Pallas kernels  7.59 us (8%)
    ppermute x22, starting transfers between devices, exchange(): return lax.ppermute(array, axis, [(i, i ^ by) for i in range(peers)])  25.8 us
    ppermute x22, waiting for transfers between devices, exchange(): return lax.ppermute(array, axis, [(i, i ^ by) for i in range(peers)])  22.1 us
    ppermute x8, waiting for transfers between devices, hop(): return lax.ppermute(array, ('delay', 'src', 'tgt'), pairs)  19.3 us
    ppermute x8, starting transfers between devices, hop(): return lax.ppermute(array, ('delay', 'src', 'tgt'), pairs)  15.4 us
    pallas_call x10, Pallas kernels, call(): pl.pallas_call(kernel, out_shape=outs, in_specs=specs, out_specs=[VMEM] *...  7.59 us
  transfers between devices with their start and end apart: 31, of which 19 were waited for; matrix products, arithmetic and copies ran while one was open for 0% of the time, Pallas kernels for 0%

profile of v3, /device:TPU:0, one launch (start us, length us, event | category | flops | bytes accessed | tf_op | source)
XLA Modules:
  0.0 92.3 jit_solution(5640563899125960910)
XLA Ops:
  0.7 0.7 copy-done.3
  1.3 3.6 %shard_map.64 = (bf16[2,4,128,128]{3,2,1,0:T(8,128)(2,1)S(1)}, bf16[2,4,128,128]{3,2,1,0:T(8,128)(2,1)S(1)}, bf16[2,4,128,128]{3,2,1,0:T(8,128)(2,1)S(1)}, bf16[...) custom-call(bf16[32,128,128]{2,1,0:T(8,128)(2,1)} %bitcast.9, s32[2,32]{1,0:T(2,128)S(1)} %bitcast.12, ...), custom_call_target="tpu_custom_call" | custom-call | tf_op jit(solution)/shard_map/pallas_call | solution.py:38
  4.9 0.7 collective-permute-start.4
  5.6 2.8 %collective-permute-start = (bf16[2,4,128,128]{3,2,1,0:T(8,128)(2,1)S(1)}, bf16[2,4,128,128]{3,2,1,0:T(8,128)(2,1)S(1)}, u32[]{:S(2)}, u32[]{:S(2)}) collective-permute-start(bf16[2,4,128,128]{3,2,1,0:T(8,128)(2,1)S(1)} %get-tuple-element.34), channel_id=1, source_target_pairs={{0,2},{1,5},{2,0},{3,7},{4,6},{5,1},{6,4},{7,3},{8,10},{9,13},{10,... | collective-permute-start | bytes 786440 | tf_op jit(solution)/shard_map/ppermute | solution.py:34
  8.5 4.9 %collective-permute-start.1 = (bf16[2,4,128,128]{3,2,1,0:T(8,128)(2,1)S(1)}, bf16[2,4,128,128]{3,2,1,0:T(8,128)(2,1)S(1)}, u32[]{:S(2)}, u32[]{:S(2)}) collective-permute-start(bf16[2,4,128,128]{3,2,1,0:T(8,128)(2,1)S(1)} %get-tuple-element.36), channel_id=1, source_target_pairs={{0,4},{1,3},{2,6},{3,1},{4,0},{5,7},{6,2},{7,5},{8,12},{9,11},{10,... | collective-permute-start | bytes 786440 | tf_op jit(solution)/shard_map/ppermute | solution.py:34
  13.4 4.5 %collective-permute-done.1.refs_3_ = bf16[2,4,128,128]{3,2,1,0:T(8,128)(2,1)S(1)} collective-permute-done((bf16[2,4,128,128]{3,2,1,0:T(8,128)(2,1)S(1)}, bf16[2,4,128,128]{3,2,1,0:T(8,128)(2,1)S(1)}, u32[]{:S(2)}, u32[]{:S(2)}) %collective-permute-start.1) | collective-permute-done | bytes 262176 | tf_op jit(solution)/shard_map/ppermute | solution.py:34
  18.0 1.9 %collective-permute-start.2 = (bf16[4,128,128]{2,1,0:T(8,128)(2,1)S(1)}, bf16[4,128,128]{2,1,0:T(8,128)(2,1)S(1)}, u32[]{:S(2)}, u32[]{:S(2)}) collective-permute-start(bf16[4,128,128]{2,1,0:T(8,128)(2,1)S(1)} %get-tuple-element.38), channel_id=1, source_target_pairs={{0,4},{1,3},{2,6},{3,1},{4,0},{5,7},{6,2},{7,5},{8,12},{9,11},{10,... | collective-permute-start | bytes 393224 | tf_op jit(solution)/shard_map/ppermute | solution.py:34
  19.9 1.5 %collective-permute-start.3 = (bf16[4,128,128]{2,1,0:T(8,128)(2,1)S(1)}, bf16[4,128,128]{2,1,0:T(8,128)(2,1)S(1)}, u32[]{:S(2)}, u32[]{:S(2)}) collective-permute-start(bf16[4,128,128]{2,1,0:T(8,128)(2,1)S(1)} %get-tuple-element.40), channel_id=1, source_target_pairs={{0,2},{1,5},{2,0},{3,7},{4,6},{5,1},{6,4},{7,3},{8,10},{9,13},{10,... | collective-permute-start | bytes 393224 | tf_op jit(solution)/shard_map/ppermute | solution.py:34
  21.4 2.1 %collective-permute-done.2.refs_1_ = bf16[4,128,128]{2,1,0:T(8,128)(2,1)S(1)} collective-permute-done((bf16[4,128,128]{2,1,0:T(8,128)(2,1)S(1)}, bf16[4,128,128]{2,1,0:T(8,128)(2,1)S(1)}, u32[]{:S(2)}, u32[]{:S(2)}) %collective-permute-start.2) | collective-permute-done | bytes 131104 | tf_op jit(solution)/shard_map/ppermute | solution.py:34
  23.5 1.4 %collective-permute-done.3.refs_3_ = bf16[4,128,128]{2,1,0:T(8,128)(2,1)S(1)} collective-permute-done((bf16[4,128,128]{2,1,0:T(8,128)(2,1)S(1)}, bf16[4,128,128]{2,1,0:T(8,128)(2,1)S(1)}, u32[]{:S(2)}, u32[]{:S(2)}) %collective-permute-start.3) | collective-permute-done | bytes 131104 | tf_op jit(solution)/shard_map/ppermute | solution.py:34
  25.5 1.6 %collective-permute-start.5 = (bf16[2,128,128]{2,1,0:T(8,128)(2,1)S(1)}, bf16[2,128,128]{2,1,0:T(8,128)(2,1)S(1)}, u32[]{:S(2)}, u32[]{:S(2)}) collective-permute-start(bf16[2,128,128]{2,1,0:T(8,128)(2,1)S(1)} %get-tuple-element.43), channel_id=1, source_target_pairs={{0,8},{4,12},{8,0},{12,4},{16,24},{20,28},{24,16},{28,20},{1,9},{5... | collective-permute-start | bytes 196616 | tf_op jit(solution)/shard_map/ppermute | solution.py:20
  27.1 1.0 %collective-permute-start.6 = (bf16[2,128,128]{2,1,0:T(8,128)(2,1)S(1)}, bf16[2,128,128]{2,1,0:T(8,128)(2,1)S(1)}, u32[]{:S(2)}, u32[]{:S(2)}) collective-permute-start(bf16[2,128,128]{2,1,0:T(8,128)(2,1)S(1)} %get-tuple-element.44), channel_id=1, source_target_pairs={{0,16},{4,20},{8,24},{12,28},{16,0},{20,4},{24,8},{28,12},{1,17},{... | collective-permute-start | bytes 196616 | tf_op jit(solution)/shard_map/ppermute | solution.py:20
  28.1 1.8 %collective-permute-start.7 = (bf16[2,128,128]{2,1,0:T(8,128)(2,1)S(1)}, bf16[2,128,128]{2,1,0:T(8,128)(2,1)S(1)}, u32[]{:S(2)}, u32[]{:S(2)}) collective-permute-start(bf16[2,128,128]{2,1,0:T(8,128)(2,1)S(1)} %get-tuple-element.45), channel_id=1, source_target_pairs={{0,24},{4,28},{8,16},{12,20},{16,8},{20,12},{24,0},{28,4},{1,25},{... | collective-permute-start | bytes 196616 | tf_op jit(solution)/shard_map/ppermute | solution.py:20
  29.9 4.8 %collective-permute-done.6.refs_1_ = bf16[2,128,128]{2,1,0:T(8,128)(2,1)S(1)} collective-permute-done((bf16[2,128,128]{2,1,0:T(8,128)(2,1)S(1)}, bf16[2,128,128]{2,1,0:T(8,128)(2,1)S(1)}, u32[]{:S(2)}, u32[]{:S(2)}) %collective-permute-start.6) | collective-permute-done | bytes 65568 | tf_op jit(solution)/shard_map/ppermute | solution.py:20
  34.9 1.9 %collective-permute-start.10 = (bf16[256,128]{1,0:T(8,128)(2,1)S(1)}, bf16[256,128]{1,0:T(8,128)(2,1)S(1)}, u32[]{:S(2)}, u32[]{:S(2)}) collective-permute-start(bf16[256,128]{1,0:T(8,128)(2,1)S(1)} %shard_map.67.refs_0_), channel_id=1, source_target_pairs={{0,24},{4,28},{8,16},{12,20},{16,8},{20,12},{24,0},{28,4},{1,25},{... | collective-permute-start | bytes 196616 | tf_op jit(solution)/shard_map/ppermute | solution.py:20
  36.9 0.8 collective-permute-start.9
  37.7 1.7 %collective-permute-start.8 = (bf16[256,128]{1,0:T(8,128)(2,1)S(1)}, bf16[256,128]{1,0:T(8,128)(2,1)S(1)}, u32[]{:S(2)}, u32[]{:S(2)}) collective-permute-start(bf16[256,128]{1,0:T(8,128)(2,1)S(1)} %shard_map.67.refs_0_), channel_id=1, source_target_pairs={{0,8},{4,12},{8,0},{12,4},{16,24},{20,28},{24,16},{28,20},{1,9},{5... | collective-permute-start | bytes 196616 | tf_op jit(solution)/shard_map/ppermute | solution.py:20
  39.4 0.7 collective-permute-start.11
  40.1 1.2 %collective-permute-done.10.refs_3_ = bf16[256,128]{1,0:T(8,128)(2,1)S(1)} collective-permute-done((bf16[256,128]{1,0:T(8,128)(2,1)S(1)}, bf16[256,128]{1,0:T(8,128)(2,1)S(1)}, u32[]{:S(2)}, u32[]{:S(2)}) %collective-permute-start.10) | collective-permute-done | bytes 65568 | tf_op jit(solution)/shard_map/ppermute | solution.py:20
  41.8 1.2 %collective-permute-done.9.refs_2_ = bf16[256,128]{1,0:T(8,128)(2,1)S(1)} collective-permute-done((bf16[256,128]{1,0:T(8,128)(2,1)S(1)}, bf16[256,128]{1,0:T(8,128)(2,1)S(1)}, u32[]{:S(2)}, u32[]{:S(2)}) %collective-permute-start.9) | collective-permute-done | bytes 65568 | tf_op jit(solution)/shard_map/ppermute | solution.py:20
  43.3 1.6 %collective-permute-start.12 = (bf16[256,128]{1,0:T(8,128)(2,1)S(1)}, bf16[256,128]{1,0:T(8,128)(2,1)S(1)}, u32[]{:S(2)}, u32[]{:S(2)}) collective-permute-start(bf16[256,128]{1,0:T(8,128)(2,1)S(1)} %collective-permute-done.8.refs_1_), channel_id=1, source_target_pairs={{0,4},{4,0},{8,12},{12,8},{16,20},{20,16},{24,28},{28,24},{1,5},{5... | collective-permute-start | bytes 196616 | tf_op jit(solution)/shard_map/ppermute | solution.py:20
  45.0 0.6 collective-permute-done.14.refs_7_
  45.6 1.6 %collective-permute-done.13.refs_6_ = bf16[256,128]{1,0:T(8,128)(2,1)S(1)} collective-permute-done((bf16[256,128]{1,0:T(8,128)(2,1)S(1)}, bf16[256,128]{1,0:T(8,128)(2,1)S(1)}, u32[]{:S(2)}, u32[]{:S(2)}) %collective-permute-start.13) | collective-permute-done | bytes 65568 | tf_op jit(solution)/shard_map/ppermute | solution.py:20
  47.2 0.7 collective-permute-done.12.refs_5_
  48.1 1.9 %collective-permute-done.16.other = bf16[2048,128]{1,0:T(8,128)(2,1)S(1)} collective-permute-done((bf16[2048,128]{1,0:T(8,128)(2,1)S(1)}, bf16[2048,128]{1,0:T(8,128)(2,1)S(1)}, u32[]{:S(2)}, u32[]{:S(2)}) %collective-permute-start.16) | collective-permute-done | bytes 524320 | tf_op jit(solution)/shard_map/ppermute | solution.py:20
  50.0 2.1 %shard_map.69 = (bf16[2,4,128,128]{3,2,1,0:T(8,128)(2,1)S(1)}, bf16[2,4,128,128]{3,2,1,0:T(8,128)(2,1)S(1)}, bf16[2,4,128,128]{3,2,1,0:T(8,128)(2,1)S(1)}, bf16[2,4,128,128]{3,2,1,0:T(8,128)(2,1)S(1)}) custom-call(bf16[32,128,128]{2,1,0:T(8,128)(2,1)S(1)} %bitcast.10, s32[2,32]{1,0:T(2,128)S(1)} %bitcast.13, s32[1]{0:T(128)} %bitcast.8.counts, ...), custom_call_target="tpu_custom_call" | custom-call | tf_op jit(solution)/shard_map/pallas_call | solution.py:38
  52.1 0.8 collective-permute-start.17
  52.9 1.3 %collective-permute-start.18 = (bf16[2,4,128,128]{3,2,1,0:T(8,128)(2,1)S(1)}, bf16[2,4,128,128]{3,2,1,0:T(8,128)(2,1)S(1)}, u32[]{:S(2)}, u32[]{:S(2)}) collective-permute-start(bf16[2,4,128,128]{3,2,1,0:T(8,128)(2,1)S(1)} %get-tuple-element.52), channel_id=1, source_target_pairs={{0,4},{1,3},{2,6},{3,1},{4,0},{5,7},{6,2},{7,5},{8,12},{9,11},{10,... | collective-permute-start | bytes 786440 | tf_op jit(solution)/shard_map/ppermute | solution.py:34
  54.3 6.9 %collective-permute-done.17.refs_1_ = bf16[2,4,128,128]{3,2,1,0:T(8,128)(2,1)S(1)} collective-permute-done((bf16[2,4,128,128]{3,2,1,0:T(8,128)(2,1)S(1)}, bf16[2,4,128,128]{3,2,1,0:T(8,128)(2,1)S(1)}, u32[]{:S(2)}, u32[]{:S(2)}) %collective-permute-start.17) | collective-permute-done | bytes 262176 | tf_op jit(solution)/shard_map/ppermute | solution.py:34
  61.3 1.6 %collective-permute-start.19 = (bf16[4,128,128]{2,1,0:T(8,128)(2,1)S(1)}, bf16[4,128,128]{2,1,0:T(8,128)(2,1)S(1)}, u32[]{:S(2)}, u32[]{:S(2)}) collective-permute-start(bf16[4,128,128]{2,1,0:T(8,128)(2,1)S(1)} %get-tuple-element.54), channel_id=1, source_target_pairs={{0,4},{1,3},{2,6},{3,1},{4,0},{5,7},{6,2},{7,5},{8,12},{9,11},{10,... | collective-permute-start | bytes 393224 | tf_op jit(solution)/shard_map/ppermute | solution.py:34
  63.4 3.8 %collective-permute-done.19.refs_1_ = bf16[4,128,128]{2,1,0:T(8,128)(2,1)S(1)} collective-permute-done((bf16[4,128,128]{2,1,0:T(8,128)(2,1)S(1)}, bf16[4,128,128]{2,1,0:T(8,128)(2,1)S(1)}, u32[]{:S(2)}, u32[]{:S(2)}) %collective-permute-start.19) | collective-permute-done | bytes 131104 | tf_op jit(solution)/shard_map/ppermute | solution.py:34
  67.2 0.7 collective-permute-done.20.refs_3_
  67.9 1.0 %collective-permute-start.21 = (bf16[2,128,128]{2,1,0:T(8,128)(2,1)S(1)}, bf16[2,128,128]{2,1,0:T(8,128)(2,1)S(1)}, u32[]{:S(2)}, u32[]{:S(2)}) collective-permute-start(bf16[2,128,128]{2,1,0:T(8,128)(2,1)S(1)} %get-tuple-element.58), channel_id=1, source_target_pairs={{0,8},{4,12},{8,0},{12,4},{16,24},{20,28},{24,16},{28,20},{1,9},{5... | collective-permute-start | bytes 196616 | tf_op jit(solution)/shard_map/ppermute | solution.py:20
  68.9 1.0 %collective-permute-start.22 = (bf16[2,128,128]{2,1,0:T(8,128)(2,1)S(1)}, bf16[2,128,128]{2,1,0:T(8,128)(2,1)S(1)}, u32[]{:S(2)}, u32[]{:S(2)}) collective-permute-start(bf16[2,128,128]{2,1,0:T(8,128)(2,1)S(1)} %get-tuple-element.59), channel_id=1, source_target_pairs={{0,16},{4,20},{8,24},{12,28},{16,0},{20,4},{24,8},{28,12},{1,17},{... | collective-permute-start | bytes 196616 | tf_op jit(solution)/shard_map/ppermute | solution.py:20
  69.9 2.5 %collective-permute-start.23 = (bf16[2,128,128]{2,1,0:T(8,128)(2,1)S(1)}, bf16[2,128,128]{2,1,0:T(8,128)(2,1)S(1)}, u32[]{:S(2)}, u32[]{:S(2)}) collective-permute-start(bf16[2,128,128]{2,1,0:T(8,128)(2,1)S(1)} %get-tuple-element.60), channel_id=1, source_target_pairs={{0,24},{4,28},{8,16},{12,20},{16,8},{20,12},{24,0},{28,4},{1,25},{... | collective-permute-start | bytes 196616 | tf_op jit(solution)/shard_map/ppermute | solution.py:20
  72.3 4.6 %collective-permute-done.22.refs_1_ = bf16[2,128,128]{2,1,0:T(8,128)(2,1)S(1)} collective-permute-done((bf16[2,128,128]{2,1,0:T(8,128)(2,1)S(1)}, bf16[2,128,128]{2,1,0:T(8,128)(2,1)S(1)}, u32[]{:S(2)}, u32[]{:S(2)}) %collective-permute-start.22) | collective-permute-done | bytes 65568 | tf_op jit(solution)/shard_map/ppermute | solution.py:20
  77.1 1.7 %collective-permute-start.26 = (bf16[256,128]{1,0:T(8,128)(2,1)S(1)}, bf16[256,128]{1,0:T(8,128)(2,1)S(1)}, u32[]{:S(2)}, u32[]{:S(2)}) collective-permute-start(bf16[256,128]{1,0:T(8,128)(2,1)S(1)} %shard_map.72.refs_0_), channel_id=1, source_target_pairs={{0,24},{4,28},{8,16},{12,20},{16,8},{20,12},{24,0},{28,4},{1,25},{... | collective-permute-start | bytes 196616 | tf_op jit(solution)/shard_map/ppermute | solution.py:20
  78.8 1.2 %collective-permute-start.25 = (bf16[256,128]{1,0:T(8,128)(2,1)S(1)}, bf16[256,128]{1,0:T(8,128)(2,1)S(1)}, u32[]{:S(2)}, u32[]{:S(2)}) collective-permute-start(bf16[256,128]{1,0:T(8,128)(2,1)S(1)} %shard_map.72.refs_0_), channel_id=1, source_target_pairs={{0,16},{4,20},{8,24},{12,28},{16,0},{20,4},{24,8},{28,12},{1,17},{... | collective-permute-start | bytes 196616 | tf_op jit(solution)/shard_map/ppermute | solution.py:20
  80.0 1.6 %collective-permute-start.24 = (bf16[256,128]{1,0:T(8,128)(2,1)S(1)}, bf16[256,128]{1,0:T(8,128)(2,1)S(1)}, u32[]{:S(2)}, u32[]{:S(2)}) collective-permute-start(bf16[256,128]{1,0:T(8,128)(2,1)S(1)} %shard_map.72.refs_0_), channel_id=1, source_target_pairs={{0,8},{4,12},{8,0},{12,4},{16,24},{20,28},{24,16},{28,20},{1,9},{5... | collective-permute-start | bytes 196616 | tf_op jit(solution)/shard_map/ppermute | solution.py:20
  81.6 1.1 %collective-permute-start.27 = (bf16[256,128]{1,0:T(8,128)(2,1)S(1)}, bf16[256,128]{1,0:T(8,128)(2,1)S(1)}, u32[]{:S(2)}, u32[]{:S(2)}) collective-permute-start(bf16[256,128]{1,0:T(8,128)(2,1)S(1)} %shard_map.72.refs_0_), channel_id=1, source_target_pairs={{0,4},{4,0},{8,12},{12,8},{16,20},{20,16},{24,28},{28,24},{1,5},{5... | collective-permute-start | bytes 196616 | tf_op jit(solution)/shard_map/ppermute | solution.py:20
  82.7 0.8 collective-permute-done.26.refs_3_
  83.4 1.2 %collective-permute-start.30 = (bf16[256,128]{1,0:T(8,128)(2,1)S(1)}, bf16[256,128]{1,0:T(8,128)(2,1)S(1)}, u32[]{:S(2)}, u32[]{:S(2)}) collective-permute-start(bf16[256,128]{1,0:T(8,128)(2,1)S(1)} %collective-permute-done.26.refs_3_), channel_id=1, source_target_pairs={{0,4},{4,0},{8,12},{12,8},{16,20},{20,16},{24,28},{28,24},{1,5},{5... | collective-permute-start | bytes 196616 | tf_op jit(solution)/shard_map/ppermute | solution.py:20
  84.7 0.7 collective-permute-done.25.refs_2_
  85.4 1.7 %collective-permute-start.29 = (bf16[256,128]{1,0:T(8,128)(2,1)S(1)}, bf16[256,128]{1,0:T(8,128)(2,1)S(1)}, u32[]{:S(2)}, u32[]{:S(2)}) collective-permute-start(bf16[256,128]{1,0:T(8,128)(2,1)S(1)} %collective-permute-done.25.refs_2_), channel_id=1, source_target_pairs={{0,4},{4,0},{8,12},{12,8},{16,20},{20,16},{24,28},{28,24},{1,5},{5... | collective-permute-start | bytes 196616 | tf_op jit(solution)/shard_map/ppermute | solution.py:20
  87.4 0.6 collective-permute-done.30.refs_7_
  88.0 2.3 %collective-permute-done.29.refs_6_ = bf16[256,128]{1,0:T(8,128)(2,1)S(1)} collective-permute-done((bf16[256,128]{1,0:T(8,128)(2,1)S(1)}, bf16[256,128]{1,0:T(8,128)(2,1)S(1)}, u32[]{:S(2)}, u32[]{:S(2)}) %collective-permute-start.29) | collective-permute-done | bytes 65568 | tf_op jit(solution)/shard_map/ppermute | solution.py:20
  90.3 1.0 %collective-permute-done.28.refs_5_ = bf16[256,128]{1,0:T(8,128)(2,1)S(1)} collective-permute-done((bf16[256,128]{1,0:T(8,128)(2,1)S(1)}, bf16[256,128]{1,0:T(8,128)(2,1)S(1)}, u32[]{:S(2)}, u32[]{:S(2)}) %collective-permute-start.28) | collective-permute-done | bytes 65568 | tf_op jit(solution)/shard_map/ppermute | solution.py:20
  91.3 1.0 %shard_map.73 = bf16[2,1,2048,128]{3,2,1,0:T(8,128)(2,1)} custom-call(bf16[1,2048,128]{2,1,0:T(8,128)(2,1)S(1)} %bitcast.11, bf16[256,128]{1,0:T(8,128)(2,1)S(1)} %shard_map.72.refs_0_, bf16[256,128]{1,0:T(8,128)(2,1)S(1)} %collective-permute-done.24.refs_1_, bf16[256,128]{1,0:T(8,128)(2,1)S(1)} %collective-permute-done.25.refs_2_, ...), custom_call_target="tpu_custom_call" | custom-call | tf_op jit(solution)/shard_map/pallas_call | solution.py:38
  (32 shorter events, 3.2 us)
Async XLA Ops:
  0.7 0.7 copy-start.3
  4.9 20.0 %collective-permute-start.4 = (bf16[2048,128]{1,0:T(8,128)(2,1)S(1)}, bf16[2048,128]{1,0:T(8,128)(2,1)S(1)}, u32[]{:S(2)}, u32[]{:S(2)}) collective-permute-start(bf16[2048,128]{1,0:T(8,128)(2,1)S(1)} %get-tuple-element.41.refs_4_), channel_id=1, source_target_pairs={{4,12},{12,20},{20,28},{5,13},{13,21},{21,29},{6,14},{14,22},{22,3... | collective-permute-start | bytes 1572872 | tf_op jit(solution)/shard_map/ppermute | solution.py:296
  5.6 7.7 %collective-permute-start = (bf16[2,4,128,128]{3,2,1,0:T(8,128)(2,1)S(1)}, bf16[2,4,128,128]{3,2,1,0:T(8,128)(2,1)S(1)}, u32[]{:S(2)}, u32[]{:S(2)}) collective-permute-start(bf16[2,4,128,128]{3,2,1,0:T(8,128)(2,1)S(1)} %get-tuple-element.34), channel_id=1, source_target_pairs={{0,2},{1,5},{2,0},{3,7},{4,6},{5,1},{6,4},{7,3},{8,10},{9,13},{10,... | collective-permute-start | bytes 786440 | tf_op jit(solution)/shard_map/ppermute | solution.py:34
  8.5 9.4 %collective-permute-start.1 = (bf16[2,4,128,128]{3,2,1,0:T(8,128)(2,1)S(1)}, bf16[2,4,128,128]{3,2,1,0:T(8,128)(2,1)S(1)}, u32[]{:S(2)}, u32[]{:S(2)}) collective-permute-start(bf16[2,4,128,128]{3,2,1,0:T(8,128)(2,1)S(1)} %get-tuple-element.36), channel_id=1, source_target_pairs={{0,4},{1,3},{2,6},{3,1},{4,0},{5,7},{6,2},{7,5},{8,12},{9,11},{10,... | collective-permute-start | bytes 786440 | tf_op jit(solution)/shard_map/ppermute | solution.py:34
  18.0 16.7 %copy-start.1 = (bf16[2,1,2048,128]{3,2,1,0:T(8,128)(2,1)S(1)}, bf16[2,1,2048,128]{3,2,1,0:T(8,128)(2,1)}, u32[]{:S(2)}) copy-start(bf16[2,1,2048,128]{3,2,1,0:T(8,128)(2,1)} %refs_3_.3) | copy-start | bytes 3145732
  18.0 5.5 %collective-permute-start.2 = (bf16[4,128,128]{2,1,0:T(8,128)(2,1)S(1)}, bf16[4,128,128]{2,1,0:T(8,128)(2,1)S(1)}, u32[]{:S(2)}, u32[]{:S(2)}) collective-permute-start(bf16[4,128,128]{2,1,0:T(8,128)(2,1)S(1)} %get-tuple-element.38), channel_id=1, source_target_pairs={{0,4},{1,3},{2,6},{3,1},{4,0},{5,7},{6,2},{7,5},{8,12},{9,11},{10,... | collective-permute-start | bytes 393224 | tf_op jit(solution)/shard_map/ppermute | solution.py:34
  19.9 5.0 %collective-permute-start.3 = (bf16[4,128,128]{2,1,0:T(8,128)(2,1)S(1)}, bf16[4,128,128]{2,1,0:T(8,128)(2,1)S(1)}, u32[]{:S(2)}, u32[]{:S(2)}) collective-permute-start(bf16[4,128,128]{2,1,0:T(8,128)(2,1)S(1)} %get-tuple-element.40), channel_id=1, source_target_pairs={{0,2},{1,5},{2,0},{3,7},{4,6},{5,1},{6,4},{7,3},{8,10},{9,13},{10,... | collective-permute-start | bytes 393224 | tf_op jit(solution)/shard_map/ppermute | solution.py:34
  24.9 9.8 %copy-start.2 = (bf16[1,16,128,128]{3,2,1,0:T(8,128)(2,1)S(1)}, bf16[1,16,128,128]{3,2,1,0:T(8,128)(2,1)}, u32[]{:S(2)}) copy-start(bf16[1,16,128,128]{3,2,1,0:T(8,128)(2,1)} %refs_4_.3) | copy-start | bytes 1572868
  25.0 22.9 %collective-permute-start.15 = (bf16[2048,128]{1,0:T(8,128)(2,1)S(1)}, bf16[2048,128]{1,0:T(8,128)(2,1)S(1)}, u32[]{:S(2)}, u32[]{:S(2)}) collective-permute-start(bf16[2048,128]{1,0:T(8,128)(2,1)S(1)} %get-tuple-element.46), channel_id=1, source_target_pairs={{0,4},{4,0},{8,12},{12,8},{16,20},{20,16},{24,28},{28,24},{1,5},{5... | collective-permute-start | bytes 1572872 | tf_op jit(solution)/shard_map/ppermute | solution.py:20
  25.5 4.4 %collective-permute-start.5 = (bf16[2,128,128]{2,1,0:T(8,128)(2,1)S(1)}, bf16[2,128,128]{2,1,0:T(8,128)(2,1)S(1)}, u32[]{:S(2)}, u32[]{:S(2)}) collective-permute-start(bf16[2,128,128]{2,1,0:T(8,128)(2,1)S(1)} %get-tuple-element.43), channel_id=1, source_target_pairs={{0,8},{4,12},{8,0},{12,4},{16,24},{20,28},{24,16},{28,20},{1,9},{5... | collective-permute-start | bytes 196616 | tf_op jit(solution)/shard_map/ppermute | solution.py:20
  27.1 7.6 %collective-permute-start.6 = (bf16[2,128,128]{2,1,0:T(8,128)(2,1)S(1)}, bf16[2,128,128]{2,1,0:T(8,128)(2,1)S(1)}, u32[]{:S(2)}, u32[]{:S(2)}) collective-permute-start(bf16[2,128,128]{2,1,0:T(8,128)(2,1)S(1)} %get-tuple-element.44), channel_id=1, source_target_pairs={{0,16},{4,20},{8,24},{12,28},{16,0},{20,4},{24,8},{28,12},{1,17},{... | collective-permute-start | bytes 196616 | tf_op jit(solution)/shard_map/ppermute | solution.py:20
  28.1 6.6 %collective-permute-start.7 = (bf16[2,128,128]{2,1,0:T(8,128)(2,1)S(1)}, bf16[2,128,128]{2,1,0:T(8,128)(2,1)S(1)}, u32[]{:S(2)}, u32[]{:S(2)}) collective-permute-start(bf16[2,128,128]{2,1,0:T(8,128)(2,1)S(1)} %get-tuple-element.45), channel_id=1, source_target_pairs={{0,24},{4,28},{8,16},{12,20},{16,8},{20,12},{24,0},{28,4},{1,25},{... | collective-permute-start | bytes 196616 | tf_op jit(solution)/shard_map/ppermute | solution.py:20
  34.7 15.3 %copy-start = (bf16[1,1,1,32,128,128]{5,4,3,2,1,0:T(8,128)(2,1)S(1)}, bf16[1,1,1,32,128,128]{5,4,3,2,1,0:T(8,128)(2,1)}, u32[]{:S(2)}) copy-start(bf16[1,1,1,32,128,128]{5,4,3,2,1,0:T(8,128)(2,1)} %param.6) | copy-start | bytes 3145732
  34.9 6.4 %collective-permute-start.10 = (bf16[256,128]{1,0:T(8,128)(2,1)S(1)}, bf16[256,128]{1,0:T(8,128)(2,1)S(1)}, u32[]{:S(2)}, u32[]{:S(2)}) collective-permute-start(bf16[256,128]{1,0:T(8,128)(2,1)S(1)} %shard_map.67.refs_0_), channel_id=1, source_target_pairs={{0,24},{4,28},{8,16},{12,20},{16,8},{20,12},{24,0},{28,4},{1,25},{... | collective-permute-start | bytes 196616 | tf_op jit(solution)/shard_map/ppermute | solution.py:20
  36.9 6.1 %collective-permute-start.9 = (bf16[256,128]{1,0:T(8,128)(2,1)S(1)}, bf16[256,128]{1,0:T(8,128)(2,1)S(1)}, u32[]{:S(2)}, u32[]{:S(2)}) collective-permute-start(bf16[256,128]{1,0:T(8,128)(2,1)S(1)} %shard_map.67.refs_0_), channel_id=1, source_target_pairs={{0,16},{4,20},{8,24},{12,28},{16,0},{20,4},{24,8},{28,12},{1,17},{... | collective-permute-start | bytes 196616 | tf_op jit(solution)/shard_map/ppermute | solution.py:20
  37.7 5.7 %collective-permute-start.8 = (bf16[256,128]{1,0:T(8,128)(2,1)S(1)}, bf16[256,128]{1,0:T(8,128)(2,1)S(1)}, u32[]{:S(2)}, u32[]{:S(2)}) collective-permute-start(bf16[256,128]{1,0:T(8,128)(2,1)S(1)} %shard_map.67.refs_0_), channel_id=1, source_target_pairs={{0,8},{4,12},{8,0},{12,4},{16,24},{20,28},{24,16},{28,20},{1,9},{5... | collective-permute-start | bytes 196616 | tf_op jit(solution)/shard_map/ppermute | solution.py:20
  39.4 5.6 %collective-permute-start.11 = (bf16[256,128]{1,0:T(8,128)(2,1)S(1)}, bf16[256,128]{1,0:T(8,128)(2,1)S(1)}, u32[]{:S(2)}, u32[]{:S(2)}) collective-permute-start(bf16[256,128]{1,0:T(8,128)(2,1)S(1)} %shard_map.67.refs_0_), channel_id=1, source_target_pairs={{0,4},{4,0},{8,12},{12,8},{16,20},{20,16},{24,28},{28,24},{1,5},{5... | collective-permute-start | bytes 196616 | tf_op jit(solution)/shard_map/ppermute | solution.py:20
  41.3 4.3 %collective-permute-start.14 = (bf16[256,128]{1,0:T(8,128)(2,1)S(1)}, bf16[256,128]{1,0:T(8,128)(2,1)S(1)}, u32[]{:S(2)}, u32[]{:S(2)}) collective-permute-start(bf16[256,128]{1,0:T(8,128)(2,1)S(1)} %collective-permute-done.10.refs_3_), channel_id=1, source_target_pairs={{0,4},{4,0},{8,12},{12,8},{16,20},{20,16},{24,28},{28,24},{1,5},{5... | collective-permute-start | bytes 196616 | tf_op jit(solution)/shard_map/ppermute | solution.py:20
  42.9 4.3 %collective-permute-start.13 = (bf16[256,128]{1,0:T(8,128)(2,1)S(1)}, bf16[256,128]{1,0:T(8,128)(2,1)S(1)}, u32[]{:S(2)}, u32[]{:S(2)}) collective-permute-start(bf16[256,128]{1,0:T(8,128)(2,1)S(1)} %collective-permute-done.9.refs_2_), channel_id=1, source_target_pairs={{0,4},{4,0},{8,12},{12,8},{16,20},{20,16},{24,28},{28,24},{1,5},{5... | collective-permute-start | bytes 196616 | tf_op jit(solution)/shard_map/ppermute | solution.py:20
  43.3 4.6 %collective-permute-start.12 = (bf16[256,128]{1,0:T(8,128)(2,1)S(1)}, bf16[256,128]{1,0:T(8,128)(2,1)S(1)}, u32[]{:S(2)}, u32[]{:S(2)}) collective-permute-start(bf16[256,128]{1,0:T(8,128)(2,1)S(1)} %collective-permute-done.8.refs_1_), channel_id=1, source_target_pairs={{0,4},{4,0},{8,12},{12,8},{16,20},{20,16},{24,28},{28,24},{1,5},{5... | collective-permute-start | bytes 196616 | tf_op jit(solution)/shard_map/ppermute | solution.py:20
  48.0 2.0 %collective-permute-start.16 = (bf16[2048,128]{1,0:T(8,128)(2,1)S(1)}, bf16[2048,128]{1,0:T(8,128)(2,1)S(1)}, u32[]{:S(2)}, u32[]{:S(2)}) collective-permute-start(bf16[2048,128]{1,0:T(8,128)(2,1)S(1)} %get-tuple-element.48.own), channel_id=1, source_target_pairs={{0,1},{1,0},{2,3},{3,2},{4,5},{5,4},{6,7},{7,6},{8,9},{9,8},{10,11... | collective-permute-start | bytes 1572872 | tf_op jit(solution)/shard_map/ppermute | solution.py:20
  52.1 9.0 %collective-permute-start.17 = (bf16[2,4,128,128]{3,2,1,0:T(8,128)(2,1)S(1)}, bf16[2,4,128,128]{3,2,1,0:T(8,128)(2,1)S(1)}, u32[]{:S(2)}, u32[]{:S(2)}) collective-permute-start(bf16[2,4,128,128]{3,2,1,0:T(8,128)(2,1)S(1)} %get-tuple-element.50), channel_id=1, source_target_pairs={{0,2},{1,5},{2,0},{3,7},{4,6},{5,1},{6,4},{7,3},{8,10},{9,13},{10,... | collective-permute-start | bytes 786440 | tf_op jit(solution)/shard_map/ppermute | solution.py:34
  52.9 8.2 %collective-permute-start.18 = (bf16[2,4,128,128]{3,2,1,0:T(8,128)(2,1)S(1)}, bf16[2,4,128,128]{3,2,1,0:T(8,128)(2,1)S(1)}, u32[]{:S(2)}, u32[]{:S(2)}) collective-permute-start(bf16[2,4,128,128]{3,2,1,0:T(8,128)(2,1)S(1)} %get-tuple-element.52), channel_id=1, source_target_pairs={{0,4},{1,3},{2,6},{3,1},{4,0},{5,7},{6,2},{7,5},{8,12},{9,11},{10,... | collective-permute-start | bytes 786440 | tf_op jit(solution)/shard_map/ppermute | solution.py:34
  61.3 5.9 %collective-permute-start.19 = (bf16[4,128,128]{2,1,0:T(8,128)(2,1)S(1)}, bf16[4,128,128]{2,1,0:T(8,128)(2,1)S(1)}, u32[]{:S(2)}, u32[]{:S(2)}) collective-permute-start(bf16[4,128,128]{2,1,0:T(8,128)(2,1)S(1)} %get-tuple-element.54), channel_id=1, source_target_pairs={{0,4},{1,3},{2,6},{3,1},{4,0},{5,7},{6,2},{7,5},{8,12},{9,11},{10,... | collective-permute-start | bytes 393224 | tf_op jit(solution)/shard_map/ppermute | solution.py:34
  62.9 5.0 %collective-permute-start.20 = (bf16[4,128,128]{2,1,0:T(8,128)(2,1)S(1)}, bf16[4,128,128]{2,1,0:T(8,128)(2,1)S(1)}, u32[]{:S(2)}, u32[]{:S(2)}) collective-permute-start(bf16[4,128,128]{2,1,0:T(8,128)(2,1)S(1)} %get-tuple-element.56), channel_id=1, source_target_pairs={{0,2},{1,5},{2,0},{3,7},{4,6},{5,1},{6,4},{7,3},{8,10},{9,13},{10,... | collective-permute-start | bytes 393224 | tf_op jit(solution)/shard_map/ppermute | solution.py:34
  67.9 4.5 %collective-permute-start.21 = (bf16[2,128,128]{2,1,0:T(8,128)(2,1)S(1)}, bf16[2,128,128]{2,1,0:T(8,128)(2,1)S(1)}, u32[]{:S(2)}, u32[]{:S(2)}) collective-permute-start(bf16[2,128,128]{2,1,0:T(8,128)(2,1)S(1)} %get-tuple-element.58), channel_id=1, source_target_pairs={{0,8},{4,12},{8,0},{12,4},{16,24},{20,28},{24,16},{28,20},{1,9},{5... | collective-permute-start | bytes 196616 | tf_op jit(solution)/shard_map/ppermute | solution.py:20
  68.9 8.0 %collective-permute-start.22 = (bf16[2,128,128]{2,1,0:T(8,128)(2,1)S(1)}, bf16[2,128,128]{2,1,0:T(8,128)(2,1)S(1)}, u32[]{:S(2)}, u32[]{:S(2)}) collective-permute-start(bf16[2,128,128]{2,1,0:T(8,128)(2,1)S(1)} %get-tuple-element.59), channel_id=1, source_target_pairs={{0,16},{4,20},{8,24},{12,28},{16,0},{20,4},{24,8},{28,12},{1,17},{... | collective-permute-start | bytes 196616 | tf_op jit(solution)/shard_map/ppermute | solution.py:20
  69.9 7.0 %collective-permute-start.23 = (bf16[2,128,128]{2,1,0:T(8,128)(2,1)S(1)}, bf16[2,128,128]{2,1,0:T(8,128)(2,1)S(1)}, u32[]{:S(2)}, u32[]{:S(2)}) collective-permute-start(bf16[2,128,128]{2,1,0:T(8,128)(2,1)S(1)} %get-tuple-element.60), channel_id=1, source_target_pairs={{0,24},{4,28},{8,16},{12,20},{16,8},{20,12},{24,0},{28,4},{1,25},{... | collective-permute-start | bytes 196616 | tf_op jit(solution)/shard_map/ppermute | solution.py:20
  77.1 6.3 %collective-permute-start.26 = (bf16[256,128]{1,0:T(8,128)(2,1)S(1)}, bf16[256,128]{1,0:T(8,128)(2,1)S(1)}, u32[]{:S(2)}, u32[]{:S(2)}) collective-permute-start(bf16[256,128]{1,0:T(8,128)(2,1)S(1)} %shard_map.72.refs_0_), channel_id=1, source_target_pairs={{0,24},{4,28},{8,16},{12,20},{16,8},{20,12},{24,0},{28,4},{1,25},{... | collective-permute-start | bytes 196616 | tf_op jit(solution)/shard_map/ppermute | solution.py:20
  78.8 6.6 %collective-permute-start.25 = (bf16[256,128]{1,0:T(8,128)(2,1)S(1)}, bf16[256,128]{1,0:T(8,128)(2,1)S(1)}, u32[]{:S(2)}, u32[]{:S(2)}) collective-permute-start(bf16[256,128]{1,0:T(8,128)(2,1)S(1)} %shard_map.72.refs_0_), channel_id=1, source_target_pairs={{0,16},{4,20},{8,24},{12,28},{16,0},{20,4},{24,8},{28,12},{1,17},{... | collective-permute-start | bytes 196616 | tf_op jit(solution)/shard_map/ppermute | solution.py:20
  80.0 7.1 %collective-permute-start.24 = (bf16[256,128]{1,0:T(8,128)(2,1)S(1)}, bf16[256,128]{1,0:T(8,128)(2,1)S(1)}, u32[]{:S(2)}, u32[]{:S(2)}) collective-permute-start(bf16[256,128]{1,0:T(8,128)(2,1)S(1)} %shard_map.72.refs_0_), channel_id=1, source_target_pairs={{0,8},{4,12},{8,0},{12,4},{16,24},{20,28},{24,16},{28,20},{1,9},{5... | collective-permute-start | bytes 196616 | tf_op jit(solution)/shard_map/ppermute | solution.py:20
  81.6 5.8 %collective-permute-start.27 = (bf16[256,128]{1,0:T(8,128)(2,1)S(1)}, bf16[256,128]{1,0:T(8,128)(2,1)S(1)}, u32[]{:S(2)}, u32[]{:S(2)}) collective-permute-start(bf16[256,128]{1,0:T(8,128)(2,1)S(1)} %shard_map.72.refs_0_), channel_id=1, source_target_pairs={{0,4},{4,0},{8,12},{12,8},{16,20},{20,16},{24,28},{28,24},{1,5},{5... | collective-permute-start | bytes 196616 | tf_op jit(solution)/shard_map/ppermute | solution.py:20
  83.4 4.6 %collective-permute-start.30 = (bf16[256,128]{1,0:T(8,128)(2,1)S(1)}, bf16[256,128]{1,0:T(8,128)(2,1)S(1)}, u32[]{:S(2)}, u32[]{:S(2)}) collective-permute-start(bf16[256,128]{1,0:T(8,128)(2,1)S(1)} %collective-permute-done.26.refs_3_), channel_id=1, source_target_pairs={{0,4},{4,0},{8,12},{12,8},{16,20},{20,16},{24,28},{28,24},{1,5},{5... | collective-permute-start | bytes 196616 | tf_op jit(solution)/shard_map/ppermute | solution.py:20
  85.4 5.0 %collective-permute-start.29 = (bf16[256,128]{1,0:T(8,128)(2,1)S(1)}, bf16[256,128]{1,0:T(8,128)(2,1)S(1)}, u32[]{:S(2)}, u32[]{:S(2)}) collective-permute-start(bf16[256,128]{1,0:T(8,128)(2,1)S(1)} %collective-permute-done.25.refs_2_), channel_id=1, source_target_pairs={{0,4},{4,0},{8,12},{12,8},{16,20},{20,16},{24,28},{28,24},{1,5},{5... | collective-permute-start | bytes 196616 | tf_op jit(solution)/shard_map/ppermute | solution.py:20
  87.0 4.3 %collective-permute-start.28 = (bf16[256,128]{1,0:T(8,128)(2,1)S(1)}, bf16[256,128]{1,0:T(8,128)(2,1)S(1)}, u32[]{:S(2)}, u32[]{:S(2)}) collective-permute-start(bf16[256,128]{1,0:T(8,128)(2,1)S(1)} %collective-permute-done.24.refs_1_), channel_id=1, source_target_pairs={{0,4},{4,0},{8,12},{12,8},{16,20},{20,16},{24,28},{28,24},{1,5},{5... | collective-permute-start | bytes 196616 | tf_op jit(solution)/shard_map/ppermute | solution.py:20

commit v4 on v3

--- a/solution.py
+++ b/solution.py
@@ -71,7 +71,7 @@
         return jax.ShapeDtypeStruct((*lead, self.piece, self.width), BF16)
 
 
-GROUP = 4
+GROUP = 16
 
 
 def tile_product(p, acc, blocks, coords, counts, column, ready=None):
@@ -79,20 +79,16 @@
         if ready is not None:
             ready(i)
         slots = [i * GROUP + j for j in range(GROUP)]
-
-        @pl.when(slots[0] < counts[0])
-        def _():
-            products = [
-                jnp.dot(blocks[c], column(coords[1, c]), preferred_element_type=F32)
-                for c in slots
-            ]
-            for c, product in zip(slots, products):
-                at = pl.ds(pl.multiple_of(coords[0, c] * p.edge, p.edge), p.edge)
-                acc[at] += jnp.where(c < counts[0], product, 0.0)
-
+        products = [
+            jnp.dot(blocks[c], column(coords[1, c]), preferred_element_type=F32)
+            for c in slots
+        ]
+        for c, product in zip(slots, products):
+            at = pl.ds(pl.multiple_of(coords[0, c] * p.edge, p.edge), p.edge)
+            acc[at] += jnp.where(c < counts[0], product, 0.0)
         return carry
 
-    lax.fori_loop(0, p.slots // GROUP, group, 0)
+    lax.fori_loop(0, p.slots // GROUP, group, 0, unroll=ready is None)
 
 
 def over_src(piece):
@@ -131,8 +127,8 @@
         outs[0][...] = acc[...].astype(BF16)
 
 
-def first_kernel(p, blocks_hbm, coords, counts, history_hbm, *rest):
-    *outs, own_half, acc, blocks, history, block_sem, history_sem = rest
+def first_kernel(p, blocks_hbm, coords_hbm, counts, history_hbm, *rest):
+    *outs, own_half, acc, blocks, history, coords, block_sem, history_sem, coords_sem = rest
     per_half = p.owned // p.edge
     rows = p.owned // 2
     copies = [
@@ -149,6 +145,7 @@
         at = pl.ds(i * GROUP, GROUP)
         return pltpu.make_async_copy(blocks_hbm.at[at], blocks.at[at], block_sem.at[i])
 
+    copies.append(pltpu.make_async_copy(coords_hbm, coords, coords_sem))
     for copy in copies:
         copy.start()
     for i in range(p.slots // GROUP):
@@ -356,7 +353,8 @@
 def gather(p, piece):
     along = [exchange(piece, "delay", 2 * k) for k in range(1, p.groups)]
     beside = exchange(piece, "delay", 1)
-    return [piece, *along, beside, *(exchange(v, "delay", 1) for v in along)]
+    over = [exchange(piece, "delay", 2 * k + 1) if k in (1,) else exchange(v, "delay", 1) for k, v in enumerate(along, 1)]
+    return [piece, *along, beside, *over]
 
 
 def shards(blocks, coords, counts, history, excitation, inverse):
@@ -373,13 +371,15 @@
     *firsts, lagged = call(
         functools.partial(first_kernel, p),
         first_outs + [half],
-        [HBM, SMEM, SMEM, HBM],
+        [HBM, HBM, SMEM, HBM],
         acc
         + [
             pltpu.VMEM(slot_blocks.shape, BF16),
             pltpu.VMEM(history.shape[1:], BF16),
+            pltpu.SMEM(places.shape, places.dtype),
             pltpu.SemaphoreType.DMA((p.slots // GROUP,)),
             pltpu.SemaphoreType.DMA((p.halves, 2)),
+            pltpu.SemaphoreType.DMA,
         ],
         slot_blocks,
         places,

time: 91.5 us -> 87.6 us (0.957); the launches traced: 92.3 us -> 87.4 us
  Pallas kernels: 7.59 us -> 5.5 us
  starting transfers between devices: 41.9 us -> 40.4 us
  waiting for transfers between devices: 41.4 us -> 40.1 us
    pallas_call x10, Pallas kernels: 7.59 us -> 5.5 us  [call(): pl.pallas_call(kernel, out_shape=outs, in_specs=specs, out_specs=[VMEM] *...]
    ppermute x8, starting transfers between devices: 15.4 us -> 14.4 us  [hop(): return lax.ppermute(array, ('delay', 'src', 'tgt'), pairs)]
    ppermute x22, waiting for transfers between devices: 22.1 us -> 21.1 us  [exchange(): return lax.ppermute(array, axis, [(i, i ^ by) for i in range(peers)])]
  transfers between devices with their start and end apart: 31 -> 31, of which waited for: 19 -> 22; matrix products, arithmetic and copies ran while one was open for 0% -> 0% of each run, Pallas kernels for 0% -> 0%
where the time goes in v4:
time: 87.6 us; the launch traced here: 87.4 us
  starting transfers between devices  40.4 us (46%)
  waiting for transfers between devices  40.1 us (46%)
  Pallas kernels  5.5 us (6%)
    ppermute x22, starting transfers between devices, exchange(): return lax.ppermute(array, axis, [(i, i ^ by) for i in range(peers)])  25.2 us
    ppermute x22, waiting for transfers between devices, exchange(): return lax.ppermute(array, axis, [(i, i ^ by) for i in range(peers)])  21.1 us
    ppermute x8, waiting for transfers between devices, hop(): return lax.ppermute(array, ('delay', 'src', 'tgt'), pairs)  18.9 us
    ppermute x8, starting transfers between devices, hop(): return lax.ppermute(array, ('delay', 'src', 'tgt'), pairs)  14.4 us
    pallas_call x10, Pallas kernels, call(): pl.pallas_call(kernel, out_shape=outs, in_specs=specs, out_specs=[VMEM] *...  5.5 us
  transfers between devices with their start and end apart: 31, of which 22 were waited for; matrix products, arithmetic and copies ran while one was open for 0% of the time, Pallas kernels for 0%

profile of v4, /device:TPU:0, one launch (start us, length us, event | category | flops | bytes accessed | tf_op | source)
XLA Modules:
  0.0 87.4 jit_solution(2979690796809672941)
XLA Ops:
  0.7 0.7 copy-done.3
  1.3 2.2 %shard_map.64 = (bf16[2,4,128,128]{3,2,1,0:T(8,128)(2,1)S(1)}, bf16[2,4,128,128]{3,2,1,0:T(8,128)(2,1)S(1)}, bf16[2,4,128,128]{3,2,1,0:T(8,128)(2,1)S(1)}, bf16[...) custom-call(bf16[32,128,128]{2,1,0:T(8,128)(2,1)} %bitcast.9, s32[2,32]{1,0:T(2,128)S(1)} %bitcast.12, ...), custom_call_target="tpu_custom_call" | custom-call | tf_op jit(solution)/shard_map/pallas_call | solution.py:38
  3.6 0.7 collective-permute-start.4
  4.3 3.0 %collective-permute-start = (bf16[2,4,128,128]{3,2,1,0:T(8,128)(2,1)S(1)}, bf16[2,4,128,128]{3,2,1,0:T(8,128)(2,1)S(1)}, u32[]{:S(2)}, u32[]{:S(2)}) collective-permute-start(bf16[2,4,128,128]{3,2,1,0:T(8,128)(2,1)S(1)} %get-tuple-element.34), channel_id=1, source_target_pairs={{0,2},{1,5},{2,0},{3,7},{4,6},{5,1},{6,4},{7,3},{8,10},{9,13},{10,... | collective-permute-start | bytes 786440 | tf_op jit(solution)/shard_map/ppermute | solution.py:34
  7.3 4.3 %collective-permute-start.1 = (bf16[2,4,128,128]{3,2,1,0:T(8,128)(2,1)S(1)}, bf16[2,4,128,128]{3,2,1,0:T(8,128)(2,1)S(1)}, u32[]{:S(2)}, u32[]{:S(2)}) collective-permute-start(bf16[2,4,128,128]{3,2,1,0:T(8,128)(2,1)S(1)} %get-tuple-element.36), channel_id=1, source_target_pairs={{0,4},{1,3},{2,6},{3,1},{4,0},{5,7},{6,2},{7,5},{8,12},{9,11},{10,... | collective-permute-start | bytes 786440 | tf_op jit(solution)/shard_map/ppermute | solution.py:34
  11.7 4.5 %collective-permute-done.1.refs_3_ = bf16[2,4,128,128]{3,2,1,0:T(8,128)(2,1)S(1)} collective-permute-done((bf16[2,4,128,128]{3,2,1,0:T(8,128)(2,1)S(1)}, bf16[2,4,128,128]{3,2,1,0:T(8,128)(2,1)S(1)}, u32[]{:S(2)}, u32[]{:S(2)}) %collective-permute-start.1) | collective-permute-done | bytes 262176 | tf_op jit(solution)/shard_map/ppermute | solution.py:34
  16.3 1.9 %collective-permute-start.2 = (bf16[4,128,128]{2,1,0:T(8,128)(2,1)S(1)}, bf16[4,128,128]{2,1,0:T(8,128)(2,1)S(1)}, u32[]{:S(2)}, u32[]{:S(2)}) collective-permute-start(bf16[4,128,128]{2,1,0:T(8,128)(2,1)S(1)} %get-tuple-element.38), channel_id=1, source_target_pairs={{0,4},{1,3},{2,6},{3,1},{4,0},{5,7},{6,2},{7,5},{8,12},{9,11},{10,... | collective-permute-start | bytes 393224 | tf_op jit(solution)/shard_map/ppermute | solution.py:34
  18.2 1.5 %collective-permute-start.3 = (bf16[4,128,128]{2,1,0:T(8,128)(2,1)S(1)}, bf16[4,128,128]{2,1,0:T(8,128)(2,1)S(1)}, u32[]{:S(2)}, u32[]{:S(2)}) collective-permute-start(bf16[4,128,128]{2,1,0:T(8,128)(2,1)S(1)} %get-tuple-element.40), channel_id=1, source_target_pairs={{0,2},{1,5},{2,0},{3,7},{4,6},{5,1},{6,4},{7,3},{8,10},{9,13},{10,... | collective-permute-start | bytes 393224 | tf_op jit(solution)/shard_map/ppermute | solution.py:34
  19.7 2.3 %collective-permute-done.2.refs_1_ = bf16[4,128,128]{2,1,0:T(8,128)(2,1)S(1)} collective-permute-done((bf16[4,128,128]{2,1,0:T(8,128)(2,1)S(1)}, bf16[4,128,128]{2,1,0:T(8,128)(2,1)S(1)}, u32[]{:S(2)}, u32[]{:S(2)}) %collective-permute-start.2) | collective-permute-done | bytes 131104 | tf_op jit(solution)/shard_map/ppermute | solution.py:34
  21.9 1.2 %collective-permute-done.3.refs_3_ = bf16[4,128,128]{2,1,0:T(8,128)(2,1)S(1)} collective-permute-done((bf16[4,128,128]{2,1,0:T(8,128)(2,1)S(1)}, bf16[4,128,128]{2,1,0:T(8,128)(2,1)S(1)}, u32[]{:S(2)}, u32[]{:S(2)}) %collective-permute-start.3) | collective-permute-done | bytes 131104 | tf_op jit(solution)/shard_map/ppermute | solution.py:34
  23.7 1.5 %collective-permute-start.5 = (bf16[2,128,128]{2,1,0:T(8,128)(2,1)S(1)}, bf16[2,128,128]{2,1,0:T(8,128)(2,1)S(1)}, u32[]{:S(2)}, u32[]{:S(2)}) collective-permute-start(bf16[2,128,128]{2,1,0:T(8,128)(2,1)S(1)} %get-tuple-element.43), channel_id=1, source_target_pairs={{0,8},{4,12},{8,0},{12,4},{16,24},{20,28},{24,16},{28,20},{1,9},{5... | collective-permute-start | bytes 196616 | tf_op jit(solution)/shard_map/ppermute | solution.py:20
  25.3 1.2 %collective-permute-start.6 = (bf16[2,128,128]{2,1,0:T(8,128)(2,1)S(1)}, bf16[2,128,128]{2,1,0:T(8,128)(2,1)S(1)}, u32[]{:S(2)}, u32[]{:S(2)}) collective-permute-start(bf16[2,128,128]{2,1,0:T(8,128)(2,1)S(1)} %get-tuple-element.44), channel_id=1, source_target_pairs={{0,16},{4,20},{8,24},{12,28},{16,0},{20,4},{24,8},{28,12},{1,17},{... | collective-permute-start | bytes 196616 | tf_op jit(solution)/shard_map/ppermute | solution.py:20
  26.4 1.7 %collective-permute-start.7 = (bf16[2,128,128]{2,1,0:T(8,128)(2,1)S(1)}, bf16[2,128,128]{2,1,0:T(8,128)(2,1)S(1)}, u32[]{:S(2)}, u32[]{:S(2)}) collective-permute-start(bf16[2,128,128]{2,1,0:T(8,128)(2,1)S(1)} %get-tuple-element.45), channel_id=1, source_target_pairs={{0,24},{4,28},{8,16},{12,20},{16,8},{20,12},{24,0},{28,4},{1,25},{... | collective-permute-start | bytes 196616 | tf_op jit(solution)/shard_map/ppermute | solution.py:20
  28.6 3.1 %collective-permute-done.6.refs_1_ = bf16[2,128,128]{2,1,0:T(8,128)(2,1)S(1)} collective-permute-done((bf16[2,128,128]{2,1,0:T(8,128)(2,1)S(1)}, bf16[2,128,128]{2,1,0:T(8,128)(2,1)S(1)}, u32[]{:S(2)}, u32[]{:S(2)}) %collective-permute-start.6) | collective-permute-done | bytes 65568 | tf_op jit(solution)/shard_map/ppermute | solution.py:20
  31.6 0.9 %collective-permute-done.7.refs_2_ = bf16[2,128,128]{2,1,0:T(8,128)(2,1)S(1)} collective-permute-done((bf16[2,128,128]{2,1,0:T(8,128)(2,1)S(1)}, bf16[2,128,128]{2,1,0:T(8,128)(2,1)S(1)}, u32[]{:S(2)}, u32[]{:S(2)}) %collective-permute-start.7) | collective-permute-done | bytes 65568 | tf_op jit(solution)/shard_map/ppermute | solution.py:20
  32.7 2.2 %collective-permute-start.12 = (bf16[256,128]{1,0:T(8,128)(2,1)S(1)}, bf16[256,128]{1,0:T(8,128)(2,1)S(1)}, u32[]{:S(2)}, u32[]{:S(2)}) collective-permute-start(bf16[256,128]{1,0:T(8,128)(2,1)S(1)} %shard_map.67.refs_0_), channel_id=1, source_target_pairs={{0,12},{4,8},{8,4},{12,0},{16,28},{20,24},{24,20},{28,16},{1,13},{... | collective-permute-start | bytes 196616 | tf_op jit(solution)/shard_map/ppermute | solution.py:20
  34.9 1.5 %collective-permute-start.10 = (bf16[256,128]{1,0:T(8,128)(2,1)S(1)}, bf16[256,128]{1,0:T(8,128)(2,1)S(1)}, u32[]{:S(2)}, u32[]{:S(2)}) collective-permute-start(bf16[256,128]{1,0:T(8,128)(2,1)S(1)} %shard_map.67.refs_0_), channel_id=1, source_target_pairs={{0,24},{4,28},{8,16},{12,20},{16,8},{20,12},{24,0},{28,4},{1,25},{... | collective-permute-start | bytes 196616 | tf_op jit(solution)/shard_map/ppermute | solution.py:20
  36.5 0.8 collective-permute-start.9
  38.1 1.6 %collective-permute-start.8 = (bf16[256,128]{1,0:T(8,128)(2,1)S(1)}, bf16[256,128]{1,0:T(8,128)(2,1)S(1)}, u32[]{:S(2)}, u32[]{:S(2)}) collective-permute-start(bf16[256,128]{1,0:T(8,128)(2,1)S(1)} %shard_map.67.refs_0_), channel_id=1, source_target_pairs={{0,8},{4,12},{8,0},{12,4},{16,24},{20,28},{24,16},{28,20},{1,9},{5... | collective-permute-start | bytes 196616 | tf_op jit(solution)/shard_map/ppermute | solution.py:20
  39.7 1.3 %collective-permute-done.10.refs_3_ = bf16[256,128]{1,0:T(8,128)(2,1)S(1)} collective-permute-done((bf16[256,128]{1,0:T(8,128)(2,1)S(1)}, bf16[256,128]{1,0:T(8,128)(2,1)S(1)}, u32[]{:S(2)}, u32[]{:S(2)}) %collective-permute-start.10) | collective-permute-done | bytes 65568 | tf_op jit(solution)/shard_map/ppermute | solution.py:20
  41.4 1.2 %collective-permute-done.9.refs_2_ = bf16[256,128]{1,0:T(8,128)(2,1)S(1)} collective-permute-done((bf16[256,128]{1,0:T(8,128)(2,1)S(1)}, bf16[256,128]{1,0:T(8,128)(2,1)S(1)}, u32[]{:S(2)}, u32[]{:S(2)}) %collective-permute-start.9) | collective-permute-done | bytes 65568 | tf_op jit(solution)/shard_map/ppermute | solution.py:20
  42.6 0.5 collective-permute-start.13
  43.1 2.2 %collective-permute-done.14.refs_7_ = bf16[256,128]{1,0:T(8,128)(2,1)S(1)} collective-permute-done((bf16[256,128]{1,0:T(8,128)(2,1)S(1)}, bf16[256,128]{1,0:T(8,128)(2,1)S(1)}, u32[]{:S(2)}, u32[]{:S(2)}) %collective-permute-start.14) | collective-permute-done | bytes 65568 | tf_op jit(solution)/shard_map/ppermute | solution.py:20
  45.3 1.5 %collective-permute-done.13.refs_6_ = bf16[256,128]{1,0:T(8,128)(2,1)S(1)} collective-permute-done((bf16[256,128]{1,0:T(8,128)(2,1)S(1)}, bf16[256,128]{1,0:T(8,128)(2,1)S(1)}, u32[]{:S(2)}, u32[]{:S(2)}) %collective-permute-start.13) | collective-permute-done | bytes 65568 | tf_op jit(solution)/shard_map/ppermute | solution.py:20
  47.0 1.9 %collective-permute-done.16.other = bf16[2048,128]{1,0:T(8,128)(2,1)S(1)} collective-permute-done((bf16[2048,128]{1,0:T(8,128)(2,1)S(1)}, bf16[2048,128]{1,0:T(8,128)(2,1)S(1)}, u32[]{:S(2)}, u32[]{:S(2)}) %collective-permute-start.16) | collective-permute-done | bytes 524320 | tf_op jit(solution)/shard_map/ppermute | solution.py:20
  48.9 1.4 %shard_map.69 = (bf16[2,4,128,128]{3,2,1,0:T(8,128)(2,1)S(1)}, bf16[2,4,128,128]{3,2,1,0:T(8,128)(2,1)S(1)}, bf16[2,4,128,128]{3,2,1,0:T(8,128)(2,1)S(1)}, bf16[2,4,128,128]{3,2,1,0:T(8,128)(2,1)S(1)}) custom-call(bf16[32,128,128]{2,1,0:T(8,128)(2,1)S(1)} %bitcast.10, s32[2,32]{1,0:T(2,128)S(1)} %bitcast.13, s32[1]{0:T(128)} %bitcast.8.counts, ...), custom_call_target="tpu_custom_call" | custom-call | tf_op jit(solution)/shard_map/pallas_call | solution.py:38
  50.3 1.1 %collective-permute-start.17 = (bf16[2,4,128,128]{3,2,1,0:T(8,128)(2,1)S(1)}, bf16[2,4,128,128]{3,2,1,0:T(8,128)(2,1)S(1)}, u32[]{:S(2)}, u32[]{:S(2)}) collective-permute-start(bf16[2,4,128,128]{3,2,1,0:T(8,128)(2,1)S(1)} %get-tuple-element.50), channel_id=1, source_target_pairs={{0,2},{1,5},{2,0},{3,7},{4,6},{5,1},{6,4},{7,3},{8,10},{9,13},{10,... | collective-permute-start | bytes 786440 | tf_op jit(solution)/shard_map/ppermute | solution.py:34
  51.4 0.6 collective-permute-start.18
  52.0 7.0 %collective-permute-done.17.refs_1_ = bf16[2,4,128,128]{3,2,1,0:T(8,128)(2,1)S(1)} collective-permute-done((bf16[2,4,128,128]{3,2,1,0:T(8,128)(2,1)S(1)}, bf16[2,4,128,128]{3,2,1,0:T(8,128)(2,1)S(1)}, u32[]{:S(2)}, u32[]{:S(2)}) %collective-permute-start.17) | collective-permute-done | bytes 262176 | tf_op jit(solution)/shard_map/ppermute | solution.py:34
  59.1 0.9 %collective-permute-start.19 = (bf16[4,128,128]{2,1,0:T(8,128)(2,1)S(1)}, bf16[4,128,128]{2,1,0:T(8,128)(2,1)S(1)}, u32[]{:S(2)}, u32[]{:S(2)}) collective-permute-start(bf16[4,128,128]{2,1,0:T(8,128)(2,1)S(1)} %get-tuple-element.54), channel_id=1, source_target_pairs={{0,4},{1,3},{2,6},{3,1},{4,0},{5,7},{6,2},{7,5},{8,12},{9,11},{10,... | collective-permute-start | bytes 393224 | tf_op jit(solution)/shard_map/ppermute | solution.py:34
  59.9 1.1 %collective-permute-start.20 = (bf16[4,128,128]{2,1,0:T(8,128)(2,1)S(1)}, bf16[4,128,128]{2,1,0:T(8,128)(2,1)S(1)}, u32[]{:S(2)}, u32[]{:S(2)}) collective-permute-start(bf16[4,128,128]{2,1,0:T(8,128)(2,1)S(1)} %get-tuple-element.56), channel_id=1, source_target_pairs={{0,2},{1,5},{2,0},{3,7},{4,6},{5,1},{6,4},{7,3},{8,10},{9,13},{10,... | collective-permute-start | bytes 393224 | tf_op jit(solution)/shard_map/ppermute | solution.py:34
  61.1 4.0 %collective-permute-done.19.refs_1_ = bf16[4,128,128]{2,1,0:T(8,128)(2,1)S(1)} collective-permute-done((bf16[4,128,128]{2,1,0:T(8,128)(2,1)S(1)}, bf16[4,128,128]{2,1,0:T(8,128)(2,1)S(1)}, u32[]{:S(2)}, u32[]{:S(2)}) %collective-permute-start.19) | collective-permute-done | bytes 131104 | tf_op jit(solution)/shard_map/ppermute | solution.py:34
  65.1 0.7 collective-permute-start.21
  65.8 1.9 %collective-permute-start.22 = (bf16[2,128,128]{2,1,0:T(8,128)(2,1)S(1)}, bf16[2,128,128]{2,1,0:T(8,128)(2,1)S(1)}, u32[]{:S(2)}, u32[]{:S(2)}) collective-permute-start(bf16[2,128,128]{2,1,0:T(8,128)(2,1)S(1)} %get-tuple-element.59), channel_id=1, source_target_pairs={{0,16},{4,20},{8,24},{12,28},{16,0},{20,4},{24,8},{28,12},{1,17},{... | collective-permute-start | bytes 196616 | tf_op jit(solution)/shard_map/ppermute | solution.py:20
  67.7 1.8 %collective-permute-start.23 = (bf16[2,128,128]{2,1,0:T(8,128)(2,1)S(1)}, bf16[2,128,128]{2,1,0:T(8,128)(2,1)S(1)}, u32[]{:S(2)}, u32[]{:S(2)}) collective-permute-start(bf16[2,128,128]{2,1,0:T(8,128)(2,1)S(1)} %get-tuple-element.60), channel_id=1, source_target_pairs={{0,24},{4,28},{8,16},{12,20},{16,8},{20,12},{24,0},{28,4},{1,25},{... | collective-permute-start | bytes 196616 | tf_op jit(solution)/shard_map/ppermute | solution.py:20
  69.6 0.6 collective-permute-done.21.refs_0_
  70.2 3.8 %collective-permute-done.22.refs_1_ = bf16[2,128,128]{2,1,0:T(8,128)(2,1)S(1)} collective-permute-done((bf16[2,128,128]{2,1,0:T(8,128)(2,1)S(1)}, bf16[2,128,128]{2,1,0:T(8,128)(2,1)S(1)}, u32[]{:S(2)}, u32[]{:S(2)}) %collective-permute-start.22) | collective-permute-done | bytes 65568 | tf_op jit(solution)/shard_map/ppermute | solution.py:20
  74.1 1.8 %collective-permute-start.26 = (bf16[256,128]{1,0:T(8,128)(2,1)S(1)}, bf16[256,128]{1,0:T(8,128)(2,1)S(1)}, u32[]{:S(2)}, u32[]{:S(2)}) collective-permute-start(bf16[256,128]{1,0:T(8,128)(2,1)S(1)} %shard_map.72.refs_0_), channel_id=1, source_target_pairs={{0,24},{4,28},{8,16},{12,20},{16,8},{20,12},{24,0},{28,4},{1,25},{... | collective-permute-start | bytes 196616 | tf_op jit(solution)/shard_map/ppermute | solution.py:20
  75.9 1.0 %collective-permute-start.25 = (bf16[256,128]{1,0:T(8,128)(2,1)S(1)}, bf16[256,128]{1,0:T(8,128)(2,1)S(1)}, u32[]{:S(2)}, u32[]{:S(2)}) collective-permute-start(bf16[256,128]{1,0:T(8,128)(2,1)S(1)} %shard_map.72.refs_0_), channel_id=1, source_target_pairs={{0,16},{4,20},{8,24},{12,28},{16,0},{20,4},{24,8},{28,12},{1,17},{... | collective-permute-start | bytes 196616 | tf_op jit(solution)/shard_map/ppermute | solution.py:20
  76.9 2.2 %collective-permute-start.28 = (bf16[256,128]{1,0:T(8,128)(2,1)S(1)}, bf16[256,128]{1,0:T(8,128)(2,1)S(1)}, u32[]{:S(2)}, u32[]{:S(2)}) collective-permute-start(bf16[256,128]{1,0:T(8,128)(2,1)S(1)} %shard_map.72.refs_0_), channel_id=1, source_target_pairs={{0,12},{4,8},{8,4},{12,0},{16,28},{20,24},{24,20},{28,16},{1,13},{... | collective-permute-start | bytes 196616 | tf_op jit(solution)/shard_map/ppermute | solution.py:20
  79.1 0.9 %collective-permute-start.27 = (bf16[256,128]{1,0:T(8,128)(2,1)S(1)}, bf16[256,128]{1,0:T(8,128)(2,1)S(1)}, u32[]{:S(2)}, u32[]{:S(2)}) collective-permute-start(bf16[256,128]{1,0:T(8,128)(2,1)S(1)} %shard_map.72.refs_0_), channel_id=1, source_target_pairs={{0,4},{4,0},{8,12},{12,8},{16,20},{20,16},{24,28},{28,24},{1,5},{5... | collective-permute-start | bytes 196616 | tf_op jit(solution)/shard_map/ppermute | solution.py:20
  80.4 0.5 collective-permute-done.26.refs_3_
  81.0 1.1 %collective-permute-start.30 = (bf16[256,128]{1,0:T(8,128)(2,1)S(1)}, bf16[256,128]{1,0:T(8,128)(2,1)S(1)}, u32[]{:S(2)}, u32[]{:S(2)}) collective-permute-start(bf16[256,128]{1,0:T(8,128)(2,1)S(1)} %collective-permute-done.26.refs_3_), channel_id=1, source_target_pairs={{0,4},{4,0},{8,12},{12,8},{16,20},{20,16},{24,28},{28,24},{1,5},{5... | collective-permute-start | bytes 196616 | tf_op jit(solution)/shard_map/ppermute | solution.py:20
  82.1 1.0 %collective-permute-start.29 = (bf16[256,128]{1,0:T(8,128)(2,1)S(1)}, bf16[256,128]{1,0:T(8,128)(2,1)S(1)}, u32[]{:S(2)}, u32[]{:S(2)}) collective-permute-start(bf16[256,128]{1,0:T(8,128)(2,1)S(1)} %collective-permute-done.25.refs_2_), channel_id=1, source_target_pairs={{0,4},{4,0},{8,12},{12,8},{16,20},{20,16},{24,28},{28,24},{1,5},{5... | collective-permute-start | bytes 196616 | tf_op jit(solution)/shard_map/ppermute | solution.py:20
  83.3 0.9 %collective-permute-done.27.refs_4_ = bf16[256,128]{1,0:T(8,128)(2,1)S(1)} collective-permute-done((bf16[256,128]{1,0:T(8,128)(2,1)S(1)}, bf16[256,128]{1,0:T(8,128)(2,1)S(1)}, u32[]{:S(2)}, u32[]{:S(2)}) %collective-permute-start.27) | collective-permute-done | bytes 65568 | tf_op jit(solution)/shard_map/ppermute | solution.py:20
  84.3 0.9 %collective-permute-done.30.refs_7_ = bf16[256,128]{1,0:T(8,128)(2,1)S(1)} collective-permute-done((bf16[256,128]{1,0:T(8,128)(2,1)S(1)}, bf16[256,128]{1,0:T(8,128)(2,1)S(1)}, u32[]{:S(2)}, u32[]{:S(2)}) %collective-permute-start.30) | collective-permute-done | bytes 65568 | tf_op jit(solution)/shard_map/ppermute | solution.py:20
  85.2 1.1 %collective-permute-done.29.refs_6_ = bf16[256,128]{1,0:T(8,128)(2,1)S(1)} collective-permute-done((bf16[256,128]{1,0:T(8,128)(2,1)S(1)}, bf16[256,128]{1,0:T(8,128)(2,1)S(1)}, u32[]{:S(2)}, u32[]{:S(2)}) %collective-permute-start.29) | collective-permute-done | bytes 65568 | tf_op jit(solution)/shard_map/ppermute | solution.py:20
  86.4 1.0 %shard_map.73 = bf16[2,1,2048,128]{3,2,1,0:T(8,128)(2,1)} custom-call(bf16[1,2048,128]{2,1,0:T(8,128)(2,1)S(1)} %bitcast.11, bf16[256,128]{1,0:T(8,128)(2,1)S(1)} %shard_map.72.refs_0_, bf16[256,128]{1,0:T(8,128)(2,1)S(1)} %collective-permute-done.24.refs_1_, bf16[256,128]{1,0:T(8,128)(2,1)S(1)} %collective-permute-done.25.refs_2_, ...), custom_call_target="tpu_custom_call" | custom-call | tf_op jit(solution)/shard_map/pallas_call | solution.py:38
  (32 shorter events, 3.8 us)
Async XLA Ops:
  0.7 0.7 copy-start.3
  3.6 19.6 %collective-permute-start.4 = (bf16[2048,128]{1,0:T(8,128)(2,1)S(1)}, bf16[2048,128]{1,0:T(8,128)(2,1)S(1)}, u32[]{:S(2)}, u32[]{:S(2)}) collective-permute-start(bf16[2048,128]{1,0:T(8,128)(2,1)S(1)} %get-tuple-element.41.refs_4_), channel_id=1, source_target_pairs={{4,12},{12,20},{20,28},{5,13},{13,21},{21,29},{6,14},{14,22},{22,3... | collective-permute-start | bytes 1572872 | tf_op jit(solution)/shard_map/ppermute | solution.py:293
  4.3 7.4 %collective-permute-start = (bf16[2,4,128,128]{3,2,1,0:T(8,128)(2,1)S(1)}, bf16[2,4,128,128]{3,2,1,0:T(8,128)(2,1)S(1)}, u32[]{:S(2)}, u32[]{:S(2)}) collective-permute-start(bf16[2,4,128,128]{3,2,1,0:T(8,128)(2,1)S(1)} %get-tuple-element.34), channel_id=1, source_target_pairs={{0,2},{1,5},{2,0},{3,7},{4,6},{5,1},{6,4},{7,3},{8,10},{9,13},{10,... | collective-permute-start | bytes 786440 | tf_op jit(solution)/shard_map/ppermute | solution.py:34
  7.3 8.8 %collective-permute-start.1 = (bf16[2,4,128,128]{3,2,1,0:T(8,128)(2,1)S(1)}, bf16[2,4,128,128]{3,2,1,0:T(8,128)(2,1)S(1)}, u32[]{:S(2)}, u32[]{:S(2)}) collective-permute-start(bf16[2,4,128,128]{3,2,1,0:T(8,128)(2,1)S(1)} %get-tuple-element.36), channel_id=1, source_target_pairs={{0,4},{1,3},{2,6},{3,1},{4,0},{5,7},{6,2},{7,5},{8,12},{9,11},{10,... | collective-permute-start | bytes 786440 | tf_op jit(solution)/shard_map/ppermute | solution.py:34
  16.3 16.3 %copy-start.1 = (bf16[2,1,2048,128]{3,2,1,0:T(8,128)(2,1)S(1)}, bf16[2,1,2048,128]{3,2,1,0:T(8,128)(2,1)}, u32[]{:S(2)}) copy-start(bf16[2,1,2048,128]{3,2,1,0:T(8,128)(2,1)} %refs_3_.3) | copy-start | bytes 3145732
  16.3 5.7 %collective-permute-start.2 = (bf16[4,128,128]{2,1,0:T(8,128)(2,1)S(1)}, bf16[4,128,128]{2,1,0:T(8,128)(2,1)S(1)}, u32[]{:S(2)}, u32[]{:S(2)}) collective-permute-start(bf16[4,128,128]{2,1,0:T(8,128)(2,1)S(1)} %get-tuple-element.38), channel_id=1, source_target_pairs={{0,4},{1,3},{2,6},{3,1},{4,0},{5,7},{6,2},{7,5},{8,12},{9,11},{10,... | collective-permute-start | bytes 393224 | tf_op jit(solution)/shard_map/ppermute | solution.py:34
  18.2 5.0 %collective-permute-start.3 = (bf16[4,128,128]{2,1,0:T(8,128)(2,1)S(1)}, bf16[4,128,128]{2,1,0:T(8,128)(2,1)S(1)}, u32[]{:S(2)}, u32[]{:S(2)}) collective-permute-start(bf16[4,128,128]{2,1,0:T(8,128)(2,1)S(1)} %get-tuple-element.40), channel_id=1, source_target_pairs={{0,2},{1,5},{2,0},{3,7},{4,6},{5,1},{6,4},{7,3},{8,10},{9,13},{10,... | collective-permute-start | bytes 393224 | tf_op jit(solution)/shard_map/ppermute | solution.py:34
  23.2 9.4 %copy-start.2 = (bf16[1,16,128,128]{3,2,1,0:T(8,128)(2,1)S(1)}, bf16[1,16,128,128]{3,2,1,0:T(8,128)(2,1)}, u32[]{:S(2)}) copy-start(bf16[1,16,128,128]{3,2,1,0:T(8,128)(2,1)} %refs_4_.3) | copy-start | bytes 1572868
  23.3 23.5 %collective-permute-start.15 = (bf16[2048,128]{1,0:T(8,128)(2,1)S(1)}, bf16[2048,128]{1,0:T(8,128)(2,1)S(1)}, u32[]{:S(2)}, u32[]{:S(2)}) collective-permute-start(bf16[2048,128]{1,0:T(8,128)(2,1)S(1)} %get-tuple-element.46), channel_id=1, source_target_pairs={{0,4},{4,0},{8,12},{12,8},{16,20},{20,16},{24,28},{28,24},{1,5},{5... | collective-permute-start | bytes 1572872 | tf_op jit(solution)/shard_map/ppermute | solution.py:20
  23.7 4.8 %collective-permute-start.5 = (bf16[2,128,128]{2,1,0:T(8,128)(2,1)S(1)}, bf16[2,128,128]{2,1,0:T(8,128)(2,1)S(1)}, u32[]{:S(2)}, u32[]{:S(2)}) collective-permute-start(bf16[2,128,128]{2,1,0:T(8,128)(2,1)S(1)} %get-tuple-element.43), channel_id=1, source_target_pairs={{0,8},{4,12},{8,0},{12,4},{16,24},{20,28},{24,16},{28,20},{1,9},{5... | collective-permute-start | bytes 196616 | tf_op jit(solution)/shard_map/ppermute | solution.py:20
  25.3 6.4 %collective-permute-start.6 = (bf16[2,128,128]{2,1,0:T(8,128)(2,1)S(1)}, bf16[2,128,128]{2,1,0:T(8,128)(2,1)S(1)}, u32[]{:S(2)}, u32[]{:S(2)}) collective-permute-start(bf16[2,128,128]{2,1,0:T(8,128)(2,1)S(1)} %get-tuple-element.44), channel_id=1, source_target_pairs={{0,16},{4,20},{8,24},{12,28},{16,0},{20,4},{24,8},{28,12},{1,17},{... | collective-permute-start | bytes 196616 | tf_op jit(solution)/shard_map/ppermute | solution.py:20
  26.4 6.1 %collective-permute-start.7 = (bf16[2,128,128]{2,1,0:T(8,128)(2,1)S(1)}, bf16[2,128,128]{2,1,0:T(8,128)(2,1)S(1)}, u32[]{:S(2)}, u32[]{:S(2)}) collective-permute-start(bf16[2,128,128]{2,1,0:T(8,128)(2,1)S(1)} %get-tuple-element.45), channel_id=1, source_target_pairs={{0,24},{4,28},{8,16},{12,20},{16,8},{20,12},{24,0},{28,4},{1,25},{... | collective-permute-start | bytes 196616 | tf_op jit(solution)/shard_map/ppermute | solution.py:20
  32.5 16.4 %copy-start = (bf16[1,1,1,32,128,128]{5,4,3,2,1,0:T(8,128)(2,1)S(1)}, bf16[1,1,1,32,128,128]{5,4,3,2,1,0:T(8,128)(2,1)}, u32[]{:S(2)}) copy-start(bf16[1,1,1,32,128,128]{5,4,3,2,1,0:T(8,128)(2,1)} %param.6) | copy-start | bytes 3145732
  32.7 5.3 %collective-permute-start.12 = (bf16[256,128]{1,0:T(8,128)(2,1)S(1)}, bf16[256,128]{1,0:T(8,128)(2,1)S(1)}, u32[]{:S(2)}, u32[]{:S(2)}) collective-permute-start(bf16[256,128]{1,0:T(8,128)(2,1)S(1)} %shard_map.67.refs_0_), channel_id=1, source_target_pairs={{0,12},{4,8},{8,4},{12,0},{16,28},{20,24},{24,20},{28,16},{1,13},{... | collective-permute-start | bytes 196616 | tf_op jit(solution)/shard_map/ppermute | solution.py:20
  34.9 6.1 %collective-permute-start.10 = (bf16[256,128]{1,0:T(8,128)(2,1)S(1)}, bf16[256,128]{1,0:T(8,128)(2,1)S(1)}, u32[]{:S(2)}, u32[]{:S(2)}) collective-permute-start(bf16[256,128]{1,0:T(8,128)(2,1)S(1)} %shard_map.67.refs_0_), channel_id=1, source_target_pairs={{0,24},{4,28},{8,16},{12,20},{16,8},{20,12},{24,0},{28,4},{1,25},{... | collective-permute-start | bytes 196616 | tf_op jit(solution)/shard_map/ppermute | solution.py:20
  36.5 6.1 %collective-permute-start.9 = (bf16[256,128]{1,0:T(8,128)(2,1)S(1)}, bf16[256,128]{1,0:T(8,128)(2,1)S(1)}, u32[]{:S(2)}, u32[]{:S(2)}) collective-permute-start(bf16[256,128]{1,0:T(8,128)(2,1)S(1)} %shard_map.67.refs_0_), channel_id=1, source_target_pairs={{0,16},{4,20},{8,24},{12,28},{16,0},{20,4},{24,8},{28,12},{1,17},{... | collective-permute-start | bytes 196616 | tf_op jit(solution)/shard_map/ppermute | solution.py:20
  37.2 5.8 %collective-permute-start.11 = (bf16[256,128]{1,0:T(8,128)(2,1)S(1)}, bf16[256,128]{1,0:T(8,128)(2,1)S(1)}, u32[]{:S(2)}, u32[]{:S(2)}) collective-permute-start(bf16[256,128]{1,0:T(8,128)(2,1)S(1)} %shard_map.67.refs_0_), channel_id=1, source_target_pairs={{0,4},{4,0},{8,12},{12,8},{16,20},{20,16},{24,28},{28,24},{1,5},{5... | collective-permute-start | bytes 196616 | tf_op jit(solution)/shard_map/ppermute | solution.py:20
  38.1 5.0 %collective-permute-start.8 = (bf16[256,128]{1,0:T(8,128)(2,1)S(1)}, bf16[256,128]{1,0:T(8,128)(2,1)S(1)}, u32[]{:S(2)}, u32[]{:S(2)}) collective-permute-start(bf16[256,128]{1,0:T(8,128)(2,1)S(1)} %shard_map.67.refs_0_), channel_id=1, source_target_pairs={{0,8},{4,12},{8,0},{12,4},{16,24},{20,28},{24,16},{28,20},{1,9},{5... | collective-permute-start | bytes 196616 | tf_op jit(solution)/shard_map/ppermute | solution.py:20
  41.1 4.3 %collective-permute-start.14 = (bf16[256,128]{1,0:T(8,128)(2,1)S(1)}, bf16[256,128]{1,0:T(8,128)(2,1)S(1)}, u32[]{:S(2)}, u32[]{:S(2)}) collective-permute-start(bf16[256,128]{1,0:T(8,128)(2,1)S(1)} %collective-permute-done.10.refs_3_), channel_id=1, source_target_pairs={{0,4},{4,0},{8,12},{12,8},{16,20},{20,16},{24,28},{28,24},{1,5},{5... | collective-permute-start | bytes 196616 | tf_op jit(solution)/shard_map/ppermute | solution.py:20
  42.6 4.3 %collective-permute-start.13 = (bf16[256,128]{1,0:T(8,128)(2,1)S(1)}, bf16[256,128]{1,0:T(8,128)(2,1)S(1)}, u32[]{:S(2)}, u32[]{:S(2)}) collective-permute-start(bf16[256,128]{1,0:T(8,128)(2,1)S(1)} %collective-permute-done.9.refs_2_), channel_id=1, source_target_pairs={{0,4},{4,0},{8,12},{12,8},{16,20},{20,16},{24,28},{28,24},{1,5},{5... | collective-permute-start | bytes 196616 | tf_op jit(solution)/shard_map/ppermute | solution.py:20
  46.9 2.0 %collective-permute-start.16 = (bf16[2048,128]{1,0:T(8,128)(2,1)S(1)}, bf16[2048,128]{1,0:T(8,128)(2,1)S(1)}, u32[]{:S(2)}, u32[]{:S(2)}) collective-permute-start(bf16[2048,128]{1,0:T(8,128)(2,1)S(1)} %get-tuple-element.48.own), channel_id=1, source_target_pairs={{0,1},{1,0},{2,3},{3,2},{4,5},{5,4},{6,7},{7,6},{8,9},{9,8},{10,11... | collective-permute-start | bytes 1572872 | tf_op jit(solution)/shard_map/ppermute | solution.py:20
  50.3 8.7 %collective-permute-start.17 = (bf16[2,4,128,128]{3,2,1,0:T(8,128)(2,1)S(1)}, bf16[2,4,128,128]{3,2,1,0:T(8,128)(2,1)S(1)}, u32[]{:S(2)}, u32[]{:S(2)}) collective-permute-start(bf16[2,4,128,128]{3,2,1,0:T(8,128)(2,1)S(1)} %get-tuple-element.50), channel_id=1, source_target_pairs={{0,2},{1,5},{2,0},{3,7},{4,6},{5,1},{6,4},{7,3},{8,10},{9,13},{10,... | collective-permute-start | bytes 786440 | tf_op jit(solution)/shard_map/ppermute | solution.py:34
  51.4 7.6 %collective-permute-start.18 = (bf16[2,4,128,128]{3,2,1,0:T(8,128)(2,1)S(1)}, bf16[2,4,128,128]{3,2,1,0:T(8,128)(2,1)S(1)}, u32[]{:S(2)}, u32[]{:S(2)}) collective-permute-start(bf16[2,4,128,128]{3,2,1,0:T(8,128)(2,1)S(1)} %get-tuple-element.52), channel_id=1, source_target_pairs={{0,4},{1,3},{2,6},{3,1},{4,0},{5,7},{6,2},{7,5},{8,12},{9,11},{10,... | collective-permute-start | bytes 786440 | tf_op jit(solution)/shard_map/ppermute | solution.py:34
  59.1 6.0 %collective-permute-start.19 = (bf16[4,128,128]{2,1,0:T(8,128)(2,1)S(1)}, bf16[4,128,128]{2,1,0:T(8,128)(2,1)S(1)}, u32[]{:S(2)}, u32[]{:S(2)}) collective-permute-start(bf16[4,128,128]{2,1,0:T(8,128)(2,1)S(1)} %get-tuple-element.54), channel_id=1, source_target_pairs={{0,4},{1,3},{2,6},{3,1},{4,0},{5,7},{6,2},{7,5},{8,12},{9,11},{10,... | collective-permute-start | bytes 393224 | tf_op jit(solution)/shard_map/ppermute | solution.py:34
  59.9 5.1 %collective-permute-start.20 = (bf16[4,128,128]{2,1,0:T(8,128)(2,1)S(1)}, bf16[4,128,128]{2,1,0:T(8,128)(2,1)S(1)}, u32[]{:S(2)}, u32[]{:S(2)}) collective-permute-start(bf16[4,128,128]{2,1,0:T(8,128)(2,1)S(1)} %get-tuple-element.56), channel_id=1, source_target_pairs={{0,2},{1,5},{2,0},{3,7},{4,6},{5,1},{6,4},{7,3},{8,10},{9,13},{10,... | collective-permute-start | bytes 393224 | tf_op jit(solution)/shard_map/ppermute | solution.py:34
  65.1 5.0 %collective-permute-start.21 = (bf16[2,128,128]{2,1,0:T(8,128)(2,1)S(1)}, bf16[2,128,128]{2,1,0:T(8,128)(2,1)S(1)}, u32[]{:S(2)}, u32[]{:S(2)}) collective-permute-start(bf16[2,128,128]{2,1,0:T(8,128)(2,1)S(1)} %get-tuple-element.58), channel_id=1, source_target_pairs={{0,8},{4,12},{8,0},{12,4},{16,24},{20,28},{24,16},{28,20},{1,9},{5... | collective-permute-start | bytes 196616 | tf_op jit(solution)/shard_map/ppermute | solution.py:20
  65.8 8.1 %collective-permute-start.22 = (bf16[2,128,128]{2,1,0:T(8,128)(2,1)S(1)}, bf16[2,128,128]{2,1,0:T(8,128)(2,1)S(1)}, u32[]{:S(2)}, u32[]{:S(2)}) collective-permute-start(bf16[2,128,128]{2,1,0:T(8,128)(2,1)S(1)} %get-tuple-element.59), channel_id=1, source_target_pairs={{0,16},{4,20},{8,24},{12,28},{16,0},{20,4},{24,8},{28,12},{1,17},{... | collective-permute-start | bytes 196616 | tf_op jit(solution)/shard_map/ppermute | solution.py:20
  67.7 6.2 %collective-permute-start.23 = (bf16[2,128,128]{2,1,0:T(8,128)(2,1)S(1)}, bf16[2,128,128]{2,1,0:T(8,128)(2,1)S(1)}, u32[]{:S(2)}, u32[]{:S(2)}) collective-permute-start(bf16[2,128,128]{2,1,0:T(8,128)(2,1)S(1)} %get-tuple-element.60), channel_id=1, source_target_pairs={{0,24},{4,28},{8,16},{12,20},{16,8},{20,12},{24,0},{28,4},{1,25},{... | collective-permute-start | bytes 196616 | tf_op jit(solution)/shard_map/ppermute | solution.py:20
  74.1 6.8 %collective-permute-start.26 = (bf16[256,128]{1,0:T(8,128)(2,1)S(1)}, bf16[256,128]{1,0:T(8,128)(2,1)S(1)}, u32[]{:S(2)}, u32[]{:S(2)}) collective-permute-start(bf16[256,128]{1,0:T(8,128)(2,1)S(1)} %shard_map.72.refs_0_), channel_id=1, source_target_pairs={{0,24},{4,28},{8,16},{12,20},{16,8},{20,12},{24,0},{28,4},{1,25},{... | collective-permute-start | bytes 196616 | tf_op jit(solution)/shard_map/ppermute | solution.py:20
  75.9 6.2 %collective-permute-start.25 = (bf16[256,128]{1,0:T(8,128)(2,1)S(1)}, bf16[256,128]{1,0:T(8,128)(2,1)S(1)}, u32[]{:S(2)}, u32[]{:S(2)}) collective-permute-start(bf16[256,128]{1,0:T(8,128)(2,1)S(1)} %shard_map.72.refs_0_), channel_id=1, source_target_pairs={{0,16},{4,20},{8,24},{12,28},{16,0},{20,4},{24,8},{28,12},{1,17},{... | collective-permute-start | bytes 196616 | tf_op jit(solution)/shard_map/ppermute | solution.py:20
  76.9 6.4 %collective-permute-start.28 = (bf16[256,128]{1,0:T(8,128)(2,1)S(1)}, bf16[256,128]{1,0:T(8,128)(2,1)S(1)}, u32[]{:S(2)}, u32[]{:S(2)}) collective-permute-start(bf16[256,128]{1,0:T(8,128)(2,1)S(1)} %shard_map.72.refs_0_), channel_id=1, source_target_pairs={{0,12},{4,8},{8,4},{12,0},{16,28},{20,24},{24,20},{28,16},{1,13},{... | collective-permute-start | bytes 196616 | tf_op jit(solution)/shard_map/ppermute | solution.py:20
  79.1 5.1 %collective-permute-start.27 = (bf16[256,128]{1,0:T(8,128)(2,1)S(1)}, bf16[256,128]{1,0:T(8,128)(2,1)S(1)}, u32[]{:S(2)}, u32[]{:S(2)}) collective-permute-start(bf16[256,128]{1,0:T(8,128)(2,1)S(1)} %shard_map.72.refs_0_), channel_id=1, source_target_pairs={{0,4},{4,0},{8,12},{12,8},{16,20},{20,16},{24,28},{28,24},{1,5},{5... | collective-permute-start | bytes 196616 | tf_op jit(solution)/shard_map/ppermute | solution.py:20
  80.1 4.3 %collective-permute-start.24 = (bf16[256,128]{1,0:T(8,128)(2,1)S(1)}, bf16[256,128]{1,0:T(8,128)(2,1)S(1)}, u32[]{:S(2)}, u32[]{:S(2)}) collective-permute-start(bf16[256,128]{1,0:T(8,128)(2,1)S(1)} %shard_map.72.refs_0_), channel_id=1, source_target_pairs={{0,8},{4,12},{8,0},{12,4},{16,24},{20,28},{24,16},{28,20},{1,9},{5... | collective-permute-start | bytes 196616 | tf_op jit(solution)/shard_map/ppermute | solution.py:20
  81.0 4.3 %collective-permute-start.30 = (bf16[256,128]{1,0:T(8,128)(2,1)S(1)}, bf16[256,128]{1,0:T(8,128)(2,1)S(1)}, u32[]{:S(2)}, u32[]{:S(2)}) collective-permute-start(bf16[256,128]{1,0:T(8,128)(2,1)S(1)} %collective-permute-done.26.refs_3_), channel_id=1, source_target_pairs={{0,4},{4,0},{8,12},{12,8},{16,20},{20,16},{24,28},{28,24},{1,5},{5... | collective-permute-start | bytes 196616 | tf_op jit(solution)/shard_map/ppermute | solution.py:20
  82.1 4.3 %collective-permute-start.29 = (bf16[256,128]{1,0:T(8,128)(2,1)S(1)}, bf16[256,128]{1,0:T(8,128)(2,1)S(1)}, u32[]{:S(2)}, u32[]{:S(2)}) collective-permute-start(bf16[256,128]{1,0:T(8,128)(2,1)S(1)} %collective-permute-done.25.refs_2_), channel_id=1, source_target_pairs={{0,4},{4,0},{8,12},{12,8},{16,20},{20,16},{24,28},{28,24},{1,5},{5... | collective-permute-start | bytes 196616 | tf_op jit(solution)/shard_map/ppermute | solution.py:20

commit v5 on v4

--- a/solution.py
+++ b/solution.py
@@ -185,15 +185,10 @@
     return value.astype(BF16)
 
 
-def second_kernel(p, *refs):
-    ins, outs = refs[:4], refs[4:]
-    y, x = lax.axis_index("src") & 1, p.x()
-    for piece in range(2):
-        keep, came = ins[2 * piece : 2 * piece + 2]
-        send, stay = outs[2 * piece : 2 * piece + 2]
-        own = jnp.where(over_src(piece), x, y)
-        send[...] = total(keep[own ^ 1], came[own ^ 1])
-        stay[...] = total(keep[own], came[own])
+def second_kernel(p, piece, keep, came, send, stay):
+    own = jnp.where(over_src(piece), p.x(), lax.axis_index("src") & 1)
+    send[...] = total(keep[own ^ 1], came[own ^ 1])
+    stay[...] = total(keep[own], came[own])
 
 
 def third_kernel(p, *refs):
@@ -296,15 +291,12 @@
         moved = [lagged, behind]
     send0, keep0, send1, keep1 = narrow(p, firsts)
     one = p.shape(p.groups)
-    send0, stay0, send1, stay1 = call(
-        functools.partial(second_kernel, p),
-        [one] * 4,
-        [VMEM] * 4,
-        [],
-        keep0,
-        hop(send0, 0, 0),
-        keep1,
-        hop(send1, 1, 0),
+    came0, came1 = hop(send0, 0, 0), hop(send1, 1, 0)
+    send0, stay0 = call(
+        functools.partial(second_kernel, p, 0), [one] * 2, [VMEM] * 2, [], keep0, came0
+    )
+    send1, stay1 = call(
+        functools.partial(second_kernel, p, 1), [one] * 2, [VMEM] * 2, [], keep1, came1
     )
     terms = call(
         functools.partial(third_kernel, p),

time: 87.6 us -> 86.5 us (0.987)
  waiting for transfers between devices: 40.1 us -> 34.8 us
  starting transfers between devices: 40.4 us -> 44.6 us
    ppermute x8, starting transfers between devices: 14.4 us -> 19.9 us  [hop(): return lax.ppermute(array, ('delay', 'src', 'tgt'), pairs)]
    ppermute x8, waiting for transfers between devices: 18.9 us -> 13.5 us  [hop(): return lax.ppermute(array, ('delay', 'src', 'tgt'), pairs)]
    ppermute x22, starting transfers between devices: 25.2 us -> 24 us  [exchange(): return lax.ppermute(array, axis, [(i, i ^ by) for i in range(peers)])]
    pallas_call x10 -> x12, Pallas kernels: 5.5 us -> 5.51 us  [call(): pl.pallas_call(kernel, out_shape=outs, in_specs=specs, out_specs=[VMEM] *...]
where the time goes in v5:
time: 86.5 us; the launch traced here: 86.3 us
  starting transfers between devices  44.6 us (52%)
  waiting for transfers between devices  34.8 us (40%)
  Pallas kernels  5.51 us (6%)
    ppermute x22, starting transfers between devices, exchange(): return lax.ppermute(array, axis, [(i, i ^ by) for i in range(peers)])  24 us
    ppermute x22, waiting for transfers between devices, exchange(): return lax.ppermute(array, axis, [(i, i ^ by) for i in range(peers)])  21.3 us
    ppermute x8, starting transfers between devices, hop(): return lax.ppermute(array, ('delay', 'src', 'tgt'), pairs)  19.9 us
    ppermute x8, waiting for transfers between devices, hop(): return lax.ppermute(array, ('delay', 'src', 'tgt'), pairs)  13.5 us
    pallas_call x12, Pallas kernels, call(): pl.pallas_call(kernel, out_shape=outs, in_specs=specs, out_specs=[VMEM] *...  5.51 us
  transfers between devices with their start and end apart: 31, of which 22 were waited for; matrix products, arithmetic and copies ran while one was open for 0% of the time, Pallas kernels for 0%

profile of v5, /device:TPU:0, one launch (start us, length us, event | category | flops | bytes accessed | tf_op | source)
XLA Modules:
  0.0 86.3 jit_solution(11060078924988956227)
XLA Ops:
  0.7 0.7 copy-done.3
  1.3 2.2 %shard_map.64 = (bf16[2,4,128,128]{3,2,1,0:T(8,128)(2,1)S(1)}, bf16[2,4,128,128]{3,2,1,0:T(8,128)(2,1)S(1)}, bf16[2,4,128,128]{3,2,1,0:T(8,128)(2,1)S(1)}, bf16[...) custom-call(bf16[32,128,128]{2,1,0:T(8,128)(2,1)} %bitcast.9, s32[2,32]{1,0:T(2,128)S(1)} %bitcast.12, ...), custom_call_target="tpu_custom_call" | custom-call | tf_op jit(solution)/shard_map/pallas_call | solution.py:38
  3.6 0.7 collective-permute-start.4
  4.3 3.0 %collective-permute-start = (bf16[2,4,128,128]{3,2,1,0:T(8,128)(2,1)S(1)}, bf16[2,4,128,128]{3,2,1,0:T(8,128)(2,1)S(1)}, u32[]{:S(2)}, u32[]{:S(2)}) collective-permute-start(bf16[2,4,128,128]{3,2,1,0:T(8,128)(2,1)S(1)} %get-tuple-element.34), channel_id=1, source_target_pairs={{0,2},{1,5},{2,0},{3,7},{4,6},{5,1},{6,4},{7,3},{8,10},{9,13},{10,... | collective-permute-start | bytes 786440 | tf_op jit(solution)/shard_map/ppermute | solution.py:34
  7.3 4.3 %collective-permute-start.2 = (bf16[2,4,128,128]{3,2,1,0:T(8,128)(2,1)S(1)}, bf16[2,4,128,128]{3,2,1,0:T(8,128)(2,1)S(1)}, u32[]{:S(2)}, u32[]{:S(2)}) collective-permute-start(bf16[2,4,128,128]{3,2,1,0:T(8,128)(2,1)S(1)} %get-tuple-element.38), channel_id=1, source_target_pairs={{0,4},{1,3},{2,6},{3,1},{4,0},{5,7},{6,2},{7,5},{8,12},{9,11},{10,... | collective-permute-start | bytes 786440 | tf_op jit(solution)/shard_map/ppermute | solution.py:34
  11.7 6.3 %collective-permute-start.1 = (bf16[4,128,128]{2,1,0:T(8,128)(2,1)S(1)}, bf16[4,128,128]{2,1,0:T(8,128)(2,1)S(1)}, u32[]{:S(2)}, u32[]{:S(2)}) collective-permute-start(bf16[4,128,128]{2,1,0:T(8,128)(2,1)S(1)} %get-tuple-element.36), channel_id=1, source_target_pairs={{0,4},{1,3},{2,6},{3,1},{4,0},{5,7},{6,2},{7,5},{8,12},{9,11},{10,... | collective-permute-start | bytes 393224 | tf_op jit(solution)/shard_map/ppermute | solution.py:34
  18.1 1.6 %collective-permute-start.3 = (bf16[4,128,128]{2,1,0:T(8,128)(2,1)S(1)}, bf16[4,128,128]{2,1,0:T(8,128)(2,1)S(1)}, u32[]{:S(2)}, u32[]{:S(2)}) collective-permute-start(bf16[4,128,128]{2,1,0:T(8,128)(2,1)S(1)} %get-tuple-element.40), channel_id=1, source_target_pairs={{0,2},{1,5},{2,0},{3,7},{4,6},{5,1},{6,4},{7,3},{8,10},{9,13},{10,... | collective-permute-start | bytes 393224 | tf_op jit(solution)/shard_map/ppermute | solution.py:34
  19.7 1.7 %collective-permute-done.1.refs_1_ = bf16[4,128,128]{2,1,0:T(8,128)(2,1)S(1)} collective-permute-done((bf16[4,128,128]{2,1,0:T(8,128)(2,1)S(1)}, bf16[4,128,128]{2,1,0:T(8,128)(2,1)S(1)}, u32[]{:S(2)}, u32[]{:S(2)}) %collective-permute-start.1) | collective-permute-done | bytes 131104 | tf_op jit(solution)/shard_map/ppermute | solution.py:34
  21.4 1.7 %collective-permute-done.3.refs_3_ = bf16[4,128,128]{2,1,0:T(8,128)(2,1)S(1)} collective-permute-done((bf16[4,128,128]{2,1,0:T(8,128)(2,1)S(1)}, bf16[4,128,128]{2,1,0:T(8,128)(2,1)S(1)}, u32[]{:S(2)}, u32[]{:S(2)}) %collective-permute-start.3) | collective-permute-done | bytes 131104 | tf_op jit(solution)/shard_map/ppermute | solution.py:34
  23.4 1.6 %collective-permute-start.5 = (bf16[2,128,128]{2,1,0:T(8,128)(2,1)S(1)}, bf16[2,128,128]{2,1,0:T(8,128)(2,1)S(1)}, u32[]{:S(2)}, u32[]{:S(2)}) collective-permute-start(bf16[2,128,128]{2,1,0:T(8,128)(2,1)S(1)} %get-tuple-element.43), channel_id=1, source_target_pairs={{0,8},{4,12},{8,0},{12,4},{16,24},{20,28},{24,16},{28,20},{1,9},{5... | collective-permute-start | bytes 196616 | tf_op jit(solution)/shard_map/ppermute | solution.py:20
  25.0 1.4 %collective-permute-start.6 = (bf16[2,128,128]{2,1,0:T(8,128)(2,1)S(1)}, bf16[2,128,128]{2,1,0:T(8,128)(2,1)S(1)}, u32[]{:S(2)}, u32[]{:S(2)}) collective-permute-start(bf16[2,128,128]{2,1,0:T(8,128)(2,1)S(1)} %get-tuple-element.44), channel_id=1, source_target_pairs={{0,16},{4,20},{8,24},{12,28},{16,0},{20,4},{24,8},{28,12},{1,17},{... | collective-permute-start | bytes 196616 | tf_op jit(solution)/shard_map/ppermute | solution.py:20
  26.4 1.4 %collective-permute-start.7 = (bf16[2,128,128]{2,1,0:T(8,128)(2,1)S(1)}, bf16[2,128,128]{2,1,0:T(8,128)(2,1)S(1)}, u32[]{:S(2)}, u32[]{:S(2)}) collective-permute-start(bf16[2,128,128]{2,1,0:T(8,128)(2,1)S(1)} %get-tuple-element.45), channel_id=1, source_target_pairs={{0,24},{4,28},{8,16},{12,20},{16,8},{20,12},{24,0},{28,4},{1,25},{... | collective-permute-start | bytes 196616 | tf_op jit(solution)/shard_map/ppermute | solution.py:20
  27.8 3.4 %collective-permute-done.6.refs_1_ = bf16[2,128,128]{2,1,0:T(8,128)(2,1)S(1)} collective-permute-done((bf16[2,128,128]{2,1,0:T(8,128)(2,1)S(1)}, bf16[2,128,128]{2,1,0:T(8,128)(2,1)S(1)}, u32[]{:S(2)}, u32[]{:S(2)}) %collective-permute-start.6) | collective-permute-done | bytes 65568 | tf_op jit(solution)/shard_map/ppermute | solution.py:20
  31.3 1.3 %collective-permute-done.7.refs_2_ = bf16[2,128,128]{2,1,0:T(8,128)(2,1)S(1)} collective-permute-done((bf16[2,128,128]{2,1,0:T(8,128)(2,1)S(1)}, bf16[2,128,128]{2,1,0:T(8,128)(2,1)S(1)}, u32[]{:S(2)}, u32[]{:S(2)}) %collective-permute-start.7) | collective-permute-done | bytes 65568 | tf_op jit(solution)/shard_map/ppermute | solution.py:20
  32.8 1.9 %collective-permute-start.12 = (bf16[256,128]{1,0:T(8,128)(2,1)S(1)}, bf16[256,128]{1,0:T(8,128)(2,1)S(1)}, u32[]{:S(2)}, u32[]{:S(2)}) collective-permute-start(bf16[256,128]{1,0:T(8,128)(2,1)S(1)} %shard_map.68.refs_0_), channel_id=1, source_target_pairs={{0,12},{4,8},{8,4},{12,0},{16,28},{20,24},{24,20},{28,16},{1,13},{... | collective-permute-start | bytes 196616 | tf_op jit(solution)/shard_map/ppermute | solution.py:20
  34.6 1.6 %collective-permute-start.10 = (bf16[256,128]{1,0:T(8,128)(2,1)S(1)}, bf16[256,128]{1,0:T(8,128)(2,1)S(1)}, u32[]{:S(2)}, u32[]{:S(2)}) collective-permute-start(bf16[256,128]{1,0:T(8,128)(2,1)S(1)} %shard_map.68.refs_0_), channel_id=1, source_target_pairs={{0,24},{4,28},{8,16},{12,20},{16,8},{20,12},{24,0},{28,4},{1,25},{... | collective-permute-start | bytes 196616 | tf_op jit(solution)/shard_map/ppermute | solution.py:20
  36.2 1.1 %collective-permute-start.9 = (bf16[256,128]{1,0:T(8,128)(2,1)S(1)}, bf16[256,128]{1,0:T(8,128)(2,1)S(1)}, u32[]{:S(2)}, u32[]{:S(2)}) collective-permute-start(bf16[256,128]{1,0:T(8,128)(2,1)S(1)} %shard_map.68.refs_0_), channel_id=1, source_target_pairs={{0,16},{4,20},{8,24},{12,28},{16,0},{20,4},{24,8},{28,12},{1,17},{... | collective-permute-start | bytes 196616 | tf_op jit(solution)/shard_map/ppermute | solution.py:20
  37.3 0.5 collective-permute-start.11
  37.8 1.2 %collective-permute-done.12.refs_5_ = bf16[256,128]{1,0:T(8,128)(2,1)S(1)} collective-permute-done((bf16[256,128]{1,0:T(8,128)(2,1)S(1)}, bf16[256,128]{1,0:T(8,128)(2,1)S(1)}, u32[]{:S(2)}, u32[]{:S(2)}) %collective-permute-start.12) | collective-permute-done | bytes 65568 | tf_op jit(solution)/shard_map/ppermute | solution.py:20
  39.3 1.4 %collective-permute-done.10.refs_3_ = bf16[256,128]{1,0:T(8,128)(2,1)S(1)} collective-permute-done((bf16[256,128]{1,0:T(8,128)(2,1)S(1)}, bf16[256,128]{1,0:T(8,128)(2,1)S(1)}, u32[]{:S(2)}, u32[]{:S(2)}) %collective-permute-start.10) | collective-permute-done | bytes 65568 | tf_op jit(solution)/shard_map/ppermute | solution.py:20
  41.1 1.0 %collective-permute-done.9.refs_2_ = bf16[256,128]{1,0:T(8,128)(2,1)S(1)} collective-permute-done((bf16[256,128]{1,0:T(8,128)(2,1)S(1)}, bf16[256,128]{1,0:T(8,128)(2,1)S(1)}, u32[]{:S(2)}, u32[]{:S(2)}) %collective-permute-start.9) | collective-permute-done | bytes 65568 | tf_op jit(solution)/shard_map/ppermute | solution.py:20
  42.1 0.6 collective-permute-start.13
  42.7 0.5 collective-permute-done.8.refs_1_
  43.2 1.7 %collective-permute-done.14.refs_7_ = bf16[256,128]{1,0:T(8,128)(2,1)S(1)} collective-permute-done((bf16[256,128]{1,0:T(8,128)(2,1)S(1)}, bf16[256,128]{1,0:T(8,128)(2,1)S(1)}, u32[]{:S(2)}, u32[]{:S(2)}) %collective-permute-start.14) | collective-permute-done | bytes 65568 | tf_op jit(solution)/shard_map/ppermute | solution.py:20
  45.0 1.4 %collective-permute-done.13.refs_6_ = bf16[256,128]{1,0:T(8,128)(2,1)S(1)} collective-permute-done((bf16[256,128]{1,0:T(8,128)(2,1)S(1)}, bf16[256,128]{1,0:T(8,128)(2,1)S(1)}, u32[]{:S(2)}, u32[]{:S(2)}) %collective-permute-start.13) | collective-permute-done | bytes 65568 | tf_op jit(solution)/shard_map/ppermute | solution.py:20
  46.6 1.9 %collective-permute-done.16.other = bf16[2048,128]{1,0:T(8,128)(2,1)S(1)} collective-permute-done((bf16[2048,128]{1,0:T(8,128)(2,1)S(1)}, bf16[2048,128]{1,0:T(8,128)(2,1)S(1)}, u32[]{:S(2)}, u32[]{:S(2)}) %collective-permute-start.16) | collective-permute-done | bytes 524320 | tf_op jit(solution)/shard_map/ppermute | solution.py:20
  48.5 1.4 %shard_map.70 = (bf16[2,4,128,128]{3,2,1,0:T(8,128)(2,1)S(1)}, bf16[2,4,128,128]{3,2,1,0:T(8,128)(2,1)S(1)}, bf16[2,4,128,128]{3,2,1,0:T(8,128)(2,1)S(1)}, bf16[2,4,128,128]{3,2,1,0:T(8,128)(2,1)S(1)}) custom-call(bf16[32,128,128]{2,1,0:T(8,128)(2,1)S(1)} %bitcast.10, s32[2,32]{1,0:T(2,128)S(1)} %bitcast.13, s32[1]{0:T(128)} %bitcast.8.counts, ...), custom_call_target="tpu_custom_call" | custom-call | tf_op jit(solution)/shard_map/pallas_call | solution.py:38
  49.8 1.6 %collective-permute-start.17 = (bf16[2,4,128,128]{3,2,1,0:T(8,128)(2,1)S(1)}, bf16[2,4,128,128]{3,2,1,0:T(8,128)(2,1)S(1)}, u32[]{:S(2)}, u32[]{:S(2)}) collective-permute-start(bf16[2,4,128,128]{3,2,1,0:T(8,128)(2,1)S(1)} %get-tuple-element.50), channel_id=1, source_target_pairs={{0,2},{1,5},{2,0},{3,7},{4,6},{5,1},{6,4},{7,3},{8,10},{9,13},{10,... | collective-permute-start | bytes 786440 | tf_op jit(solution)/shard_map/ppermute | solution.py:34
  51.4 0.6 collective-permute-start.19
  52.0 6.6 %collective-permute-done.17.came = bf16[2,4,128,128]{3,2,1,0:T(8,128)(2,1)S(1)} collective-permute-done((bf16[2,4,128,128]{3,2,1,0:T(8,128)(2,1)S(1)}, bf16[2,4,128,128]{3,2,1,0:T(8,128)(2,1)S(1)}, u32[]{:S(2)}, u32[]{:S(2)}) %collective-permute-start.17) | collective-permute-done | bytes 262176 | tf_op jit(solution)/shard_map/ppermute | solution.py:34
  58.7 0.9 %collective-permute-start.18 = (bf16[4,128,128]{2,1,0:T(8,128)(2,1)S(1)}, bf16[4,128,128]{2,1,0:T(8,128)(2,1)S(1)}, u32[]{:S(2)}, u32[]{:S(2)}) collective-permute-start(bf16[4,128,128]{2,1,0:T(8,128)(2,1)S(1)} %get-tuple-element.52), channel_id=1, source_target_pairs={{0,4},{1,3},{2,6},{3,1},{4,0},{5,7},{6,2},{7,5},{8,12},{9,11},{10,... | collective-permute-start | bytes 393224 | tf_op jit(solution)/shard_map/ppermute | solution.py:34
  59.6 1.6 %collective-permute-start.20 = (bf16[4,128,128]{2,1,0:T(8,128)(2,1)S(1)}, bf16[4,128,128]{2,1,0:T(8,128)(2,1)S(1)}, u32[]{:S(2)}, u32[]{:S(2)}) collective-permute-start(bf16[4,128,128]{2,1,0:T(8,128)(2,1)S(1)} %get-tuple-element.56), channel_id=1, source_target_pairs={{0,2},{1,5},{2,0},{3,7},{4,6},{5,1},{6,4},{7,3},{8,10},{9,13},{10,... | collective-permute-start | bytes 393224 | tf_op jit(solution)/shard_map/ppermute | solution.py:34
  61.2 2.7 %collective-permute-done.18.refs_1_ = bf16[4,128,128]{2,1,0:T(8,128)(2,1)S(1)} collective-permute-done((bf16[4,128,128]{2,1,0:T(8,128)(2,1)S(1)}, bf16[4,128,128]{2,1,0:T(8,128)(2,1)S(1)}, u32[]{:S(2)}, u32[]{:S(2)}) %collective-permute-start.18) | collective-permute-done | bytes 131104 | tf_op jit(solution)/shard_map/ppermute | solution.py:34
  63.9 0.7 collective-permute-done.20.refs_3_
  64.7 0.5 collective-permute-start.21
  65.2 1.9 %collective-permute-start.22 = (bf16[2,128,128]{2,1,0:T(8,128)(2,1)S(1)}, bf16[2,128,128]{2,1,0:T(8,128)(2,1)S(1)}, u32[]{:S(2)}, u32[]{:S(2)}) collective-permute-start(bf16[2,128,128]{2,1,0:T(8,128)(2,1)S(1)} %get-tuple-element.59), channel_id=1, source_target_pairs={{0,16},{4,20},{8,24},{12,28},{16,0},{20,4},{24,8},{28,12},{1,17},{... | collective-permute-start | bytes 196616 | tf_op jit(solution)/shard_map/ppermute | solution.py:20
  67.0 2.1 %collective-permute-start.23 = (bf16[2,128,128]{2,1,0:T(8,128)(2,1)S(1)}, bf16[2,128,128]{2,1,0:T(8,128)(2,1)S(1)}, u32[]{:S(2)}, u32[]{:S(2)}) collective-permute-start(bf16[2,128,128]{2,1,0:T(8,128)(2,1)S(1)} %get-tuple-element.60), channel_id=1, source_target_pairs={{0,24},{4,28},{8,16},{12,20},{16,8},{20,12},{24,0},{28,4},{1,25},{... | collective-permute-start | bytes 196616 | tf_op jit(solution)/shard_map/ppermute | solution.py:20
  69.1 2.6 %collective-permute-done.22.refs_1_ = bf16[2,128,128]{2,1,0:T(8,128)(2,1)S(1)} collective-permute-done((bf16[2,128,128]{2,1,0:T(8,128)(2,1)S(1)}, bf16[2,128,128]{2,1,0:T(8,128)(2,1)S(1)}, u32[]{:S(2)}, u32[]{:S(2)}) %collective-permute-start.22) | collective-permute-done | bytes 65568 | tf_op jit(solution)/shard_map/ppermute | solution.py:20
  71.8 1.5 %collective-permute-done.23.refs_2_ = bf16[2,128,128]{2,1,0:T(8,128)(2,1)S(1)} collective-permute-done((bf16[2,128,128]{2,1,0:T(8,128)(2,1)S(1)}, bf16[2,128,128]{2,1,0:T(8,128)(2,1)S(1)}, u32[]{:S(2)}, u32[]{:S(2)}) %collective-permute-start.23) | collective-permute-done | bytes 65568 | tf_op jit(solution)/shard_map/ppermute | solution.py:20
  73.4 2.2 %collective-permute-start.26 = (bf16[256,128]{1,0:T(8,128)(2,1)S(1)}, bf16[256,128]{1,0:T(8,128)(2,1)S(1)}, u32[]{:S(2)}, u32[]{:S(2)}) collective-permute-start(bf16[256,128]{1,0:T(8,128)(2,1)S(1)} %shard_map.74.refs_0_), channel_id=1, source_target_pairs={{0,24},{4,28},{8,16},{12,20},{16,8},{20,12},{24,0},{28,4},{1,25},{... | collective-permute-start | bytes 196616 | tf_op jit(solution)/shard_map/ppermute | solution.py:20
  75.9 2.7 %collective-permute-start.28 = (bf16[256,128]{1,0:T(8,128)(2,1)S(1)}, bf16[256,128]{1,0:T(8,128)(2,1)S(1)}, u32[]{:S(2)}, u32[]{:S(2)}) collective-permute-start(bf16[256,128]{1,0:T(8,128)(2,1)S(1)} %shard_map.74.refs_0_), channel_id=1, source_target_pairs={{0,12},{4,8},{8,4},{12,0},{16,28},{20,24},{24,20},{28,16},{1,13},{... | collective-permute-start | bytes 196616 | tf_op jit(solution)/shard_map/ppermute | solution.py:20
  78.6 0.7 collective-permute-start.27
  79.5 1.3 %collective-permute-start.30 = (bf16[256,128]{1,0:T(8,128)(2,1)S(1)}, bf16[256,128]{1,0:T(8,128)(2,1)S(1)}, u32[]{:S(2)}, u32[]{:S(2)}) collective-permute-start(bf16[256,128]{1,0:T(8,128)(2,1)S(1)} %collective-permute-done.26.refs_3_), channel_id=1, source_target_pairs={{0,4},{4,0},{8,12},{12,8},{16,20},{20,16},{24,28},{28,24},{1,5},{5... | collective-permute-start | bytes 196616 | tf_op jit(solution)/shard_map/ppermute | solution.py:20
  81.0 1.3 %collective-permute-start.29 = (bf16[256,128]{1,0:T(8,128)(2,1)S(1)}, bf16[256,128]{1,0:T(8,128)(2,1)S(1)}, u32[]{:S(2)}, u32[]{:S(2)}) collective-permute-start(bf16[256,128]{1,0:T(8,128)(2,1)S(1)} %collective-permute-done.25.refs_2_), channel_id=1, source_target_pairs={{0,4},{4,0},{8,12},{12,8},{16,20},{20,16},{24,28},{28,24},{1,5},{5... | collective-permute-start | bytes 196616 | tf_op jit(solution)/shard_map/ppermute | solution.py:20
  82.3 0.5 collective-permute-done.27.refs_4_
  82.9 0.7 collective-permute-done.24.refs_1_
  83.8 1.5 %collective-permute-done.29.refs_6_ = bf16[256,128]{1,0:T(8,128)(2,1)S(1)} collective-permute-done((bf16[256,128]{1,0:T(8,128)(2,1)S(1)}, bf16[256,128]{1,0:T(8,128)(2,1)S(1)}, u32[]{:S(2)}, u32[]{:S(2)}) %collective-permute-start.29) | collective-permute-done | bytes 65568 | tf_op jit(solution)/shard_map/ppermute | solution.py:20
  85.3 1.0 %shard_map.75 = bf16[2,1,2048,128]{3,2,1,0:T(8,128)(2,1)} custom-call(bf16[1,2048,128]{2,1,0:T(8,128)(2,1)S(1)} %bitcast.11, bf16[256,128]{1,0:T(8,128)(2,1)S(1)} %shard_map.74.refs_0_, bf16[256,128]{1,0:T(8,128)(2,1)S(1)} %collective-permute-done.24.refs_1_, bf16[256,128]{1,0:T(8,128)(2,1)S(1)} %collective-permute-done.25.refs_2_, ...), custom_call_target="tpu_custom_call" | custom-call | tf_op jit(solution)/shard_map/pallas_call | solution.py:38
  (34 shorter events, 2.8 us)
Async XLA Ops:
  0.7 0.7 copy-start.3
  3.6 19.6 %collective-permute-start.4 = (bf16[2048,128]{1,0:T(8,128)(2,1)S(1)}, bf16[2048,128]{1,0:T(8,128)(2,1)S(1)}, u32[]{:S(2)}, u32[]{:S(2)}) collective-permute-start(bf16[2048,128]{1,0:T(8,128)(2,1)S(1)} %get-tuple-element.41.refs_4_), channel_id=1, source_target_pairs={{4,12},{12,20},{20,28},{5,13},{13,21},{21,29},{6,14},{14,22},{22,3... | collective-permute-start | bytes 1572872 | tf_op jit(solution)/shard_map/ppermute | solution.py:288
  4.3 7.4 %collective-permute-start = (bf16[2,4,128,128]{3,2,1,0:T(8,128)(2,1)S(1)}, bf16[2,4,128,128]{3,2,1,0:T(8,128)(2,1)S(1)}, u32[]{:S(2)}, u32[]{:S(2)}) collective-permute-start(bf16[2,4,128,128]{3,2,1,0:T(8,128)(2,1)S(1)} %get-tuple-element.34), channel_id=1, source_target_pairs={{0,2},{1,5},{2,0},{3,7},{4,6},{5,1},{6,4},{7,3},{8,10},{9,13},{10,... | collective-permute-start | bytes 786440 | tf_op jit(solution)/shard_map/ppermute | solution.py:34
  7.3 10.8 %collective-permute-start.2 = (bf16[2,4,128,128]{3,2,1,0:T(8,128)(2,1)S(1)}, bf16[2,4,128,128]{3,2,1,0:T(8,128)(2,1)S(1)}, u32[]{:S(2)}, u32[]{:S(2)}) collective-permute-start(bf16[2,4,128,128]{3,2,1,0:T(8,128)(2,1)S(1)} %get-tuple-element.38), channel_id=1, source_target_pairs={{0,4},{1,3},{2,6},{3,1},{4,0},{5,7},{6,2},{7,5},{8,12},{9,11},{10,... | collective-permute-start | bytes 786440 | tf_op jit(solution)/shard_map/ppermute | solution.py:34
  11.7 9.7 %collective-permute-start.1 = (bf16[4,128,128]{2,1,0:T(8,128)(2,1)S(1)}, bf16[4,128,128]{2,1,0:T(8,128)(2,1)S(1)}, u32[]{:S(2)}, u32[]{:S(2)}) collective-permute-start(bf16[4,128,128]{2,1,0:T(8,128)(2,1)S(1)} %get-tuple-element.36), channel_id=1, source_target_pairs={{0,4},{1,3},{2,6},{3,1},{4,0},{5,7},{6,2},{7,5},{8,12},{9,11},{10,... | collective-permute-start | bytes 393224 | tf_op jit(solution)/shard_map/ppermute | solution.py:34
  18.1 14.5 %copy-start.1 = (bf16[2,1,2048,128]{3,2,1,0:T(8,128)(2,1)S(1)}, bf16[2,1,2048,128]{3,2,1,0:T(8,128)(2,1)}, u32[]{:S(2)}) copy-start(bf16[2,1,2048,128]{3,2,1,0:T(8,128)(2,1)} %refs_3_.3) | copy-start | bytes 3145732
  18.1 5.0 %collective-permute-start.3 = (bf16[4,128,128]{2,1,0:T(8,128)(2,1)S(1)}, bf16[4,128,128]{2,1,0:T(8,128)(2,1)S(1)}, u32[]{:S(2)}, u32[]{:S(2)}) collective-permute-start(bf16[4,128,128]{2,1,0:T(8,128)(2,1)S(1)} %get-tuple-element.40), channel_id=1, source_target_pairs={{0,2},{1,5},{2,0},{3,7},{4,6},{5,1},{6,4},{7,3},{8,10},{9,13},{10,... | collective-permute-start | bytes 393224 | tf_op jit(solution)/shard_map/ppermute | solution.py:34
  23.2 9.4 %copy-start.2 = (bf16[1,16,128,128]{3,2,1,0:T(8,128)(2,1)S(1)}, bf16[1,16,128,128]{3,2,1,0:T(8,128)(2,1)}, u32[]{:S(2)}) copy-start(bf16[1,16,128,128]{3,2,1,0:T(8,128)(2,1)} %refs_4_.3) | copy-start | bytes 1572868
  23.3 23.1 %collective-permute-start.15 = (bf16[2048,128]{1,0:T(8,128)(2,1)S(1)}, bf16[2048,128]{1,0:T(8,128)(2,1)S(1)}, u32[]{:S(2)}, u32[]{:S(2)}) collective-permute-start(bf16[2048,128]{1,0:T(8,128)(2,1)S(1)} %get-tuple-element.46), channel_id=1, source_target_pairs={{0,4},{4,0},{8,12},{12,8},{16,20},{20,16},{24,28},{28,24},{1,5},{5... | collective-permute-start | bytes 1572872 | tf_op jit(solution)/shard_map/ppermute | solution.py:20
  23.4 4.4 %collective-permute-start.5 = (bf16[2,128,128]{2,1,0:T(8,128)(2,1)S(1)}, bf16[2,128,128]{2,1,0:T(8,128)(2,1)S(1)}, u32[]{:S(2)}, u32[]{:S(2)}) collective-permute-start(bf16[2,128,128]{2,1,0:T(8,128)(2,1)S(1)} %get-tuple-element.43), channel_id=1, source_target_pairs={{0,8},{4,12},{8,0},{12,4},{16,24},{20,28},{24,16},{28,20},{1,9},{5... | collective-permute-start | bytes 196616 | tf_op jit(solution)/shard_map/ppermute | solution.py:20
  25.0 6.3 %collective-permute-start.6 = (bf16[2,128,128]{2,1,0:T(8,128)(2,1)S(1)}, bf16[2,128,128]{2,1,0:T(8,128)(2,1)S(1)}, u32[]{:S(2)}, u32[]{:S(2)}) collective-permute-start(bf16[2,128,128]{2,1,0:T(8,128)(2,1)S(1)} %get-tuple-element.44), channel_id=1, source_target_pairs={{0,16},{4,20},{8,24},{12,28},{16,0},{20,4},{24,8},{28,12},{1,17},{... | collective-permute-start | bytes 196616 | tf_op jit(solution)/shard_map/ppermute | solution.py:20
  26.4 6.2 %collective-permute-start.7 = (bf16[2,128,128]{2,1,0:T(8,128)(2,1)S(1)}, bf16[2,128,128]{2,1,0:T(8,128)(2,1)S(1)}, u32[]{:S(2)}, u32[]{:S(2)}) collective-permute-start(bf16[2,128,128]{2,1,0:T(8,128)(2,1)S(1)} %get-tuple-element.45), channel_id=1, source_target_pairs={{0,24},{4,28},{8,16},{12,20},{16,8},{20,12},{24,0},{28,4},{1,25},{... | collective-permute-start | bytes 196616 | tf_op jit(solution)/shard_map/ppermute | solution.py:20
  32.6 15.9 %copy-start = (bf16[1,1,1,32,128,128]{5,4,3,2,1,0:T(8,128)(2,1)S(1)}, bf16[1,1,1,32,128,128]{5,4,3,2,1,0:T(8,128)(2,1)}, u32[]{:S(2)}) copy-start(bf16[1,1,1,32,128,128]{5,4,3,2,1,0:T(8,128)(2,1)} %param.6) | copy-start | bytes 3145732
  32.8 6.2 %collective-permute-start.12 = (bf16[256,128]{1,0:T(8,128)(2,1)S(1)}, bf16[256,128]{1,0:T(8,128)(2,1)S(1)}, u32[]{:S(2)}, u32[]{:S(2)}) collective-permute-start(bf16[256,128]{1,0:T(8,128)(2,1)S(1)} %shard_map.68.refs_0_), channel_id=1, source_target_pairs={{0,12},{4,8},{8,4},{12,0},{16,28},{20,24},{24,20},{28,16},{1,13},{... | collective-permute-start | bytes 196616 | tf_op jit(solution)/shard_map/ppermute | solution.py:20
  34.6 6.1 %collective-permute-start.10 = (bf16[256,128]{1,0:T(8,128)(2,1)S(1)}, bf16[256,128]{1,0:T(8,128)(2,1)S(1)}, u32[]{:S(2)}, u32[]{:S(2)}) collective-permute-start(bf16[256,128]{1,0:T(8,128)(2,1)S(1)} %shard_map.68.refs_0_), channel_id=1, source_target_pairs={{0,24},{4,28},{8,16},{12,20},{16,8},{20,12},{24,0},{28,4},{1,25},{... | collective-permute-start | bytes 196616 | tf_op jit(solution)/shard_map/ppermute | solution.py:20
  36.2 5.9 %collective-permute-start.9 = (bf16[256,128]{1,0:T(8,128)(2,1)S(1)}, bf16[256,128]{1,0:T(8,128)(2,1)S(1)}, u32[]{:S(2)}, u32[]{:S(2)}) collective-permute-start(bf16[256,128]{1,0:T(8,128)(2,1)S(1)} %shard_map.68.refs_0_), channel_id=1, source_target_pairs={{0,16},{4,20},{8,24},{12,28},{16,0},{20,4},{24,8},{28,12},{1,17},{... | collective-permute-start | bytes 196616 | tf_op jit(solution)/shard_map/ppermute | solution.py:20
  37.3 5.4 %collective-permute-start.11 = (bf16[256,128]{1,0:T(8,128)(2,1)S(1)}, bf16[256,128]{1,0:T(8,128)(2,1)S(1)}, u32[]{:S(2)}, u32[]{:S(2)}) collective-permute-start(bf16[256,128]{1,0:T(8,128)(2,1)S(1)} %shard_map.68.refs_0_), channel_id=1, source_target_pairs={{0,4},{4,0},{8,12},{12,8},{16,20},{20,16},{24,28},{28,24},{1,5},{5... | collective-permute-start | bytes 196616 | tf_op jit(solution)/shard_map/ppermute | solution.py:20
  39.0 4.3 %collective-permute-start.8 = (bf16[256,128]{1,0:T(8,128)(2,1)S(1)}, bf16[256,128]{1,0:T(8,128)(2,1)S(1)}, u32[]{:S(2)}, u32[]{:S(2)}) collective-permute-start(bf16[256,128]{1,0:T(8,128)(2,1)S(1)} %shard_map.68.refs_0_), channel_id=1, source_target_pairs={{0,8},{4,12},{8,0},{12,4},{16,24},{20,28},{24,16},{28,20},{1,9},{5... | collective-permute-start | bytes 196616 | tf_op jit(solution)/shard_map/ppermute | solution.py:20
  40.7 4.3 %collective-permute-start.14 = (bf16[256,128]{1,0:T(8,128)(2,1)S(1)}, bf16[256,128]{1,0:T(8,128)(2,1)S(1)}, u32[]{:S(2)}, u32[]{:S(2)}) collective-permute-start(bf16[256,128]{1,0:T(8,128)(2,1)S(1)} %collective-permute-done.10.refs_3_), channel_id=1, source_target_pairs={{0,4},{4,0},{8,12},{12,8},{16,20},{20,16},{24,28},{28,24},{1,5},{5... | collective-permute-start | bytes 196616 | tf_op jit(solution)/shard_map/ppermute | solution.py:20
  42.1 4.3 %collective-permute-start.13 = (bf16[256,128]{1,0:T(8,128)(2,1)S(1)}, bf16[256,128]{1,0:T(8,128)(2,1)S(1)}, u32[]{:S(2)}, u32[]{:S(2)}) collective-permute-start(bf16[256,128]{1,0:T(8,128)(2,1)S(1)} %collective-permute-done.9.refs_2_), channel_id=1, source_target_pairs={{0,4},{4,0},{8,12},{12,8},{16,20},{20,16},{24,28},{28,24},{1,5},{5... | collective-permute-start | bytes 196616 | tf_op jit(solution)/shard_map/ppermute | solution.py:20
  46.5 2.0 %collective-permute-start.16 = (bf16[2048,128]{1,0:T(8,128)(2,1)S(1)}, bf16[2048,128]{1,0:T(8,128)(2,1)S(1)}, u32[]{:S(2)}, u32[]{:S(2)}) collective-permute-start(bf16[2048,128]{1,0:T(8,128)(2,1)S(1)} %get-tuple-element.48.own), channel_id=1, source_target_pairs={{0,1},{1,0},{2,3},{3,2},{4,5},{5,4},{6,7},{7,6},{8,9},{9,8},{10,11... | collective-permute-start | bytes 1572872 | tf_op jit(solution)/shard_map/ppermute | solution.py:20
  49.8 8.8 %collective-permute-start.17 = (bf16[2,4,128,128]{3,2,1,0:T(8,128)(2,1)S(1)}, bf16[2,4,128,128]{3,2,1,0:T(8,128)(2,1)S(1)}, u32[]{:S(2)}, u32[]{:S(2)}) collective-permute-start(bf16[2,4,128,128]{3,2,1,0:T(8,128)(2,1)S(1)} %get-tuple-element.50), channel_id=1, source_target_pairs={{0,2},{1,5},{2,0},{3,7},{4,6},{5,1},{6,4},{7,3},{8,10},{9,13},{10,... | collective-permute-start | bytes 786440 | tf_op jit(solution)/shard_map/ppermute | solution.py:34
  51.4 8.1 %collective-permute-start.19 = (bf16[2,4,128,128]{3,2,1,0:T(8,128)(2,1)S(1)}, bf16[2,4,128,128]{3,2,1,0:T(8,128)(2,1)S(1)}, u32[]{:S(2)}, u32[]{:S(2)}) collective-permute-start(bf16[2,4,128,128]{3,2,1,0:T(8,128)(2,1)S(1)} %get-tuple-element.54), channel_id=1, source_target_pairs={{0,4},{1,3},{2,6},{3,1},{4,0},{5,7},{6,2},{7,5},{8,12},{9,11},{10,... | collective-permute-start | bytes 786440 | tf_op jit(solution)/shard_map/ppermute | solution.py:34
  58.7 5.2 %collective-permute-start.18 = (bf16[4,128,128]{2,1,0:T(8,128)(2,1)S(1)}, bf16[4,128,128]{2,1,0:T(8,128)(2,1)S(1)}, u32[]{:S(2)}, u32[]{:S(2)}) collective-permute-start(bf16[4,128,128]{2,1,0:T(8,128)(2,1)S(1)} %get-tuple-element.52), channel_id=1, source_target_pairs={{0,4},{1,3},{2,6},{3,1},{4,0},{5,7},{6,2},{7,5},{8,12},{9,11},{10,... | collective-permute-start | bytes 393224 | tf_op jit(solution)/shard_map/ppermute | solution.py:34
  59.6 5.0 %collective-permute-start.20 = (bf16[4,128,128]{2,1,0:T(8,128)(2,1)S(1)}, bf16[4,128,128]{2,1,0:T(8,128)(2,1)S(1)}, u32[]{:S(2)}, u32[]{:S(2)}) collective-permute-start(bf16[4,128,128]{2,1,0:T(8,128)(2,1)S(1)} %get-tuple-element.56), channel_id=1, source_target_pairs={{0,2},{1,5},{2,0},{3,7},{4,6},{5,1},{6,4},{7,3},{8,10},{9,13},{10,... | collective-permute-start | bytes 393224 | tf_op jit(solution)/shard_map/ppermute | solution.py:34
  64.7 4.5 %collective-permute-start.21 = (bf16[2,128,128]{2,1,0:T(8,128)(2,1)S(1)}, bf16[2,128,128]{2,1,0:T(8,128)(2,1)S(1)}, u32[]{:S(2)}, u32[]{:S(2)}) collective-permute-start(bf16[2,128,128]{2,1,0:T(8,128)(2,1)S(1)} %get-tuple-element.58), channel_id=1, source_target_pairs={{0,8},{4,12},{8,0},{12,4},{16,24},{20,28},{24,16},{28,20},{1,9},{5... | collective-permute-start | bytes 196616 | tf_op jit(solution)/shard_map/ppermute | solution.py:20
  65.2 6.6 %collective-permute-start.22 = (bf16[2,128,128]{2,1,0:T(8,128)(2,1)S(1)}, bf16[2,128,128]{2,1,0:T(8,128)(2,1)S(1)}, u32[]{:S(2)}, u32[]{:S(2)}) collective-permute-start(bf16[2,128,128]{2,1,0:T(8,128)(2,1)S(1)} %get-tuple-element.59), channel_id=1, source_target_pairs={{0,16},{4,20},{8,24},{12,28},{16,0},{20,4},{24,8},{28,12},{1,17},{... | collective-permute-start | bytes 196616 | tf_op jit(solution)/shard_map/ppermute | solution.py:20
  67.0 6.2 %collective-permute-start.23 = (bf16[2,128,128]{2,1,0:T(8,128)(2,1)S(1)}, bf16[2,128,128]{2,1,0:T(8,128)(2,1)S(1)}, u32[]{:S(2)}, u32[]{:S(2)}) collective-permute-start(bf16[2,128,128]{2,1,0:T(8,128)(2,1)S(1)} %get-tuple-element.60), channel_id=1, source_target_pairs={{0,24},{4,28},{8,16},{12,20},{16,8},{20,12},{24,0},{28,4},{1,25},{... | collective-permute-start | bytes 196616 | tf_op jit(solution)/shard_map/ppermute | solution.py:20
  73.4 6.1 %collective-permute-start.26 = (bf16[256,128]{1,0:T(8,128)(2,1)S(1)}, bf16[256,128]{1,0:T(8,128)(2,1)S(1)}, u32[]{:S(2)}, u32[]{:S(2)}) collective-permute-start(bf16[256,128]{1,0:T(8,128)(2,1)S(1)} %shard_map.74.refs_0_), channel_id=1, source_target_pairs={{0,24},{4,28},{8,16},{12,20},{16,8},{20,12},{24,0},{28,4},{1,25},{... | collective-permute-start | bytes 196616 | tf_op jit(solution)/shard_map/ppermute | solution.py:20
  75.6 5.5 %collective-permute-start.25 = (bf16[256,128]{1,0:T(8,128)(2,1)S(1)}, bf16[256,128]{1,0:T(8,128)(2,1)S(1)}, u32[]{:S(2)}, u32[]{:S(2)}) collective-permute-start(bf16[256,128]{1,0:T(8,128)(2,1)S(1)} %shard_map.74.refs_0_), channel_id=1, source_target_pairs={{0,16},{4,20},{8,24},{12,28},{16,0},{20,4},{24,8},{28,12},{1,17},{... | collective-permute-start | bytes 196616 | tf_op jit(solution)/shard_map/ppermute | solution.py:20
  75.9 6.4 %collective-permute-start.28 = (bf16[256,128]{1,0:T(8,128)(2,1)S(1)}, bf16[256,128]{1,0:T(8,128)(2,1)S(1)}, u32[]{:S(2)}, u32[]{:S(2)}) collective-permute-start(bf16[256,128]{1,0:T(8,128)(2,1)S(1)} %shard_map.74.refs_0_), channel_id=1, source_target_pairs={{0,12},{4,8},{8,4},{12,0},{16,28},{20,24},{24,20},{28,16},{1,13},{... | collective-permute-start | bytes 196616 | tf_op jit(solution)/shard_map/ppermute | solution.py:20
  78.6 4.3 %collective-permute-start.27 = (bf16[256,128]{1,0:T(8,128)(2,1)S(1)}, bf16[256,128]{1,0:T(8,128)(2,1)S(1)}, u32[]{:S(2)}, u32[]{:S(2)}) collective-permute-start(bf16[256,128]{1,0:T(8,128)(2,1)S(1)} %shard_map.74.refs_0_), channel_id=1, source_target_pairs={{0,4},{4,0},{8,12},{12,8},{16,20},{20,16},{24,28},{28,24},{1,5},{5... | collective-permute-start | bytes 196616 | tf_op jit(solution)/shard_map/ppermute | solution.py:20
  79.3 4.3 %collective-permute-start.24 = (bf16[256,128]{1,0:T(8,128)(2,1)S(1)}, bf16[256,128]{1,0:T(8,128)(2,1)S(1)}, u32[]{:S(2)}, u32[]{:S(2)}) collective-permute-start(bf16[256,128]{1,0:T(8,128)(2,1)S(1)} %shard_map.74.refs_0_), channel_id=1, source_target_pairs={{0,8},{4,12},{8,0},{12,4},{16,24},{20,28},{24,16},{28,20},{1,9},{5... | collective-permute-start | bytes 196616 | tf_op jit(solution)/shard_map/ppermute | solution.py:20
  79.5 4.3 %collective-permute-start.30 = (bf16[256,128]{1,0:T(8,128)(2,1)S(1)}, bf16[256,128]{1,0:T(8,128)(2,1)S(1)}, u32[]{:S(2)}, u32[]{:S(2)}) collective-permute-start(bf16[256,128]{1,0:T(8,128)(2,1)S(1)} %collective-permute-done.26.refs_3_), channel_id=1, source_target_pairs={{0,4},{4,0},{8,12},{12,8},{16,20},{20,16},{24,28},{28,24},{1,5},{5... | collective-permute-start | bytes 196616 | tf_op jit(solution)/shard_map/ppermute | solution.py:20
  81.0 4.3 %collective-permute-start.29 = (bf16[256,128]{1,0:T(8,128)(2,1)S(1)}, bf16[256,128]{1,0:T(8,128)(2,1)S(1)}, u32[]{:S(2)}, u32[]{:S(2)}) collective-permute-start(bf16[256,128]{1,0:T(8,128)(2,1)S(1)} %collective-permute-done.25.refs_2_), channel_id=1, source_target_pairs={{0,4},{4,0},{8,12},{12,8},{16,20},{20,16},{24,28},{28,24},{1,5},{5... | collective-permute-start | bytes 196616 | tf_op jit(solution)/shard_map/ppermute | solution.py:20

commit v6 on v5

--- a/solution.py
+++ b/solution.py
@@ -104,16 +104,13 @@
         return source[pl.ds(start, p.piece)].astype(BF16)
 
     for piece in range(2):
-        send, keep = outs[2 * piece], outs[2 * piece + 1]
+        far, near, keep, stay = outs[4 * piece : 4 * piece + 4]
         by_src = over_src(piece)
-        for j in range(2):
-            for g in range(p.groups):
-                send[j, g] = rows(
-                    jnp.where(by_src, y ^ 1, j), jnp.where(by_src, j, x ^ 1), g, piece
-                )
-                keep[j, g] = rows(
-                    jnp.where(by_src, y, j), jnp.where(by_src, j, x), g, piece
-                )
+        for g in range(p.groups):
+            far[g] = rows(y ^ 1, x ^ 1, g, piece)
+            near[g] = rows(jnp.where(by_src, y ^ 1, y), jnp.where(by_src, x, x ^ 1), g, piece)
+            keep[g] = rows(jnp.where(by_src, y, y ^ 1), jnp.where(by_src, x ^ 1, x), g, piece)
+            stay[g] = rows(y, x, g, piece)
 
 
 def split_kernel(p, source, *outs):
@@ -185,14 +182,12 @@
     return value.astype(BF16)
 
 
-def second_kernel(p, piece, keep, came, send, stay):
-    own = jnp.where(over_src(piece), p.x(), lax.axis_index("src") & 1)
-    send[...] = total(keep[own ^ 1], came[own ^ 1])
-    stay[...] = total(keep[own], came[own])
+def second_kernel(p, keep, came, send):
+    send[...] = total(keep[...], came[...])
 
 
 def third_kernel(p, *refs):
-    ins, outs = refs[:4], refs[4:]
+    ins, outs = refs[:6], refs[6:]
     if len(outs) > p.groups:
         mine, behind, *outs, onward = outs
 
@@ -208,8 +203,7 @@
     for k, ref in enumerate(outs):
         g = here ^ k
         for piece in range(2):
-            stay, came = ins[2 * piece : 2 * piece + 2]
-            ref[piece] = total(stay[g], came[g])
+            ref[piece] = total(*(term[g] for term in ins[3 * piece : 3 * piece + 3]))
 
 
 def current_kernel(p, step, keep, *refs):
@@ -278,7 +272,7 @@
         rest = total(keep, exchange(send, "src", by))
         by //= 2
     return call(
-        functools.partial(split_kernel, p), [p.shape(2, p.groups)] * 4, [VMEM], [], rest
+        functools.partial(split_kernel, p), [p.shape(p.groups)] * 8, [VMEM], [], rest
     )
 
 
@@ -289,24 +283,24 @@
             lagged, "delay", [(i, i + 2) for i in range(1, p.bins - 2, 2)]
         )
         moved = [lagged, behind]
-    send0, keep0, send1, keep1 = narrow(p, firsts)
-    one = p.shape(p.groups)
-    came0, came1 = hop(send0, 0, 0), hop(send1, 1, 0)
-    send0, stay0 = call(
-        functools.partial(second_kernel, p, 0), [one] * 2, [VMEM] * 2, [], keep0, came0
-    )
-    send1, stay1 = call(
-        functools.partial(second_kernel, p, 1), [one] * 2, [VMEM] * 2, [], keep1, came1
-    )
+    far0, near0, keep0, stay0, far1, near1, keep1, stay1 = narrow(p, firsts)
+    far0, far1 = hop(far0, 0, 0), hop(far1, 1, 0)
+    near0, near1 = hop(near0, 0, 0), hop(near1, 1, 0)
+    one = [p.shape(p.groups)]
+    second = functools.partial(second_kernel, p)
+    (send0,) = call(second, one, [VMEM] * 2, [], keep0, far0)
+    (send1,) = call(second, one, [VMEM] * 2, [], keep1, far1)
     terms = call(
         functools.partial(third_kernel, p),
         [p.shape(2)] * p.groups
         + [jax.ShapeDtypeStruct(v.shape, BF16) for v in moved[:1]],
-        [VMEM] * (4 + len(moved)),
+        [VMEM] * (6 + len(moved)),
         [],
         stay0,
+        near0,
         hop(send0, 0, 1),
         stay1,
+        near1,
         hop(send1, 1, 1),
         *moved,
     )
@@ -355,7 +349,7 @@
     slot_blocks = blocks.reshape(blocks.shape[3:])
     places = coords.reshape(-1, 2).T
     used = counts.reshape(-1)
-    first_outs = [p.shape(2, p.groups)] * 4
+    first_outs = [p.shape(p.groups)] * 8
     if p.srcs > 2:
         first_outs = [jax.ShapeDtypeStruct((p.tile_rows, p.width), BF16)]
     half = jax.ShapeDtypeStruct((p.owned, p.width), BF16)

time: 86.5 us -> 84.1 us (0.972)
  waiting for transfers between devices: 34.8 us -> 31.5 us
  starting transfers between devices: 44.6 us -> 45.5 us
    ppermute x8 -> x12, waiting for transfers between devices: 13.5 us -> 9.12 us  [hop(): return lax.ppermute(array, ('delay', 'src', 'tgt'), pairs)]
    ppermute x22, waiting for transfers between devices: 21.3 us -> 22.3 us  [exchange(): return lax.ppermute(array, axis, [(i, i ^ by) for i in range(peers)])]
    ppermute x8 -> x12, starting transfers between devices: 19.9 us -> 20.4 us  [hop(): return lax.ppermute(array, ('delay', 'src', 'tgt'), pairs)]
  transfers between devices with their start and end apart: 31 -> 35, of which waited for: 22 -> 23; matrix products, arithmetic and copies ran while one was open for 0% -> 0% of each run, Pallas kernels for 0% -> 0%
where the time goes in v6:
time: 84.1 us; the launch traced here: 83.9 us
  starting transfers between devices  45.5 us (54%)
  waiting for transfers between devices  31.5 us (37%)
  Pallas kernels  5.44 us (6%)
    ppermute x22, starting transfers between devices, exchange(): return lax.ppermute(array, axis, [(i, i ^ by) for i in range(peers)])  24.5 us
    ppermute x22, waiting for transfers between devices, exchange(): return lax.ppermute(array, axis, [(i, i ^ by) for i in range(peers)])  22.3 us
    ppermute x12, starting transfers between devices, hop(): return lax.ppermute(array, ('delay', 'src', 'tgt'), pairs)  20.4 us
    ppermute x12, waiting for transfers between devices, hop(): return lax.ppermute(array, ('delay', 'src', 'tgt'), pairs)  9.12 us
    pallas_call x12, Pallas kernels, call(): pl.pallas_call(kernel, out_shape=outs, in_specs=specs, out_specs=[VMEM] *...  5.44 us
  transfers between devices with their start and end apart: 35, of which 23 were waited for; matrix products, arithmetic and copies ran while one was open for 0% of the time, Pallas kernels for 0%

profile of v6, /device:TPU:0, one launch (start us, length us, event | category | flops | bytes accessed | tf_op | source)
XLA Modules:
  0.0 83.9 jit_solution(10814442033145286787)
XLA Ops:
  0.7 0.7 copy-done.3
  1.3 2.2 %shard_map.64 = (bf16[4,128,128]{2,1,0:T(8,128)(2,1)S(1)}, bf16[4,128,128]{2,1,0:T(8,128)(2,1)S(1)}, bf16[4,128,128]{2,1,0:T(8,128)(2,1)S(1)}, bf16[4,128,128]{2...) custom-call(bf16[32,128,128]{2,1,0:T(8,128)(2,1)} %bitcast.9, ...), custom_call_target="tpu_custom_call" | custom-call | tf_op jit(solution)/shard_map/pallas_call | solution.py:38
  3.6 0.7 collective-permute-start.6
  4.3 3.0 %collective-permute-start.1 = (bf16[4,128,128]{2,1,0:T(8,128)(2,1)S(1)}, bf16[4,128,128]{2,1,0:T(8,128)(2,1)S(1)}, u32[]{:S(2)}, u32[]{:S(2)}) collective-permute-start(bf16[4,128,128]{2,1,0:T(8,128)(2,1)S(1)} %get-tuple-element.36), channel_id=1, source_target_pairs={{0,2},{1,5},{2,0},{3,7},{4,6},{5,1},{6,4},{7,3},{8,10},{9,13},{10,... | collective-permute-start | bytes 393224 | tf_op jit(solution)/shard_map/ppermute | solution.py:34
  7.3 4.3 %collective-permute-start.4 = (bf16[4,128,128]{2,1,0:T(8,128)(2,1)S(1)}, bf16[4,128,128]{2,1,0:T(8,128)(2,1)S(1)}, u32[]{:S(2)}, u32[]{:S(2)}) collective-permute-start(bf16[4,128,128]{2,1,0:T(8,128)(2,1)S(1)} %get-tuple-element.40), channel_id=1, source_target_pairs={{0,4},{1,3},{2,6},{3,1},{4,0},{5,7},{6,2},{7,5},{8,12},{9,11},{10,... | collective-permute-start | bytes 393224 | tf_op jit(solution)/shard_map/ppermute | solution.py:34
  11.6 0.5 collective-permute-start
  12.2 3.3 %collective-permute-start.2 = (bf16[4,128,128]{2,1,0:T(8,128)(2,1)S(1)}, bf16[4,128,128]{2,1,0:T(8,128)(2,1)S(1)}, u32[]{:S(2)}, u32[]{:S(2)}) collective-permute-start(bf16[4,128,128]{2,1,0:T(8,128)(2,1)S(1)} %shard_map.65), channel_id=1, source_target_pairs={{0,4},{1,3},{2,6},{3,1},{4,0},{5,7},{6,2},{7,5},{8,12},{9,11},{10,... | collective-permute-start | bytes 393224 | tf_op jit(solution)/shard_map/ppermute | solution.py:34
  16.0 2.1 %collective-permute-start.5 = (bf16[4,128,128]{2,1,0:T(8,128)(2,1)S(1)}, bf16[4,128,128]{2,1,0:T(8,128)(2,1)S(1)}, u32[]{:S(2)}, u32[]{:S(2)}) collective-permute-start(bf16[4,128,128]{2,1,0:T(8,128)(2,1)S(1)} %shard_map.66), channel_id=1, source_target_pairs={{0,2},{1,5},{2,0},{3,7},{4,6},{5,1},{6,4},{7,3},{8,10},{9,13},{10,... | collective-permute-start | bytes 393224 | tf_op jit(solution)/shard_map/ppermute | solution.py:34
  18.5 1.7 %collective-permute-done.2.refs_2_ = bf16[4,128,128]{2,1,0:T(8,128)(2,1)S(1)} collective-permute-done((bf16[4,128,128]{2,1,0:T(8,128)(2,1)S(1)}, bf16[4,128,128]{2,1,0:T(8,128)(2,1)S(1)}, u32[]{:S(2)}, u32[]{:S(2)}) %collective-permute-start.2) | collective-permute-done | bytes 131104 | tf_op jit(solution)/shard_map/ppermute | solution.py:34
  20.2 0.8 collective-permute-done.5.refs_5_
  21.2 0.7 collective-permute-start.17
  21.9 2.0 %collective-permute-start.7 = (bf16[2,128,128]{2,1,0:T(8,128)(2,1)S(1)}, bf16[2,128,128]{2,1,0:T(8,128)(2,1)S(1)}, u32[]{:S(2)}, u32[]{:S(2)}) collective-permute-start(bf16[2,128,128]{2,1,0:T(8,128)(2,1)S(1)} %get-tuple-element.43), channel_id=1, source_target_pairs={{0,8},{4,12},{8,0},{12,4},{16,24},{20,28},{24,16},{28,20},{1,9},{5... | collective-permute-start | bytes 196616 | tf_op jit(solution)/shard_map/ppermute | solution.py:20
  23.9 2.6 %collective-permute-start.8 = (bf16[2,128,128]{2,1,0:T(8,128)(2,1)S(1)}, bf16[2,128,128]{2,1,0:T(8,128)(2,1)S(1)}, u32[]{:S(2)}, u32[]{:S(2)}) collective-permute-start(bf16[2,128,128]{2,1,0:T(8,128)(2,1)S(1)} %get-tuple-element.44), channel_id=1, source_target_pairs={{0,16},{4,20},{8,24},{12,28},{16,0},{20,4},{24,8},{28,12},{1,17},{... | collective-permute-start | bytes 196616 | tf_op jit(solution)/shard_map/ppermute | solution.py:20
  26.8 3.6 %collective-permute-done.8.refs_1_ = bf16[2,128,128]{2,1,0:T(8,128)(2,1)S(1)} collective-permute-done((bf16[2,128,128]{2,1,0:T(8,128)(2,1)S(1)}, bf16[2,128,128]{2,1,0:T(8,128)(2,1)S(1)}, u32[]{:S(2)}, u32[]{:S(2)}) %collective-permute-start.8) | collective-permute-done | bytes 65568 | tf_op jit(solution)/shard_map/ppermute | solution.py:20
  30.4 2.4 %collective-permute-done.9.refs_2_ = bf16[2,128,128]{2,1,0:T(8,128)(2,1)S(1)} collective-permute-done((bf16[2,128,128]{2,1,0:T(8,128)(2,1)S(1)}, bf16[2,128,128]{2,1,0:T(8,128)(2,1)S(1)}, u32[]{:S(2)}, u32[]{:S(2)}) %collective-permute-start.9) | collective-permute-done | bytes 65568 | tf_op jit(solution)/shard_map/ppermute | solution.py:20
  33.0 1.7 %collective-permute-start.12 = (bf16[256,128]{1,0:T(8,128)(2,1)S(1)}, bf16[256,128]{1,0:T(8,128)(2,1)S(1)}, u32[]{:S(2)}, u32[]{:S(2)}) collective-permute-start(bf16[256,128]{1,0:T(8,128)(2,1)S(1)} %shard_map.68.refs_0_), channel_id=1, source_target_pairs={{0,24},{4,28},{8,16},{12,20},{16,8},{20,12},{24,0},{28,4},{1,25},{... | collective-permute-start | bytes 196616 | tf_op jit(solution)/shard_map/ppermute | solution.py:20
  34.8 1.1 %collective-permute-start.11 = (bf16[256,128]{1,0:T(8,128)(2,1)S(1)}, bf16[256,128]{1,0:T(8,128)(2,1)S(1)}, u32[]{:S(2)}, u32[]{:S(2)}) collective-permute-start(bf16[256,128]{1,0:T(8,128)(2,1)S(1)} %shard_map.68.refs_0_), channel_id=1, source_target_pairs={{0,16},{4,20},{8,24},{12,28},{16,0},{20,4},{24,8},{28,12},{1,17},{... | collective-permute-start | bytes 196616 | tf_op jit(solution)/shard_map/ppermute | solution.py:20
  35.9 2.1 %collective-permute-start.13 = (bf16[256,128]{1,0:T(8,128)(2,1)S(1)}, bf16[256,128]{1,0:T(8,128)(2,1)S(1)}, u32[]{:S(2)}, u32[]{:S(2)}) collective-permute-start(bf16[256,128]{1,0:T(8,128)(2,1)S(1)} %shard_map.68.refs_0_), channel_id=1, source_target_pairs={{0,4},{4,0},{8,12},{12,8},{16,20},{20,16},{24,28},{28,24},{1,5},{5... | collective-permute-start | bytes 196616 | tf_op jit(solution)/shard_map/ppermute | solution.py:20
  38.0 1.7 %collective-permute-done.14.refs_5_ = bf16[256,128]{1,0:T(8,128)(2,1)S(1)} collective-permute-done((bf16[256,128]{1,0:T(8,128)(2,1)S(1)}, bf16[256,128]{1,0:T(8,128)(2,1)S(1)}, u32[]{:S(2)}, u32[]{:S(2)}) %collective-permute-start.14) | collective-permute-done | bytes 65568 | tf_op jit(solution)/shard_map/ppermute | solution.py:20
  39.9 0.7 collective-permute-done.11.refs_2_
  40.6 1.3 %collective-permute-start.15 = (bf16[256,128]{1,0:T(8,128)(2,1)S(1)}, bf16[256,128]{1,0:T(8,128)(2,1)S(1)}, u32[]{:S(2)}, u32[]{:S(2)}) collective-permute-start(bf16[256,128]{1,0:T(8,128)(2,1)S(1)} %collective-permute-done.11.refs_2_), channel_id=1, source_target_pairs={{0,4},{4,0},{8,12},{12,8},{16,20},{20,16},{24,28},{28,24},{1,5},{5... | collective-permute-start | bytes 196616 | tf_op jit(solution)/shard_map/ppermute | solution.py:20
  41.9 2.0 %collective-permute-done.10.refs_1_ = bf16[256,128]{1,0:T(8,128)(2,1)S(1)} collective-permute-done((bf16[256,128]{1,0:T(8,128)(2,1)S(1)}, bf16[256,128]{1,0:T(8,128)(2,1)S(1)}, u32[]{:S(2)}, u32[]{:S(2)}) %collective-permute-start.10) | collective-permute-done | bytes 65568 | tf_op jit(solution)/shard_map/ppermute | solution.py:20
  43.9 0.9 %collective-permute-done.15.refs_6_ = bf16[256,128]{1,0:T(8,128)(2,1)S(1)} collective-permute-done((bf16[256,128]{1,0:T(8,128)(2,1)S(1)}, bf16[256,128]{1,0:T(8,128)(2,1)S(1)}, u32[]{:S(2)}, u32[]{:S(2)}) %collective-permute-start.15) | collective-permute-done | bytes 65568 | tf_op jit(solution)/shard_map/ppermute | solution.py:20
  45.0 1.9 %collective-permute-done.18.other = bf16[2048,128]{1,0:T(8,128)(2,1)S(1)} collective-permute-done((bf16[2048,128]{1,0:T(8,128)(2,1)S(1)}, bf16[2048,128]{1,0:T(8,128)(2,1)S(1)}, u32[]{:S(2)}, u32[]{:S(2)}) %collective-permute-start.18) | collective-permute-done | bytes 524320 | tf_op jit(solution)/shard_map/ppermute | solution.py:20
  46.9 1.4 %shard_map.70 = (bf16[4,128,128]{2,1,0:T(8,128)(2,1)S(1)}, bf16[4,128,128]{2,1,0:T(8,128)(2,1)S(1)}, bf16[4,128,128]{2,1,0:T(8,128)(2,1)S(1)}, bf16[4,128,128]{2...) custom-call(bf16[32,128,128]{2,1,0:T(8,128)(2,1)S(1)} %bitcast.10, ...), custom_call_target="tpu_custom_call" | custom-call | tf_op jit(solution)/shard_map/pallas_call | solution.py:38
  48.3 1.8 %collective-permute-start.20 = (bf16[4,128,128]{2,1,0:T(8,128)(2,1)S(1)}, bf16[4,128,128]{2,1,0:T(8,128)(2,1)S(1)}, u32[]{:S(2)}, u32[]{:S(2)}) collective-permute-start(bf16[4,128,128]{2,1,0:T(8,128)(2,1)S(1)} %get-tuple-element.52), channel_id=1, source_target_pairs={{0,2},{1,5},{2,0},{3,7},{4,6},{5,1},{6,4},{7,3},{8,10},{9,13},{10,... | collective-permute-start | bytes 393224 | tf_op jit(solution)/shard_map/ppermute | solution.py:34
  50.1 1.1 %collective-permute-start.23 = (bf16[4,128,128]{2,1,0:T(8,128)(2,1)S(1)}, bf16[4,128,128]{2,1,0:T(8,128)(2,1)S(1)}, u32[]{:S(2)}, u32[]{:S(2)}) collective-permute-start(bf16[4,128,128]{2,1,0:T(8,128)(2,1)S(1)} %get-tuple-element.56), channel_id=1, source_target_pairs={{0,4},{1,3},{2,6},{3,1},{4,0},{5,7},{6,2},{7,5},{8,12},{9,11},{10,... | collective-permute-start | bytes 393224 | tf_op jit(solution)/shard_map/ppermute | solution.py:34
  51.2 0.5 collective-permute-start.19
  51.7 0.7 collective-permute-start.22
  52.4 2.1 %collective-permute-done.20.came = bf16[4,128,128]{2,1,0:T(8,128)(2,1)S(1)} collective-permute-done((bf16[4,128,128]{2,1,0:T(8,128)(2,1)S(1)}, bf16[4,128,128]{2,1,0:T(8,128)(2,1)S(1)}, u32[]{:S(2)}, u32[]{:S(2)}) %collective-permute-start.20) | collective-permute-done | bytes 131104 | tf_op jit(solution)/shard_map/ppermute | solution.py:34
  54.6 1.5 %collective-permute-start.21 = (bf16[4,128,128]{2,1,0:T(8,128)(2,1)S(1)}, bf16[4,128,128]{2,1,0:T(8,128)(2,1)S(1)}, u32[]{:S(2)}, u32[]{:S(2)}) collective-permute-start(bf16[4,128,128]{2,1,0:T(8,128)(2,1)S(1)} %shard_map.71), channel_id=1, source_target_pairs={{0,4},{1,3},{2,6},{3,1},{4,0},{5,7},{6,2},{7,5},{8,12},{9,11},{10,... | collective-permute-start | bytes 393224 | tf_op jit(solution)/shard_map/ppermute | solution.py:34
  56.2 1.6 %collective-permute-start.24 = (bf16[4,128,128]{2,1,0:T(8,128)(2,1)S(1)}, bf16[4,128,128]{2,1,0:T(8,128)(2,1)S(1)}, u32[]{:S(2)}, u32[]{:S(2)}) collective-permute-start(bf16[4,128,128]{2,1,0:T(8,128)(2,1)S(1)} %shard_map.72), channel_id=1, source_target_pairs={{0,2},{1,5},{2,0},{3,7},{4,6},{5,1},{6,4},{7,3},{8,10},{9,13},{10,... | collective-permute-start | bytes 393224 | tf_op jit(solution)/shard_map/ppermute | solution.py:34
  57.8 2.6 %collective-permute-done.21.refs_2_ = bf16[4,128,128]{2,1,0:T(8,128)(2,1)S(1)} collective-permute-done((bf16[4,128,128]{2,1,0:T(8,128)(2,1)S(1)}, bf16[4,128,128]{2,1,0:T(8,128)(2,1)S(1)}, u32[]{:S(2)}, u32[]{:S(2)}) %collective-permute-start.21) | collective-permute-done | bytes 131104 | tf_op jit(solution)/shard_map/ppermute | solution.py:34
  60.4 0.9 %collective-permute-done.24.refs_5_ = bf16[4,128,128]{2,1,0:T(8,128)(2,1)S(1)} collective-permute-done((bf16[4,128,128]{2,1,0:T(8,128)(2,1)S(1)}, bf16[4,128,128]{2,1,0:T(8,128)(2,1)S(1)}, u32[]{:S(2)}, u32[]{:S(2)}) %collective-permute-start.24) | collective-permute-done | bytes 131104 | tf_op jit(solution)/shard_map/ppermute | solution.py:34
  61.3 2.1 %collective-permute-start.25 = (bf16[2,128,128]{2,1,0:T(8,128)(2,1)S(1)}, bf16[2,128,128]{2,1,0:T(8,128)(2,1)S(1)}, u32[]{:S(2)}, u32[]{:S(2)}) collective-permute-start(bf16[2,128,128]{2,1,0:T(8,128)(2,1)S(1)} %get-tuple-element.58), channel_id=1, source_target_pairs={{0,8},{4,12},{8,0},{12,4},{16,24},{20,28},{24,16},{28,20},{1,9},{5... | collective-permute-start | bytes 196616 | tf_op jit(solution)/shard_map/ppermute | solution.py:20
  63.4 2.4 %collective-permute-start.27 = (bf16[2,128,128]{2,1,0:T(8,128)(2,1)S(1)}, bf16[2,128,128]{2,1,0:T(8,128)(2,1)S(1)}, u32[]{:S(2)}, u32[]{:S(2)}) collective-permute-start(bf16[2,128,128]{2,1,0:T(8,128)(2,1)S(1)} %get-tuple-element.60), channel_id=1, source_target_pairs={{0,24},{4,28},{8,16},{12,20},{16,8},{20,12},{24,0},{28,4},{1,25},{... | collective-permute-start | bytes 196616 | tf_op jit(solution)/shard_map/ppermute | solution.py:20
  65.8 4.4 %collective-permute-done.26.refs_1_ = bf16[2,128,128]{2,1,0:T(8,128)(2,1)S(1)} collective-permute-done((bf16[2,128,128]{2,1,0:T(8,128)(2,1)S(1)}, bf16[2,128,128]{2,1,0:T(8,128)(2,1)S(1)}, u32[]{:S(2)}, u32[]{:S(2)}) %collective-permute-start.26) | collective-permute-done | bytes 65568 | tf_op jit(solution)/shard_map/ppermute | solution.py:20
  70.4 1.8 %collective-permute-start.30 = (bf16[256,128]{1,0:T(8,128)(2,1)S(1)}, bf16[256,128]{1,0:T(8,128)(2,1)S(1)}, u32[]{:S(2)}, u32[]{:S(2)}) collective-permute-start(bf16[256,128]{1,0:T(8,128)(2,1)S(1)} %shard_map.74.refs_0_), channel_id=1, source_target_pairs={{0,24},{4,28},{8,16},{12,20},{16,8},{20,12},{24,0},{28,4},{1,25},{... | collective-permute-start | bytes 196616 | tf_op jit(solution)/shard_map/ppermute | solution.py:20
  72.2 1.1 %collective-permute-start.29 = (bf16[256,128]{1,0:T(8,128)(2,1)S(1)}, bf16[256,128]{1,0:T(8,128)(2,1)S(1)}, u32[]{:S(2)}, u32[]{:S(2)}) collective-permute-start(bf16[256,128]{1,0:T(8,128)(2,1)S(1)} %shard_map.74.refs_0_), channel_id=1, source_target_pairs={{0,16},{4,20},{8,24},{12,28},{16,0},{20,4},{24,8},{28,12},{1,17},{... | collective-permute-start | bytes 196616 | tf_op jit(solution)/shard_map/ppermute | solution.py:20
  73.3 1.7 %collective-permute-start.32 = (bf16[256,128]{1,0:T(8,128)(2,1)S(1)}, bf16[256,128]{1,0:T(8,128)(2,1)S(1)}, u32[]{:S(2)}, u32[]{:S(2)}) collective-permute-start(bf16[256,128]{1,0:T(8,128)(2,1)S(1)} %shard_map.74.refs_0_), channel_id=1, source_target_pairs={{0,12},{4,8},{8,4},{12,0},{16,28},{20,24},{24,20},{28,16},{1,13},{... | collective-permute-start | bytes 196616 | tf_op jit(solution)/shard_map/ppermute | solution.py:20
  74.9 1.4 %collective-permute-start.31 = (bf16[256,128]{1,0:T(8,128)(2,1)S(1)}, bf16[256,128]{1,0:T(8,128)(2,1)S(1)}, u32[]{:S(2)}, u32[]{:S(2)}) collective-permute-start(bf16[256,128]{1,0:T(8,128)(2,1)S(1)} %shard_map.74.refs_0_), channel_id=1, source_target_pairs={{0,4},{4,0},{8,12},{12,8},{16,20},{20,16},{24,28},{28,24},{1,5},{5... | collective-permute-start | bytes 196616 | tf_op jit(solution)/shard_map/ppermute | solution.py:20
  76.8 1.2 %collective-permute-start.34 = (bf16[256,128]{1,0:T(8,128)(2,1)S(1)}, bf16[256,128]{1,0:T(8,128)(2,1)S(1)}, u32[]{:S(2)}, u32[]{:S(2)}) collective-permute-start(bf16[256,128]{1,0:T(8,128)(2,1)S(1)} %collective-permute-done.30.refs_3_), channel_id=1, source_target_pairs={{0,4},{4,0},{8,12},{12,8},{16,20},{20,16},{24,28},{28,24},{1,5},{5... | collective-permute-start | bytes 196616 | tf_op jit(solution)/shard_map/ppermute | solution.py:20
  78.0 0.6 collective-permute-done.29.refs_2_
  78.6 0.5 collective-permute-start.33
  79.7 0.9 %collective-permute-done.28.refs_1_ = bf16[256,128]{1,0:T(8,128)(2,1)S(1)} collective-permute-done((bf16[256,128]{1,0:T(8,128)(2,1)S(1)}, bf16[256,128]{1,0:T(8,128)(2,1)S(1)}, u32[]{:S(2)}, u32[]{:S(2)}) %collective-permute-start.28) | collective-permute-done | bytes 65568 | tf_op jit(solution)/shard_map/ppermute | solution.py:20
  80.6 0.9 %collective-permute-done.34.refs_7_ = bf16[256,128]{1,0:T(8,128)(2,1)S(1)} collective-permute-done((bf16[256,128]{1,0:T(8,128)(2,1)S(1)}, bf16[256,128]{1,0:T(8,128)(2,1)S(1)}, u32[]{:S(2)}, u32[]{:S(2)}) %collective-permute-start.34) | collective-permute-done | bytes 65568 | tf_op jit(solution)/shard_map/ppermute | solution.py:20
  81.5 1.4 %collective-permute-done.33.refs_6_ = bf16[256,128]{1,0:T(8,128)(2,1)S(1)} collective-permute-done((bf16[256,128]{1,0:T(8,128)(2,1)S(1)}, bf16[256,128]{1,0:T(8,128)(2,1)S(1)}, u32[]{:S(2)}, u32[]{:S(2)}) %collective-permute-start.33) | collective-permute-done | bytes 65568 | tf_op jit(solution)/shard_map/ppermute | solution.py:20
  82.9 1.0 %shard_map.75 = bf16[2,1,2048,128]{3,2,1,0:T(8,128)(2,1)} custom-call(bf16[1,2048,128]{2,1,0:T(8,128)(2,1)S(1)} %bitcast.11, bf16[256,128]{1,0:T(8,128)(2,1)S(1)} %shard_map.74.refs_0_, bf16[256,128]{1,0:T(8,128)(2,1)S(1)} %collective-permute-done.28.refs_1_, bf16[256,128]{1,0:T(8,128)(2,1)S(1)} %collective-permute-done.29.refs_2_, ...), custom_call_target="tpu_custom_call" | custom-call | tf_op jit(solution)/shard_map/pallas_call | solution.py:38
  (42 shorter events, 3.6 us)
Async XLA Ops:
  0.7 0.7 copy-start.3
  3.6 17.4 %collective-permute-start.6 = (bf16[2048,128]{1,0:T(8,128)(2,1)S(1)}, bf16[2048,128]{1,0:T(8,128)(2,1)S(1)}, u32[]{:S(2)}, u32[]{:S(2)}) collective-permute-start(bf16[2048,128]{1,0:T(8,128)(2,1)S(1)} %get-tuple-element.41.refs_6_), channel_id=1, source_target_pairs={{4,12},{12,20},{20,28},{5,13},{13,21},{21,29},{6,14},{14,22},{22,3... | collective-permute-start | bytes 1572872 | tf_op jit(solution)/shard_map/ppermute | solution.py:282
  4.3 7.9 %collective-permute-start.1 = (bf16[4,128,128]{2,1,0:T(8,128)(2,1)S(1)}, bf16[4,128,128]{2,1,0:T(8,128)(2,1)S(1)}, u32[]{:S(2)}, u32[]{:S(2)}) collective-permute-start(bf16[4,128,128]{2,1,0:T(8,128)(2,1)S(1)} %get-tuple-element.36), channel_id=1, source_target_pairs={{0,2},{1,5},{2,0},{3,7},{4,6},{5,1},{6,4},{7,3},{8,10},{9,13},{10,... | collective-permute-start | bytes 393224 | tf_op jit(solution)/shard_map/ppermute | solution.py:34
  7.3 8.6 %collective-permute-start.4 = (bf16[4,128,128]{2,1,0:T(8,128)(2,1)S(1)}, bf16[4,128,128]{2,1,0:T(8,128)(2,1)S(1)}, u32[]{:S(2)}, u32[]{:S(2)}) collective-permute-start(bf16[4,128,128]{2,1,0:T(8,128)(2,1)S(1)} %get-tuple-element.40), channel_id=1, source_target_pairs={{0,4},{1,3},{2,6},{3,1},{4,0},{5,7},{6,2},{7,5},{8,12},{9,11},{10,... | collective-permute-start | bytes 393224 | tf_op jit(solution)/shard_map/ppermute | solution.py:34
  11.6 6.4 %collective-permute-start = (bf16[4,128,128]{2,1,0:T(8,128)(2,1)S(1)}, bf16[4,128,128]{2,1,0:T(8,128)(2,1)S(1)}, u32[]{:S(2)}, u32[]{:S(2)}) collective-permute-start(bf16[4,128,128]{2,1,0:T(8,128)(2,1)S(1)} %get-tuple-element.34), channel_id=1, source_target_pairs={{0,2},{1,5},{2,0},{3,7},{4,6},{5,1},{6,4},{7,3},{8,10},{9,13},{10,... | collective-permute-start | bytes 393224 | tf_op jit(solution)/shard_map/ppermute | solution.py:34
  12.1 6.4 %collective-permute-start.3 = (bf16[4,128,128]{2,1,0:T(8,128)(2,1)S(1)}, bf16[4,128,128]{2,1,0:T(8,128)(2,1)S(1)}, u32[]{:S(2)}, u32[]{:S(2)}) collective-permute-start(bf16[4,128,128]{2,1,0:T(8,128)(2,1)S(1)} %get-tuple-element.38), channel_id=1, source_target_pairs={{0,4},{1,3},{2,6},{3,1},{4,0},{5,7},{6,2},{7,5},{8,12},{9,11},{10,... | collective-permute-start | bytes 393224 | tf_op jit(solution)/shard_map/ppermute | solution.py:34
  12.2 8.0 %collective-permute-start.2 = (bf16[4,128,128]{2,1,0:T(8,128)(2,1)S(1)}, bf16[4,128,128]{2,1,0:T(8,128)(2,1)S(1)}, u32[]{:S(2)}, u32[]{:S(2)}) collective-permute-start(bf16[4,128,128]{2,1,0:T(8,128)(2,1)S(1)} %shard_map.65), channel_id=1, source_target_pairs={{0,4},{1,3},{2,6},{3,1},{4,0},{5,7},{6,2},{7,5},{8,12},{9,11},{10,... | collective-permute-start | bytes 393224 | tf_op jit(solution)/shard_map/ppermute | solution.py:34
  15.9 16.8 %copy-start.1 = (bf16[2,1,2048,128]{3,2,1,0:T(8,128)(2,1)S(1)}, bf16[2,1,2048,128]{3,2,1,0:T(8,128)(2,1)}, u32[]{:S(2)}) copy-start(bf16[2,1,2048,128]{3,2,1,0:T(8,128)(2,1)} %refs_3_.3) | copy-start | bytes 3145732
  16.0 5.0 %collective-permute-start.5 = (bf16[4,128,128]{2,1,0:T(8,128)(2,1)S(1)}, bf16[4,128,128]{2,1,0:T(8,128)(2,1)S(1)}, u32[]{:S(2)}, u32[]{:S(2)}) collective-permute-start(bf16[4,128,128]{2,1,0:T(8,128)(2,1)S(1)} %shard_map.66), channel_id=1, source_target_pairs={{0,2},{1,5},{2,0},{3,7},{4,6},{5,1},{6,4},{7,3},{8,10},{9,13},{10,... | collective-permute-start | bytes 393224 | tf_op jit(solution)/shard_map/ppermute | solution.py:34
  21.0 11.8 %copy-start.2 = (bf16[1,16,128,128]{3,2,1,0:T(8,128)(2,1)S(1)}, bf16[1,16,128,128]{3,2,1,0:T(8,128)(2,1)}, u32[]{:S(2)}) copy-start(bf16[1,16,128,128]{3,2,1,0:T(8,128)(2,1)} %refs_4_.3) | copy-start | bytes 1572868
  21.2 23.7 %collective-permute-start.17 = (bf16[2048,128]{1,0:T(8,128)(2,1)S(1)}, bf16[2048,128]{1,0:T(8,128)(2,1)S(1)}, u32[]{:S(2)}, u32[]{:S(2)}) collective-permute-start(bf16[2048,128]{1,0:T(8,128)(2,1)S(1)} %get-tuple-element.46), channel_id=1, source_target_pairs={{0,4},{4,0},{8,12},{12,8},{16,20},{20,16},{24,28},{28,24},{1,5},{5... | collective-permute-start | bytes 1572872 | tf_op jit(solution)/shard_map/ppermute | solution.py:20
  21.9 4.9 %collective-permute-start.7 = (bf16[2,128,128]{2,1,0:T(8,128)(2,1)S(1)}, bf16[2,128,128]{2,1,0:T(8,128)(2,1)S(1)}, u32[]{:S(2)}, u32[]{:S(2)}) collective-permute-start(bf16[2,128,128]{2,1,0:T(8,128)(2,1)S(1)} %get-tuple-element.43), channel_id=1, source_target_pairs={{0,8},{4,12},{8,0},{12,4},{16,24},{20,28},{24,16},{28,20},{1,9},{5... | collective-permute-start | bytes 196616 | tf_op jit(solution)/shard_map/ppermute | solution.py:20
  23.9 6.6 %collective-permute-start.8 = (bf16[2,128,128]{2,1,0:T(8,128)(2,1)S(1)}, bf16[2,128,128]{2,1,0:T(8,128)(2,1)S(1)}, u32[]{:S(2)}, u32[]{:S(2)}) collective-permute-start(bf16[2,128,128]{2,1,0:T(8,128)(2,1)S(1)} %get-tuple-element.44), channel_id=1, source_target_pairs={{0,16},{4,20},{8,24},{12,28},{16,0},{20,4},{24,8},{28,12},{1,17},{... | collective-permute-start | bytes 196616 | tf_op jit(solution)/shard_map/ppermute | solution.py:20
  26.4 6.3 %collective-permute-start.9 = (bf16[2,128,128]{2,1,0:T(8,128)(2,1)S(1)}, bf16[2,128,128]{2,1,0:T(8,128)(2,1)S(1)}, u32[]{:S(2)}, u32[]{:S(2)}) collective-permute-start(bf16[2,128,128]{2,1,0:T(8,128)(2,1)S(1)} %get-tuple-element.45), channel_id=1, source_target_pairs={{0,24},{4,28},{8,16},{12,20},{16,8},{20,12},{24,0},{28,4},{1,25},{... | collective-permute-start | bytes 196616 | tf_op jit(solution)/shard_map/ppermute | solution.py:20
  32.8 14.1 %copy-start = (bf16[1,1,1,32,128,128]{5,4,3,2,1,0:T(8,128)(2,1)S(1)}, bf16[1,1,1,32,128,128]{5,4,3,2,1,0:T(8,128)(2,1)}, u32[]{:S(2)}) copy-start(bf16[1,1,1,32,128,128]{5,4,3,2,1,0:T(8,128)(2,1)} %param.6) | copy-start | bytes 3145732
  33.0 6.7 %collective-permute-start.14 = (bf16[256,128]{1,0:T(8,128)(2,1)S(1)}, bf16[256,128]{1,0:T(8,128)(2,1)S(1)}, u32[]{:S(2)}, u32[]{:S(2)}) collective-permute-start(bf16[256,128]{1,0:T(8,128)(2,1)S(1)} %shard_map.68.refs_0_), channel_id=1, source_target_pairs={{0,12},{4,8},{8,4},{12,0},{16,28},{20,24},{24,20},{28,16},{1,13},{... | collective-permute-start | bytes 196616 | tf_op jit(solution)/shard_map/ppermute | solution.py:20
  33.0 6.6 %collective-permute-start.12 = (bf16[256,128]{1,0:T(8,128)(2,1)S(1)}, bf16[256,128]{1,0:T(8,128)(2,1)S(1)}, u32[]{:S(2)}, u32[]{:S(2)}) collective-permute-start(bf16[256,128]{1,0:T(8,128)(2,1)S(1)} %shard_map.68.refs_0_), channel_id=1, source_target_pairs={{0,24},{4,28},{8,16},{12,20},{16,8},{20,12},{24,0},{28,4},{1,25},{... | collective-permute-start | bytes 196616 | tf_op jit(solution)/shard_map/ppermute | solution.py:20
  34.8 5.8 %collective-permute-start.11 = (bf16[256,128]{1,0:T(8,128)(2,1)S(1)}, bf16[256,128]{1,0:T(8,128)(2,1)S(1)}, u32[]{:S(2)}, u32[]{:S(2)}) collective-permute-start(bf16[256,128]{1,0:T(8,128)(2,1)S(1)} %shard_map.68.refs_0_), channel_id=1, source_target_pairs={{0,16},{4,20},{8,24},{12,28},{16,0},{20,4},{24,8},{28,12},{1,17},{... | collective-permute-start | bytes 196616 | tf_op jit(solution)/shard_map/ppermute | solution.py:20
  35.9 6.0 %collective-permute-start.13 = (bf16[256,128]{1,0:T(8,128)(2,1)S(1)}, bf16[256,128]{1,0:T(8,128)(2,1)S(1)}, u32[]{:S(2)}, u32[]{:S(2)}) collective-permute-start(bf16[256,128]{1,0:T(8,128)(2,1)S(1)} %shard_map.68.refs_0_), channel_id=1, source_target_pairs={{0,4},{4,0},{8,12},{12,8},{16,20},{20,16},{24,28},{28,24},{1,5},{5... | collective-permute-start | bytes 196616 | tf_op jit(solution)/shard_map/ppermute | solution.py:20
  39.7 4.3 %collective-permute-start.10 = (bf16[256,128]{1,0:T(8,128)(2,1)S(1)}, bf16[256,128]{1,0:T(8,128)(2,1)S(1)}, u32[]{:S(2)}, u32[]{:S(2)}) collective-permute-start(bf16[256,128]{1,0:T(8,128)(2,1)S(1)} %shard_map.68.refs_0_), channel_id=1, source_target_pairs={{0,8},{4,12},{8,0},{12,4},{16,24},{20,28},{24,16},{28,20},{1,9},{5... | collective-permute-start | bytes 196616 | tf_op jit(solution)/shard_map/ppermute | solution.py:20
  39.7 4.3 %collective-permute-start.16 = (bf16[256,128]{1,0:T(8,128)(2,1)S(1)}, bf16[256,128]{1,0:T(8,128)(2,1)S(1)}, u32[]{:S(2)}, u32[]{:S(2)}) collective-permute-start(bf16[256,128]{1,0:T(8,128)(2,1)S(1)} %collective-permute-done.12.refs_3_), channel_id=1, source_target_pairs={{0,4},{4,0},{8,12},{12,8},{16,20},{20,16},{24,28},{28,24},{1,5},{5... | collective-permute-start | bytes 196616 | tf_op jit(solution)/shard_map/ppermute | solution.py:20
  40.6 4.3 %collective-permute-start.15 = (bf16[256,128]{1,0:T(8,128)(2,1)S(1)}, bf16[256,128]{1,0:T(8,128)(2,1)S(1)}, u32[]{:S(2)}, u32[]{:S(2)}) collective-permute-start(bf16[256,128]{1,0:T(8,128)(2,1)S(1)} %collective-permute-done.11.refs_2_), channel_id=1, source_target_pairs={{0,4},{4,0},{8,12},{12,8},{16,20},{20,16},{24,28},{28,24},{1,5},{5... | collective-permute-start | bytes 196616 | tf_op jit(solution)/shard_map/ppermute | solution.py:20
  44.9 2.0 %collective-permute-start.18 = (bf16[2048,128]{1,0:T(8,128)(2,1)S(1)}, bf16[2048,128]{1,0:T(8,128)(2,1)S(1)}, u32[]{:S(2)}, u32[]{:S(2)}) collective-permute-start(bf16[2048,128]{1,0:T(8,128)(2,1)S(1)} %get-tuple-element.48.own), channel_id=1, source_target_pairs={{0,1},{1,0},{2,3},{3,2},{4,5},{5,4},{6,7},{7,6},{8,9},{9,8},{10,11... | collective-permute-start | bytes 1572872 | tf_op jit(solution)/shard_map/ppermute | solution.py:20
  48.3 6.2 %collective-permute-start.20 = (bf16[4,128,128]{2,1,0:T(8,128)(2,1)S(1)}, bf16[4,128,128]{2,1,0:T(8,128)(2,1)S(1)}, u32[]{:S(2)}, u32[]{:S(2)}) collective-permute-start(bf16[4,128,128]{2,1,0:T(8,128)(2,1)S(1)} %get-tuple-element.52), channel_id=1, source_target_pairs={{0,2},{1,5},{2,0},{3,7},{4,6},{5,1},{6,4},{7,3},{8,10},{9,13},{10,... | collective-permute-start | bytes 393224 | tf_op jit(solution)/shard_map/ppermute | solution.py:34
  50.1 6.1 %collective-permute-start.23 = (bf16[4,128,128]{2,1,0:T(8,128)(2,1)S(1)}, bf16[4,128,128]{2,1,0:T(8,128)(2,1)S(1)}, u32[]{:S(2)}, u32[]{:S(2)}) collective-permute-start(bf16[4,128,128]{2,1,0:T(8,128)(2,1)S(1)} %get-tuple-element.56), channel_id=1, source_target_pairs={{0,4},{1,3},{2,6},{3,1},{4,0},{5,7},{6,2},{7,5},{8,12},{9,11},{10,... | collective-permute-start | bytes 393224 | tf_op jit(solution)/shard_map/ppermute | solution.py:34
  51.2 6.6 %collective-permute-start.19 = (bf16[4,128,128]{2,1,0:T(8,128)(2,1)S(1)}, bf16[4,128,128]{2,1,0:T(8,128)(2,1)S(1)}, u32[]{:S(2)}, u32[]{:S(2)}) collective-permute-start(bf16[4,128,128]{2,1,0:T(8,128)(2,1)S(1)} %get-tuple-element.50), channel_id=1, source_target_pairs={{0,2},{1,5},{2,0},{3,7},{4,6},{5,1},{6,4},{7,3},{8,10},{9,13},{10,... | collective-permute-start | bytes 393224 | tf_op jit(solution)/shard_map/ppermute | solution.py:34
  51.7 6.1 %collective-permute-start.22 = (bf16[4,128,128]{2,1,0:T(8,128)(2,1)S(1)}, bf16[4,128,128]{2,1,0:T(8,128)(2,1)S(1)}, u32[]{:S(2)}, u32[]{:S(2)}) collective-permute-start(bf16[4,128,128]{2,1,0:T(8,128)(2,1)S(1)} %get-tuple-element.54), channel_id=1, source_target_pairs={{0,4},{1,3},{2,6},{3,1},{4,0},{5,7},{6,2},{7,5},{8,12},{9,11},{10,... | collective-permute-start | bytes 393224 | tf_op jit(solution)/shard_map/ppermute | solution.py:34
  54.6 5.8 %collective-permute-start.21 = (bf16[4,128,128]{2,1,0:T(8,128)(2,1)S(1)}, bf16[4,128,128]{2,1,0:T(8,128)(2,1)S(1)}, u32[]{:S(2)}, u32[]{:S(2)}) collective-permute-start(bf16[4,128,128]{2,1,0:T(8,128)(2,1)S(1)} %shard_map.71), channel_id=1, source_target_pairs={{0,4},{1,3},{2,6},{3,1},{4,0},{5,7},{6,2},{7,5},{8,12},{9,11},{10,... | collective-permute-start | bytes 393224 | tf_op jit(solution)/shard_map/ppermute | solution.py:34
  56.2 5.0 %collective-permute-start.24 = (bf16[4,128,128]{2,1,0:T(8,128)(2,1)S(1)}, bf16[4,128,128]{2,1,0:T(8,128)(2,1)S(1)}, u32[]{:S(2)}, u32[]{:S(2)}) collective-permute-start(bf16[4,128,128]{2,1,0:T(8,128)(2,1)S(1)} %shard_map.72), channel_id=1, source_target_pairs={{0,2},{1,5},{2,0},{3,7},{4,6},{5,1},{6,4},{7,3},{8,10},{9,13},{10,... | collective-permute-start | bytes 393224 | tf_op jit(solution)/shard_map/ppermute | solution.py:34
  61.3 4.5 %collective-permute-start.25 = (bf16[2,128,128]{2,1,0:T(8,128)(2,1)S(1)}, bf16[2,128,128]{2,1,0:T(8,128)(2,1)S(1)}, u32[]{:S(2)}, u32[]{:S(2)}) collective-permute-start(bf16[2,128,128]{2,1,0:T(8,128)(2,1)S(1)} %get-tuple-element.58), channel_id=1, source_target_pairs={{0,8},{4,12},{8,0},{12,4},{16,24},{20,28},{24,16},{28,20},{1,9},{5... | collective-permute-start | bytes 196616 | tf_op jit(solution)/shard_map/ppermute | solution.py:20
  63.4 6.8 %collective-permute-start.26 = (bf16[2,128,128]{2,1,0:T(8,128)(2,1)S(1)}, bf16[2,128,128]{2,1,0:T(8,128)(2,1)S(1)}, u32[]{:S(2)}, u32[]{:S(2)}) collective-permute-start(bf16[2,128,128]{2,1,0:T(8,128)(2,1)S(1)} %get-tuple-element.59), channel_id=1, source_target_pairs={{0,16},{4,20},{8,24},{12,28},{16,0},{20,4},{24,8},{28,12},{1,17},{... | collective-permute-start | bytes 196616 | tf_op jit(solution)/shard_map/ppermute | solution.py:20
  63.4 6.8 %collective-permute-start.27 = (bf16[2,128,128]{2,1,0:T(8,128)(2,1)S(1)}, bf16[2,128,128]{2,1,0:T(8,128)(2,1)S(1)}, u32[]{:S(2)}, u32[]{:S(2)}) collective-permute-start(bf16[2,128,128]{2,1,0:T(8,128)(2,1)S(1)} %get-tuple-element.60), channel_id=1, source_target_pairs={{0,24},{4,28},{8,16},{12,20},{16,8},{20,12},{24,0},{28,4},{1,25},{... | collective-permute-start | bytes 196616 | tf_op jit(solution)/shard_map/ppermute | solution.py:20
  70.4 6.3 %collective-permute-start.30 = (bf16[256,128]{1,0:T(8,128)(2,1)S(1)}, bf16[256,128]{1,0:T(8,128)(2,1)S(1)}, u32[]{:S(2)}, u32[]{:S(2)}) collective-permute-start(bf16[256,128]{1,0:T(8,128)(2,1)S(1)} %shard_map.74.refs_0_), channel_id=1, source_target_pairs={{0,24},{4,28},{8,16},{12,20},{16,8},{20,12},{24,0},{28,4},{1,25},{... | collective-permute-start | bytes 196616 | tf_op jit(solution)/shard_map/ppermute | solution.py:20
  72.2 6.4 %collective-permute-start.29 = (bf16[256,128]{1,0:T(8,128)(2,1)S(1)}, bf16[256,128]{1,0:T(8,128)(2,1)S(1)}, u32[]{:S(2)}, u32[]{:S(2)}) collective-permute-start(bf16[256,128]{1,0:T(8,128)(2,1)S(1)} %shard_map.74.refs_0_), channel_id=1, source_target_pairs={{0,16},{4,20},{8,24},{12,28},{16,0},{20,4},{24,8},{28,12},{1,17},{... | collective-permute-start | bytes 196616 | tf_op jit(solution)/shard_map/ppermute | solution.py:20
  73.3 6.0 %collective-permute-start.32 = (bf16[256,128]{1,0:T(8,128)(2,1)S(1)}, bf16[256,128]{1,0:T(8,128)(2,1)S(1)}, u32[]{:S(2)}, u32[]{:S(2)}) collective-permute-start(bf16[256,128]{1,0:T(8,128)(2,1)S(1)} %shard_map.74.refs_0_), channel_id=1, source_target_pairs={{0,12},{4,8},{8,4},{12,0},{16,28},{20,24},{24,20},{28,16},{1,13},{... | collective-permute-start | bytes 196616 | tf_op jit(solution)/shard_map/ppermute | solution.py:20
  74.9 4.8 %collective-permute-start.31 = (bf16[256,128]{1,0:T(8,128)(2,1)S(1)}, bf16[256,128]{1,0:T(8,128)(2,1)S(1)}, u32[]{:S(2)}, u32[]{:S(2)}) collective-permute-start(bf16[256,128]{1,0:T(8,128)(2,1)S(1)} %shard_map.74.refs_0_), channel_id=1, source_target_pairs={{0,4},{4,0},{8,12},{12,8},{16,20},{20,16},{24,28},{28,24},{1,5},{5... | collective-permute-start | bytes 196616 | tf_op jit(solution)/shard_map/ppermute | solution.py:20
  76.3 4.3 %collective-permute-start.28 = (bf16[256,128]{1,0:T(8,128)(2,1)S(1)}, bf16[256,128]{1,0:T(8,128)(2,1)S(1)}, u32[]{:S(2)}, u32[]{:S(2)}) collective-permute-start(bf16[256,128]{1,0:T(8,128)(2,1)S(1)} %shard_map.74.refs_0_), channel_id=1, source_target_pairs={{0,8},{4,12},{8,0},{12,4},{16,24},{20,28},{24,16},{28,20},{1,9},{5... | collective-permute-start | bytes 196616 | tf_op jit(solution)/shard_map/ppermute | solution.py:20
  76.8 4.7 %collective-permute-start.34 = (bf16[256,128]{1,0:T(8,128)(2,1)S(1)}, bf16[256,128]{1,0:T(8,128)(2,1)S(1)}, u32[]{:S(2)}, u32[]{:S(2)}) collective-permute-start(bf16[256,128]{1,0:T(8,128)(2,1)S(1)} %collective-permute-done.30.refs_3_), channel_id=1, source_target_pairs={{0,4},{4,0},{8,12},{12,8},{16,20},{20,16},{24,28},{28,24},{1,5},{5... | collective-permute-start | bytes 196616 | tf_op jit(solution)/shard_map/ppermute | solution.py:20
  78.6 4.3 %collective-permute-start.33 = (bf16[256,128]{1,0:T(8,128)(2,1)S(1)}, bf16[256,128]{1,0:T(8,128)(2,1)S(1)}, u32[]{:S(2)}, u32[]{:S(2)}) collective-permute-start(bf16[256,128]{1,0:T(8,128)(2,1)S(1)} %collective-permute-done.29.refs_2_), channel_id=1, source_target_pairs={{0,4},{4,0},{8,12},{12,8},{16,20},{20,16},{24,28},{28,24},{1,5},{5... | collective-permute-start | bytes 196616 | tf_op jit(solution)/shard_map/ppermute | solution.py:20

commit v7 on v6

--- a/solution.py
+++ b/solution.py
@@ -32,6 +32,23 @@
                     ((d * srcs + s) * cores + t, (to[0] * srcs + to[1]) * cores + t)
                 )
     return lax.ppermute(array, ("delay", "src", "tgt"), pairs)
+
+
+def along_g(p, array, k):
+    cores = lax.axis_size("tgt")
+    return lax.ppermute(
+        array,
+        ("delay", "tgt"),
+        [
+            (d * cores + t, (d ^ (2 * (k if t % 2 == 0 else p.groups - k))) * cores + t)
+            for d in range(p.bins)
+            for t in range(cores)
+        ],
+    )
+
+
+def own_turn(p, k):
+    return jnp.where(lax.axis_index("tgt") & 1 == 0, k, p.groups - k) if k else 0
 
 
 def call(kernel, outs, specs, scratch, *args, grant=32 * MIB):
@@ -201,7 +218,7 @@
 
     here = p.g()
     for k, ref in enumerate(outs):
-        g = here ^ k
+        g = here ^ own_turn(p, k)
         for piece in range(2):
             ref[piece] = total(*(term[g] for term in ins[3 * piece : 3 * piece + 3]))
 
@@ -315,7 +332,7 @@
         ]
         by *= 2
     keep, *sends = terms
-    came = [exchange(v, "delay", 2 * k) for k, v in enumerate(sends, 1)]
+    came = [along_g(p, v, k) for k, v in enumerate(sends, 1)]
     return [keep, *came], shifted
 
 

time: 84.1 us -> 83.3 us (level)
  waiting for transfers between devices: 31.5 us -> 29.9 us
    ppermute x22 -> x16, waiting for transfers between devices: 22.3 us -> 10.7 us  [exchange(): return lax.ppermute(array, axis, [(i, i ^ by) for i in range(peers)])]
    ppermute x0 -> x6, waiting for transfers between devices: none -> 10.1 us  [along_g(): lax.ppermute(array, ('delay', 'tgt'), [(d * cores + t, (d ^ 2 * (k if t %...]
    ppermute x0 -> x6, starting transfers between devices: none -> 9.02 us  [along_g(): lax.ppermute(array, ('delay', 'tgt'), [(d * cores + t, (d ^ 2 * (k if t %...]
    ppermute x22 -> x16, starting transfers between devices: 24.5 us -> 16.3 us  [exchange(): return lax.ppermute(array, axis, [(i, i ^ by) for i in range(peers)])]
  transfers between devices with their start and end apart: 35 -> 35, of which waited for: 23 -> 26; matrix products, arithmetic and copies ran while one was open for 0% -> 0% of each run, Pallas kernels for 0% -> 0%
where the time goes in v7:
time: 83.3 us; the launch traced here: 83.1 us
  starting transfers between devices  46.3 us (56%)
  waiting for transfers between devices  29.9 us (36%)
  Pallas kernels  5.44 us (7%)
    ppermute x12, starting transfers between devices, hop(): return lax.ppermute(array, ('delay', 'src', 'tgt'), pairs)  20.3 us
    ppermute x16, starting transfers between devices, exchange(): return lax.ppermute(array, axis, [(i, i ^ by) for i in range(peers)])  16.3 us
    ppermute x16, waiting for transfers between devices, exchange(): return lax.ppermute(array, axis, [(i, i ^ by) for i in range(peers)])  10.7 us
    ppermute x6, waiting for transfers between devices, along_g(): lax.ppermute(array, ('delay', 'tgt'), [(d * cores + t, (d ^ 2 * (k if t %...  10.1 us
    ppermute x12, waiting for transfers between devices, hop(): return lax.ppermute(array, ('delay', 'src', 'tgt'), pairs)  9.11 us
    ppermute x6, starting transfers between devices, along_g(): lax.ppermute(array, ('delay', 'tgt'), [(d * cores + t, (d ^ 2 * (k if t %...  9.02 us
    pallas_call x12, Pallas kernels, call(): pl.pallas_call(kernel, out_shape=outs, in_specs=specs, out_specs=[VMEM] *...  5.44 us
  transfers between devices with their start and end apart: 35, of which 26 were waited for; matrix products, arithmetic and copies ran while one was open for 0% of the time, Pallas kernels for 0%

profile of v7, /device:TPU:0, one launch (start us, length us, event | category | flops | bytes accessed | tf_op | source)
XLA Modules:
  0.0 83.1 jit_solution(6962512788269189717)
XLA Ops:
  0.7 0.7 copy-done.3
  1.3 2.2 %shard_map.64 = (bf16[4,128,128]{2,1,0:T(8,128)(2,1)S(1)}, bf16[4,128,128]{2,1,0:T(8,128)(2,1)S(1)}, bf16[4,128,128]{2,1,0:T(8,128)(2,1)S(1)}, bf16[4,128,128]{2...) custom-call(bf16[32,128,128]{2,1,0:T(8,128)(2,1)} %bitcast.9, ...), custom_call_target="tpu_custom_call" | custom-call | tf_op jit(solution)/shard_map/pallas_call | solution.py:55
  3.6 0.7 collective-permute-start.6
  4.3 3.0 %collective-permute-start.1 = (bf16[4,128,128]{2,1,0:T(8,128)(2,1)S(1)}, bf16[4,128,128]{2,1,0:T(8,128)(2,1)S(1)}, u32[]{:S(2)}, u32[]{:S(2)}) collective-permute-start(bf16[4,128,128]{2,1,0:T(8,128)(2,1)S(1)} %get-tuple-element.36), channel_id=1, source_target_pairs={{0,2},{1,5},{2,0},{3,7},{4,6},{5,1},{6,4},{7,3},{8,10},{9,13},{10,... | collective-permute-start | bytes 393224 | tf_op jit(solution)/shard_map/ppermute | solution.py:34
  7.3 4.3 %collective-permute-start.4 = (bf16[4,128,128]{2,1,0:T(8,128)(2,1)S(1)}, bf16[4,128,128]{2,1,0:T(8,128)(2,1)S(1)}, u32[]{:S(2)}, u32[]{:S(2)}) collective-permute-start(bf16[4,128,128]{2,1,0:T(8,128)(2,1)S(1)} %get-tuple-element.40), channel_id=1, source_target_pairs={{0,4},{1,3},{2,6},{3,1},{4,0},{5,7},{6,2},{7,5},{8,12},{9,11},{10,... | collective-permute-start | bytes 393224 | tf_op jit(solution)/shard_map/ppermute | solution.py:34
  12.2 3.3 %collective-permute-start.2 = (bf16[4,128,128]{2,1,0:T(8,128)(2,1)S(1)}, bf16[4,128,128]{2,1,0:T(8,128)(2,1)S(1)}, u32[]{:S(2)}, u32[]{:S(2)}) collective-permute-start(bf16[4,128,128]{2,1,0:T(8,128)(2,1)S(1)} %shard_map.65), channel_id=1, source_target_pairs={{0,4},{1,3},{2,6},{3,1},{4,0},{5,7},{6,2},{7,5},{8,12},{9,11},{10,... | collective-permute-start | bytes 393224 | tf_op jit(solution)/shard_map/ppermute | solution.py:34
  16.0 2.1 %collective-permute-start.5 = (bf16[4,128,128]{2,1,0:T(8,128)(2,1)S(1)}, bf16[4,128,128]{2,1,0:T(8,128)(2,1)S(1)}, u32[]{:S(2)}, u32[]{:S(2)}) collective-permute-start(bf16[4,128,128]{2,1,0:T(8,128)(2,1)S(1)} %shard_map.66), channel_id=1, source_target_pairs={{0,2},{1,5},{2,0},{3,7},{4,6},{5,1},{6,4},{7,3},{8,10},{9,13},{10,... | collective-permute-start | bytes 393224 | tf_op jit(solution)/shard_map/ppermute | solution.py:34
  18.5 1.7 %collective-permute-done.2.refs_2_ = bf16[4,128,128]{2,1,0:T(8,128)(2,1)S(1)} collective-permute-done((bf16[4,128,128]{2,1,0:T(8,128)(2,1)S(1)}, bf16[4,128,128]{2,1,0:T(8,128)(2,1)S(1)}, u32[]{:S(2)}, u32[]{:S(2)}) %collective-permute-start.2) | collective-permute-done | bytes 131104 | tf_op jit(solution)/shard_map/ppermute | solution.py:34
  20.2 0.8 collective-permute-done.5.refs_5_
  21.2 0.7 collective-permute-start.17
  21.9 2.0 %collective-permute-start.7 = (bf16[2,128,128]{2,1,0:T(8,128)(2,1)S(1)}, bf16[2,128,128]{2,1,0:T(8,128)(2,1)S(1)}, u32[]{:S(2)}, u32[]{:S(2)}) collective-permute-start(bf16[2,128,128]{2,1,0:T(8,128)(2,1)S(1)} %get-tuple-element.43), channel_id=1, source_target_pairs={{0,8},{1,25},{4,12},{5,29},{8,0},{9,17},{12,4},{13,21},{16,24},{17... | collective-permute-start | bytes 196616 | tf_op jit(solution)/shard_map/ppermute | solution.py:39
  23.9 2.6 %collective-permute-start.8 = (bf16[2,128,128]{2,1,0:T(8,128)(2,1)S(1)}, bf16[2,128,128]{2,1,0:T(8,128)(2,1)S(1)}, u32[]{:S(2)}, u32[]{:S(2)}) collective-permute-start(bf16[2,128,128]{2,1,0:T(8,128)(2,1)S(1)} %get-tuple-element.44), channel_id=1, source_target_pairs={{0,16},{1,17},{4,20},{5,21},{8,24},{9,25},{12,28},{13,29},{16,0},{... | collective-permute-start | bytes 196616 | tf_op jit(solution)/shard_map/ppermute | solution.py:39
  26.8 3.1 %collective-permute-done.8.refs_1_ = bf16[2,128,128]{2,1,0:T(8,128)(2,1)S(1)} collective-permute-done((bf16[2,128,128]{2,1,0:T(8,128)(2,1)S(1)}, bf16[2,128,128]{2,1,0:T(8,128)(2,1)S(1)}, u32[]{:S(2)}, u32[]{:S(2)}) %collective-permute-start.8) | collective-permute-done | bytes 65568 | tf_op jit(solution)/shard_map/ppermute | solution.py:39
  29.9 2.7 %collective-permute-done.9.refs_2_ = bf16[2,128,128]{2,1,0:T(8,128)(2,1)S(1)} collective-permute-done((bf16[2,128,128]{2,1,0:T(8,128)(2,1)S(1)}, bf16[2,128,128]{2,1,0:T(8,128)(2,1)S(1)}, u32[]{:S(2)}, u32[]{:S(2)}) %collective-permute-start.9) | collective-permute-done | bytes 65568 | tf_op jit(solution)/shard_map/ppermute | solution.py:39
  32.9 1.9 %collective-permute-start.12 = (bf16[256,128]{1,0:T(8,128)(2,1)S(1)}, bf16[256,128]{1,0:T(8,128)(2,1)S(1)}, u32[]{:S(2)}, u32[]{:S(2)}) collective-permute-start(bf16[256,128]{1,0:T(8,128)(2,1)S(1)} %shard_map.68.refs_0_), channel_id=1, source_target_pairs={{0,24},{4,28},{8,16},{12,20},{16,8},{20,12},{24,0},{28,4},{1,25},{... | collective-permute-start | bytes 196616 | tf_op jit(solution)/shard_map/ppermute | solution.py:20
  34.8 1.0 %collective-permute-start.11 = (bf16[256,128]{1,0:T(8,128)(2,1)S(1)}, bf16[256,128]{1,0:T(8,128)(2,1)S(1)}, u32[]{:S(2)}, u32[]{:S(2)}) collective-permute-start(bf16[256,128]{1,0:T(8,128)(2,1)S(1)} %shard_map.68.refs_0_), channel_id=1, source_target_pairs={{0,16},{4,20},{8,24},{12,28},{16,0},{20,4},{24,8},{28,12},{1,17},{... | collective-permute-start | bytes 196616 | tf_op jit(solution)/shard_map/ppermute | solution.py:20
  35.8 2.0 %collective-permute-start.13 = (bf16[256,128]{1,0:T(8,128)(2,1)S(1)}, bf16[256,128]{1,0:T(8,128)(2,1)S(1)}, u32[]{:S(2)}, u32[]{:S(2)}) collective-permute-start(bf16[256,128]{1,0:T(8,128)(2,1)S(1)} %shard_map.68.refs_0_), channel_id=1, source_target_pairs={{0,4},{4,0},{8,12},{12,8},{16,20},{20,16},{24,28},{28,24},{1,5},{5... | collective-permute-start | bytes 196616 | tf_op jit(solution)/shard_map/ppermute | solution.py:20
  38.4 0.7 collective-permute-done.12.refs_3_
  39.1 0.8 collective-permute-start.16
  40.5 1.2 %collective-permute-start.15 = (bf16[256,128]{1,0:T(8,128)(2,1)S(1)}, bf16[256,128]{1,0:T(8,128)(2,1)S(1)}, u32[]{:S(2)}, u32[]{:S(2)}) collective-permute-start(bf16[256,128]{1,0:T(8,128)(2,1)S(1)} %collective-permute-done.11.refs_2_), channel_id=1, source_target_pairs={{0,4},{4,0},{8,12},{12,8},{16,20},{20,16},{24,28},{28,24},{1,5},{5... | collective-permute-start | bytes 196616 | tf_op jit(solution)/shard_map/ppermute | solution.py:20
  41.7 0.9 %collective-permute-done.10.refs_1_ = bf16[256,128]{1,0:T(8,128)(2,1)S(1)} collective-permute-done((bf16[256,128]{1,0:T(8,128)(2,1)S(1)}, bf16[256,128]{1,0:T(8,128)(2,1)S(1)}, u32[]{:S(2)}, u32[]{:S(2)}) %collective-permute-start.10) | collective-permute-done | bytes 65568 | tf_op jit(solution)/shard_map/ppermute | solution.py:20
  42.7 0.7 collective-permute-done.16.refs_7_
  43.3 1.4 %collective-permute-done.15.refs_6_ = bf16[256,128]{1,0:T(8,128)(2,1)S(1)} collective-permute-done((bf16[256,128]{1,0:T(8,128)(2,1)S(1)}, bf16[256,128]{1,0:T(8,128)(2,1)S(1)}, u32[]{:S(2)}, u32[]{:S(2)}) %collective-permute-start.15) | collective-permute-done | bytes 65568 | tf_op jit(solution)/shard_map/ppermute | solution.py:20
  44.9 1.9 %collective-permute-done.18.other = bf16[2048,128]{1,0:T(8,128)(2,1)S(1)} collective-permute-done((bf16[2048,128]{1,0:T(8,128)(2,1)S(1)}, bf16[2048,128]{1,0:T(8,128)(2,1)S(1)}, u32[]{:S(2)}, u32[]{:S(2)}) %collective-permute-start.18) | collective-permute-done | bytes 524320 | tf_op jit(solution)/shard_map/ppermute | solution.py:20
  46.8 1.4 %shard_map.70 = (bf16[4,128,128]{2,1,0:T(8,128)(2,1)S(1)}, bf16[4,128,128]{2,1,0:T(8,128)(2,1)S(1)}, bf16[4,128,128]{2,1,0:T(8,128)(2,1)S(1)}, bf16[4,128,128]{2...) custom-call(bf16[32,128,128]{2,1,0:T(8,128)(2,1)S(1)} %bitcast.10, ...), custom_call_target="tpu_custom_call" | custom-call | tf_op jit(solution)/shard_map/pallas_call | solution.py:55
  48.2 1.6 %collective-permute-start.20 = (bf16[4,128,128]{2,1,0:T(8,128)(2,1)S(1)}, bf16[4,128,128]{2,1,0:T(8,128)(2,1)S(1)}, u32[]{:S(2)}, u32[]{:S(2)}) collective-permute-start(bf16[4,128,128]{2,1,0:T(8,128)(2,1)S(1)} %get-tuple-element.52), channel_id=1, source_target_pairs={{0,2},{1,5},{2,0},{3,7},{4,6},{5,1},{6,4},{7,3},{8,10},{9,13},{10,... | collective-permute-start | bytes 393224 | tf_op jit(solution)/shard_map/ppermute | solution.py:34
  49.8 1.1 %collective-permute-start.23 = (bf16[4,128,128]{2,1,0:T(8,128)(2,1)S(1)}, bf16[4,128,128]{2,1,0:T(8,128)(2,1)S(1)}, u32[]{:S(2)}, u32[]{:S(2)}) collective-permute-start(bf16[4,128,128]{2,1,0:T(8,128)(2,1)S(1)} %get-tuple-element.56), channel_id=1, source_target_pairs={{0,4},{1,3},{2,6},{3,1},{4,0},{5,7},{6,2},{7,5},{8,12},{9,11},{10,... | collective-permute-start | bytes 393224 | tf_op jit(solution)/shard_map/ppermute | solution.py:34
  51.5 0.8 collective-permute-start.22
  52.3 2.2 %collective-permute-done.20.came = bf16[4,128,128]{2,1,0:T(8,128)(2,1)S(1)} collective-permute-done((bf16[4,128,128]{2,1,0:T(8,128)(2,1)S(1)}, bf16[4,128,128]{2,1,0:T(8,128)(2,1)S(1)}, u32[]{:S(2)}, u32[]{:S(2)}) %collective-permute-start.20) | collective-permute-done | bytes 131104 | tf_op jit(solution)/shard_map/ppermute | solution.py:34
  54.5 1.4 %collective-permute-start.21 = (bf16[4,128,128]{2,1,0:T(8,128)(2,1)S(1)}, bf16[4,128,128]{2,1,0:T(8,128)(2,1)S(1)}, u32[]{:S(2)}, u32[]{:S(2)}) collective-permute-start(bf16[4,128,128]{2,1,0:T(8,128)(2,1)S(1)} %shard_map.71), channel_id=1, source_target_pairs={{0,4},{1,3},{2,6},{3,1},{4,0},{5,7},{6,2},{7,5},{8,12},{9,11},{10,... | collective-permute-start | bytes 393224 | tf_op jit(solution)/shard_map/ppermute | solution.py:34
  56.0 1.5 %collective-permute-start.24 = (bf16[4,128,128]{2,1,0:T(8,128)(2,1)S(1)}, bf16[4,128,128]{2,1,0:T(8,128)(2,1)S(1)}, u32[]{:S(2)}, u32[]{:S(2)}) collective-permute-start(bf16[4,128,128]{2,1,0:T(8,128)(2,1)S(1)} %shard_map.72), channel_id=1, source_target_pairs={{0,2},{1,5},{2,0},{3,7},{4,6},{5,1},{6,4},{7,3},{8,10},{9,13},{10,... | collective-permute-start | bytes 393224 | tf_op jit(solution)/shard_map/ppermute | solution.py:34
  57.5 2.7 %collective-permute-done.21.refs_2_ = bf16[4,128,128]{2,1,0:T(8,128)(2,1)S(1)} collective-permute-done((bf16[4,128,128]{2,1,0:T(8,128)(2,1)S(1)}, bf16[4,128,128]{2,1,0:T(8,128)(2,1)S(1)}, u32[]{:S(2)}, u32[]{:S(2)}) %collective-permute-start.21) | collective-permute-done | bytes 131104 | tf_op jit(solution)/shard_map/ppermute | solution.py:34
  60.3 0.8 collective-permute-done.24.refs_5_
  61.1 1.7 %collective-permute-start.25 = (bf16[2,128,128]{2,1,0:T(8,128)(2,1)S(1)}, bf16[2,128,128]{2,1,0:T(8,128)(2,1)S(1)}, u32[]{:S(2)}, u32[]{:S(2)}) collective-permute-start(bf16[2,128,128]{2,1,0:T(8,128)(2,1)S(1)} %get-tuple-element.58), channel_id=1, source_target_pairs={{0,8},{1,25},{4,12},{5,29},{8,0},{9,17},{12,4},{13,21},{16,24},{17... | collective-permute-start | bytes 196616 | tf_op jit(solution)/shard_map/ppermute | solution.py:39
  63.4 2.2 %collective-permute-start.27 = (bf16[2,128,128]{2,1,0:T(8,128)(2,1)S(1)}, bf16[2,128,128]{2,1,0:T(8,128)(2,1)S(1)}, u32[]{:S(2)}, u32[]{:S(2)}) collective-permute-start(bf16[2,128,128]{2,1,0:T(8,128)(2,1)S(1)} %get-tuple-element.60), channel_id=1, source_target_pairs={{0,24},{1,9},{4,28},{5,13},{8,16},{9,1},{12,20},{13,5},{16,8},{17,... | collective-permute-start | bytes 196616 | tf_op jit(solution)/shard_map/ppermute | solution.py:39
  65.6 1.5 %collective-permute-done.25.refs_0_ = bf16[2,128,128]{2,1,0:T(8,128)(2,1)S(1)} collective-permute-done((bf16[2,128,128]{2,1,0:T(8,128)(2,1)S(1)}, bf16[2,128,128]{2,1,0:T(8,128)(2,1)S(1)}, u32[]{:S(2)}, u32[]{:S(2)}) %collective-permute-start.25) | collective-permute-done | bytes 65568 | tf_op jit(solution)/shard_map/ppermute | solution.py:39
  67.1 1.5 %collective-permute-done.26.refs_1_ = bf16[2,128,128]{2,1,0:T(8,128)(2,1)S(1)} collective-permute-done((bf16[2,128,128]{2,1,0:T(8,128)(2,1)S(1)}, bf16[2,128,128]{2,1,0:T(8,128)(2,1)S(1)}, u32[]{:S(2)}, u32[]{:S(2)}) %collective-permute-start.26) | collective-permute-done | bytes 65568 | tf_op jit(solution)/shard_map/ppermute | solution.py:39
  68.6 0.9 %collective-permute-done.27.refs_2_ = bf16[2,128,128]{2,1,0:T(8,128)(2,1)S(1)} collective-permute-done((bf16[2,128,128]{2,1,0:T(8,128)(2,1)S(1)}, bf16[2,128,128]{2,1,0:T(8,128)(2,1)S(1)}, u32[]{:S(2)}, u32[]{:S(2)}) %collective-permute-start.27) | collective-permute-done | bytes 65568 | tf_op jit(solution)/shard_map/ppermute | solution.py:39
  69.7 2.2 %collective-permute-start.30 = (bf16[256,128]{1,0:T(8,128)(2,1)S(1)}, bf16[256,128]{1,0:T(8,128)(2,1)S(1)}, u32[]{:S(2)}, u32[]{:S(2)}) collective-permute-start(bf16[256,128]{1,0:T(8,128)(2,1)S(1)} %shard_map.74.refs_0_), channel_id=1, source_target_pairs={{0,24},{4,28},{8,16},{12,20},{16,8},{20,12},{24,0},{28,4},{1,25},{... | collective-permute-start | bytes 196616 | tf_op jit(solution)/shard_map/ppermute | solution.py:20
  72.2 2.6 %collective-permute-start.32 = (bf16[256,128]{1,0:T(8,128)(2,1)S(1)}, bf16[256,128]{1,0:T(8,128)(2,1)S(1)}, u32[]{:S(2)}, u32[]{:S(2)}) collective-permute-start(bf16[256,128]{1,0:T(8,128)(2,1)S(1)} %shard_map.74.refs_0_), channel_id=1, source_target_pairs={{0,12},{4,8},{8,4},{12,0},{16,28},{20,24},{24,20},{28,16},{1,13},{... | collective-permute-start | bytes 196616 | tf_op jit(solution)/shard_map/ppermute | solution.py:20
  74.9 0.7 collective-permute-start.31
  75.7 0.7 collective-permute-done.30.refs_3_
  76.4 1.3 %collective-permute-start.34 = (bf16[256,128]{1,0:T(8,128)(2,1)S(1)}, bf16[256,128]{1,0:T(8,128)(2,1)S(1)}, u32[]{:S(2)}, u32[]{:S(2)}) collective-permute-start(bf16[256,128]{1,0:T(8,128)(2,1)S(1)} %collective-permute-done.30.refs_3_), channel_id=1, source_target_pairs={{0,4},{4,0},{8,12},{12,8},{16,20},{20,16},{24,28},{28,24},{1,5},{5... | collective-permute-start | bytes 196616 | tf_op jit(solution)/shard_map/ppermute | solution.py:20
  77.8 1.1 %collective-permute-start.33 = (bf16[256,128]{1,0:T(8,128)(2,1)S(1)}, bf16[256,128]{1,0:T(8,128)(2,1)S(1)}, u32[]{:S(2)}, u32[]{:S(2)}) collective-permute-start(bf16[256,128]{1,0:T(8,128)(2,1)S(1)} %collective-permute-done.29.refs_2_), channel_id=1, source_target_pairs={{0,4},{4,0},{8,12},{12,8},{16,20},{20,16},{24,28},{28,24},{1,5},{5... | collective-permute-start | bytes 196616 | tf_op jit(solution)/shard_map/ppermute | solution.py:20
  79.1 0.7 collective-permute-done.28.refs_1_
  79.9 0.8 collective-permute-done.34.refs_7_
  80.7 1.4 %collective-permute-done.33.refs_6_ = bf16[256,128]{1,0:T(8,128)(2,1)S(1)} collective-permute-done((bf16[256,128]{1,0:T(8,128)(2,1)S(1)}, bf16[256,128]{1,0:T(8,128)(2,1)S(1)}, u32[]{:S(2)}, u32[]{:S(2)}) %collective-permute-start.33) | collective-permute-done | bytes 65568 | tf_op jit(solution)/shard_map/ppermute | solution.py:20
  82.1 1.0 %shard_map.75 = bf16[2,1,2048,128]{3,2,1,0:T(8,128)(2,1)} custom-call(bf16[1,2048,128]{2,1,0:T(8,128)(2,1)S(1)} %bitcast.11, bf16[256,128]{1,0:T(8,128)(2,1)S(1)} %shard_map.74.refs_0_, bf16[256,128]{1,0:T(8,128)(2,1)S(1)} %collective-permute-done.28.refs_1_, bf16[256,128]{1,0:T(8,128)(2,1)S(1)} %collective-permute-done.29.refs_2_, ...), custom_call_target="tpu_custom_call" | custom-call | tf_op jit(solution)/shard_map/pallas_call | solution.py:55
  (42 shorter events, 5.8 us)
Async XLA Ops:
  0.7 0.7 copy-start.3
  3.6 17.4 %collective-permute-start.6 = (bf16[2048,128]{1,0:T(8,128)(2,1)S(1)}, bf16[2048,128]{1,0:T(8,128)(2,1)S(1)}, u32[]{:S(2)}, u32[]{:S(2)}) collective-permute-start(bf16[2048,128]{1,0:T(8,128)(2,1)S(1)} %get-tuple-element.41.refs_6_), channel_id=1, source_target_pairs={{4,12},{12,20},{20,28},{5,13},{13,21},{21,29},{6,14},{14,22},{22,3... | collective-permute-start | bytes 1572872 | tf_op jit(solution)/shard_map/ppermute | solution.py:299
  4.3 7.9 %collective-permute-start.1 = (bf16[4,128,128]{2,1,0:T(8,128)(2,1)S(1)}, bf16[4,128,128]{2,1,0:T(8,128)(2,1)S(1)}, u32[]{:S(2)}, u32[]{:S(2)}) collective-permute-start(bf16[4,128,128]{2,1,0:T(8,128)(2,1)S(1)} %get-tuple-element.36), channel_id=1, source_target_pairs={{0,2},{1,5},{2,0},{3,7},{4,6},{5,1},{6,4},{7,3},{8,10},{9,13},{10,... | collective-permute-start | bytes 393224 | tf_op jit(solution)/shard_map/ppermute | solution.py:34
  7.3 8.6 %collective-permute-start.4 = (bf16[4,128,128]{2,1,0:T(8,128)(2,1)S(1)}, bf16[4,128,128]{2,1,0:T(8,128)(2,1)S(1)}, u32[]{:S(2)}, u32[]{:S(2)}) collective-permute-start(bf16[4,128,128]{2,1,0:T(8,128)(2,1)S(1)} %get-tuple-element.40), channel_id=1, source_target_pairs={{0,4},{1,3},{2,6},{3,1},{4,0},{5,7},{6,2},{7,5},{8,12},{9,11},{10,... | collective-permute-start | bytes 393224 | tf_op jit(solution)/shard_map/ppermute | solution.py:34
  11.6 6.4 %collective-permute-start = (bf16[4,128,128]{2,1,0:T(8,128)(2,1)S(1)}, bf16[4,128,128]{2,1,0:T(8,128)(2,1)S(1)}, u32[]{:S(2)}, u32[]{:S(2)}) collective-permute-start(bf16[4,128,128]{2,1,0:T(8,128)(2,1)S(1)} %get-tuple-element.34), channel_id=1, source_target_pairs={{0,2},{1,5},{2,0},{3,7},{4,6},{5,1},{6,4},{7,3},{8,10},{9,13},{10,... | collective-permute-start | bytes 393224 | tf_op jit(solution)/shard_map/ppermute | solution.py:34
  12.1 6.4 %collective-permute-start.3 = (bf16[4,128,128]{2,1,0:T(8,128)(2,1)S(1)}, bf16[4,128,128]{2,1,0:T(8,128)(2,1)S(1)}, u32[]{:S(2)}, u32[]{:S(2)}) collective-permute-start(bf16[4,128,128]{2,1,0:T(8,128)(2,1)S(1)} %get-tuple-element.38), channel_id=1, source_target_pairs={{0,4},{1,3},{2,6},{3,1},{4,0},{5,7},{6,2},{7,5},{8,12},{9,11},{10,... | collective-permute-start | bytes 393224 | tf_op jit(solution)/shard_map/ppermute | solution.py:34
  12.2 8.0 %collective-permute-start.2 = (bf16[4,128,128]{2,1,0:T(8,128)(2,1)S(1)}, bf16[4,128,128]{2,1,0:T(8,128)(2,1)S(1)}, u32[]{:S(2)}, u32[]{:S(2)}) collective-permute-start(bf16[4,128,128]{2,1,0:T(8,128)(2,1)S(1)} %shard_map.65), channel_id=1, source_target_pairs={{0,4},{1,3},{2,6},{3,1},{4,0},{5,7},{6,2},{7,5},{8,12},{9,11},{10,... | collective-permute-start | bytes 393224 | tf_op jit(solution)/shard_map/ppermute | solution.py:34
  15.9 16.7 %copy-start.1 = (bf16[2,1,2048,128]{3,2,1,0:T(8,128)(2,1)S(1)}, bf16[2,1,2048,128]{3,2,1,0:T(8,128)(2,1)}, u32[]{:S(2)}) copy-start(bf16[2,1,2048,128]{3,2,1,0:T(8,128)(2,1)} %refs_3_.3) | copy-start | bytes 3145732
  16.0 5.0 %collective-permute-start.5 = (bf16[4,128,128]{2,1,0:T(8,128)(2,1)S(1)}, bf16[4,128,128]{2,1,0:T(8,128)(2,1)S(1)}, u32[]{:S(2)}, u32[]{:S(2)}) collective-permute-start(bf16[4,128,128]{2,1,0:T(8,128)(2,1)S(1)} %shard_map.66), channel_id=1, source_target_pairs={{0,2},{1,5},{2,0},{3,7},{4,6},{5,1},{6,4},{7,3},{8,10},{9,13},{10,... | collective-permute-start | bytes 393224 | tf_op jit(solution)/shard_map/ppermute | solution.py:34
  21.0 11.6 %copy-start.2 = (bf16[1,16,128,128]{3,2,1,0:T(8,128)(2,1)S(1)}, bf16[1,16,128,128]{3,2,1,0:T(8,128)(2,1)}, u32[]{:S(2)}) copy-start(bf16[1,16,128,128]{3,2,1,0:T(8,128)(2,1)} %refs_4_.3) | copy-start | bytes 1572868
  21.2 23.6 %collective-permute-start.17 = (bf16[2048,128]{1,0:T(8,128)(2,1)S(1)}, bf16[2048,128]{1,0:T(8,128)(2,1)S(1)}, u32[]{:S(2)}, u32[]{:S(2)}) collective-permute-start(bf16[2048,128]{1,0:T(8,128)(2,1)S(1)} %get-tuple-element.46), channel_id=1, source_target_pairs={{0,4},{4,0},{8,12},{12,8},{16,20},{20,16},{24,28},{28,24},{1,5},{5... | collective-permute-start | bytes 1572872 | tf_op jit(solution)/shard_map/ppermute | solution.py:20
  21.9 4.9 %collective-permute-start.7 = (bf16[2,128,128]{2,1,0:T(8,128)(2,1)S(1)}, bf16[2,128,128]{2,1,0:T(8,128)(2,1)S(1)}, u32[]{:S(2)}, u32[]{:S(2)}) collective-permute-start(bf16[2,128,128]{2,1,0:T(8,128)(2,1)S(1)} %get-tuple-element.43), channel_id=1, source_target_pairs={{0,8},{1,25},{4,12},{5,29},{8,0},{9,17},{12,4},{13,21},{16,24},{17... | collective-permute-start | bytes 196616 | tf_op jit(solution)/shard_map/ppermute | solution.py:39
  23.9 6.0 %collective-permute-start.8 = (bf16[2,128,128]{2,1,0:T(8,128)(2,1)S(1)}, bf16[2,128,128]{2,1,0:T(8,128)(2,1)S(1)}, u32[]{:S(2)}, u32[]{:S(2)}) collective-permute-start(bf16[2,128,128]{2,1,0:T(8,128)(2,1)S(1)} %get-tuple-element.44), channel_id=1, source_target_pairs={{0,16},{1,17},{4,20},{5,21},{8,24},{9,25},{12,28},{13,29},{16,0},{... | collective-permute-start | bytes 196616 | tf_op jit(solution)/shard_map/ppermute | solution.py:39
  26.4 6.1 %collective-permute-start.9 = (bf16[2,128,128]{2,1,0:T(8,128)(2,1)S(1)}, bf16[2,128,128]{2,1,0:T(8,128)(2,1)S(1)}, u32[]{:S(2)}, u32[]{:S(2)}) collective-permute-start(bf16[2,128,128]{2,1,0:T(8,128)(2,1)S(1)} %get-tuple-element.45), channel_id=1, source_target_pairs={{0,24},{1,9},{4,28},{5,13},{8,16},{9,1},{12,20},{13,5},{16,8},{17,... | collective-permute-start | bytes 196616 | tf_op jit(solution)/shard_map/ppermute | solution.py:39
  32.6 14.2 %copy-start = (bf16[1,1,1,32,128,128]{5,4,3,2,1,0:T(8,128)(2,1)S(1)}, bf16[1,1,1,32,128,128]{5,4,3,2,1,0:T(8,128)(2,1)}, u32[]{:S(2)}) copy-start(bf16[1,1,1,32,128,128]{5,4,3,2,1,0:T(8,128)(2,1)} %param.6) | copy-start | bytes 3145732
  32.8 5.6 %collective-permute-start.14 = (bf16[256,128]{1,0:T(8,128)(2,1)S(1)}, bf16[256,128]{1,0:T(8,128)(2,1)S(1)}, u32[]{:S(2)}, u32[]{:S(2)}) collective-permute-start(bf16[256,128]{1,0:T(8,128)(2,1)S(1)} %shard_map.68.refs_0_), channel_id=1, source_target_pairs={{0,12},{4,8},{8,4},{12,0},{16,28},{20,24},{24,20},{28,16},{1,13},{... | collective-permute-start | bytes 196616 | tf_op jit(solution)/shard_map/ppermute | solution.py:20
  32.9 6.2 %collective-permute-start.12 = (bf16[256,128]{1,0:T(8,128)(2,1)S(1)}, bf16[256,128]{1,0:T(8,128)(2,1)S(1)}, u32[]{:S(2)}, u32[]{:S(2)}) collective-permute-start(bf16[256,128]{1,0:T(8,128)(2,1)S(1)} %shard_map.68.refs_0_), channel_id=1, source_target_pairs={{0,24},{4,28},{8,16},{12,20},{16,8},{20,12},{24,0},{28,4},{1,25},{... | collective-permute-start | bytes 196616 | tf_op jit(solution)/shard_map/ppermute | solution.py:20
  34.8 5.7 %collective-permute-start.11 = (bf16[256,128]{1,0:T(8,128)(2,1)S(1)}, bf16[256,128]{1,0:T(8,128)(2,1)S(1)}, u32[]{:S(2)}, u32[]{:S(2)}) collective-permute-start(bf16[256,128]{1,0:T(8,128)(2,1)S(1)} %shard_map.68.refs_0_), channel_id=1, source_target_pairs={{0,16},{4,20},{8,24},{12,28},{16,0},{20,4},{24,8},{28,12},{1,17},{... | collective-permute-start | bytes 196616 | tf_op jit(solution)/shard_map/ppermute | solution.py:20
  35.8 6.0 %collective-permute-start.13 = (bf16[256,128]{1,0:T(8,128)(2,1)S(1)}, bf16[256,128]{1,0:T(8,128)(2,1)S(1)}, u32[]{:S(2)}, u32[]{:S(2)}) collective-permute-start(bf16[256,128]{1,0:T(8,128)(2,1)S(1)} %shard_map.68.refs_0_), channel_id=1, source_target_pairs={{0,4},{4,0},{8,12},{12,8},{16,20},{20,16},{24,28},{28,24},{1,5},{5... | collective-permute-start | bytes 196616 | tf_op jit(solution)/shard_map/ppermute | solution.py:20
  38.4 4.3 %collective-permute-start.10 = (bf16[256,128]{1,0:T(8,128)(2,1)S(1)}, bf16[256,128]{1,0:T(8,128)(2,1)S(1)}, u32[]{:S(2)}, u32[]{:S(2)}) collective-permute-start(bf16[256,128]{1,0:T(8,128)(2,1)S(1)} %shard_map.68.refs_0_), channel_id=1, source_target_pairs={{0,8},{4,12},{8,0},{12,4},{16,24},{20,28},{24,16},{28,20},{1,9},{5... | collective-permute-start | bytes 196616 | tf_op jit(solution)/shard_map/ppermute | solution.py:20
  39.1 4.3 %collective-permute-start.16 = (bf16[256,128]{1,0:T(8,128)(2,1)S(1)}, bf16[256,128]{1,0:T(8,128)(2,1)S(1)}, u32[]{:S(2)}, u32[]{:S(2)}) collective-permute-start(bf16[256,128]{1,0:T(8,128)(2,1)S(1)} %collective-permute-done.12.refs_3_), channel_id=1, source_target_pairs={{0,4},{4,0},{8,12},{12,8},{16,20},{20,16},{24,28},{28,24},{1,5},{5... | collective-permute-start | bytes 196616 | tf_op jit(solution)/shard_map/ppermute | solution.py:20
  40.5 4.3 %collective-permute-start.15 = (bf16[256,128]{1,0:T(8,128)(2,1)S(1)}, bf16[256,128]{1,0:T(8,128)(2,1)S(1)}, u32[]{:S(2)}, u32[]{:S(2)}) collective-permute-start(bf16[256,128]{1,0:T(8,128)(2,1)S(1)} %collective-permute-done.11.refs_2_), channel_id=1, source_target_pairs={{0,4},{4,0},{8,12},{12,8},{16,20},{20,16},{24,28},{28,24},{1,5},{5... | collective-permute-start | bytes 196616 | tf_op jit(solution)/shard_map/ppermute | solution.py:20
  44.8 2.0 %collective-permute-start.18 = (bf16[2048,128]{1,0:T(8,128)(2,1)S(1)}, bf16[2048,128]{1,0:T(8,128)(2,1)S(1)}, u32[]{:S(2)}, u32[]{:S(2)}) collective-permute-start(bf16[2048,128]{1,0:T(8,128)(2,1)S(1)} %get-tuple-element.48.own), channel_id=1, source_target_pairs={{0,1},{1,0},{2,3},{3,2},{4,5},{5,4},{6,7},{7,6},{8,9},{9,8},{10,11... | collective-permute-start | bytes 1572872 | tf_op jit(solution)/shard_map/ppermute | solution.py:20
  48.2 6.3 %collective-permute-start.20 = (bf16[4,128,128]{2,1,0:T(8,128)(2,1)S(1)}, bf16[4,128,128]{2,1,0:T(8,128)(2,1)S(1)}, u32[]{:S(2)}, u32[]{:S(2)}) collective-permute-start(bf16[4,128,128]{2,1,0:T(8,128)(2,1)S(1)} %get-tuple-element.52), channel_id=1, source_target_pairs={{0,2},{1,5},{2,0},{3,7},{4,6},{5,1},{6,4},{7,3},{8,10},{9,13},{10,... | collective-permute-start | bytes 393224 | tf_op jit(solution)/shard_map/ppermute | solution.py:34
  49.8 6.1 %collective-permute-start.23 = (bf16[4,128,128]{2,1,0:T(8,128)(2,1)S(1)}, bf16[4,128,128]{2,1,0:T(8,128)(2,1)S(1)}, u32[]{:S(2)}, u32[]{:S(2)}) collective-permute-start(bf16[4,128,128]{2,1,0:T(8,128)(2,1)S(1)} %get-tuple-element.56), channel_id=1, source_target_pairs={{0,4},{1,3},{2,6},{3,1},{4,0},{5,7},{6,2},{7,5},{8,12},{9,11},{10,... | collective-permute-start | bytes 393224 | tf_op jit(solution)/shard_map/ppermute | solution.py:34
  51.0 6.6 %collective-permute-start.19 = (bf16[4,128,128]{2,1,0:T(8,128)(2,1)S(1)}, bf16[4,128,128]{2,1,0:T(8,128)(2,1)S(1)}, u32[]{:S(2)}, u32[]{:S(2)}) collective-permute-start(bf16[4,128,128]{2,1,0:T(8,128)(2,1)S(1)} %get-tuple-element.50), channel_id=1, source_target_pairs={{0,2},{1,5},{2,0},{3,7},{4,6},{5,1},{6,4},{7,3},{8,10},{9,13},{10,... | collective-permute-start | bytes 393224 | tf_op jit(solution)/shard_map/ppermute | solution.py:34
  51.5 6.0 %collective-permute-start.22 = (bf16[4,128,128]{2,1,0:T(8,128)(2,1)S(1)}, bf16[4,128,128]{2,1,0:T(8,128)(2,1)S(1)}, u32[]{:S(2)}, u32[]{:S(2)}) collective-permute-start(bf16[4,128,128]{2,1,0:T(8,128)(2,1)S(1)} %get-tuple-element.54), channel_id=1, source_target_pairs={{0,4},{1,3},{2,6},{3,1},{4,0},{5,7},{6,2},{7,5},{8,12},{9,11},{10,... | collective-permute-start | bytes 393224 | tf_op jit(solution)/shard_map/ppermute | solution.py:34
  54.5 5.7 %collective-permute-start.21 = (bf16[4,128,128]{2,1,0:T(8,128)(2,1)S(1)}, bf16[4,128,128]{2,1,0:T(8,128)(2,1)S(1)}, u32[]{:S(2)}, u32[]{:S(2)}) collective-permute-start(bf16[4,128,128]{2,1,0:T(8,128)(2,1)S(1)} %shard_map.71), channel_id=1, source_target_pairs={{0,4},{1,3},{2,6},{3,1},{4,0},{5,7},{6,2},{7,5},{8,12},{9,11},{10,... | collective-permute-start | bytes 393224 | tf_op jit(solution)/shard_map/ppermute | solution.py:34
  56.0 5.0 %collective-permute-start.24 = (bf16[4,128,128]{2,1,0:T(8,128)(2,1)S(1)}, bf16[4,128,128]{2,1,0:T(8,128)(2,1)S(1)}, u32[]{:S(2)}, u32[]{:S(2)}) collective-permute-start(bf16[4,128,128]{2,1,0:T(8,128)(2,1)S(1)} %shard_map.72), channel_id=1, source_target_pairs={{0,2},{1,5},{2,0},{3,7},{4,6},{5,1},{6,4},{7,3},{8,10},{9,13},{10,... | collective-permute-start | bytes 393224 | tf_op jit(solution)/shard_map/ppermute | solution.py:34
  61.1 6.0 %collective-permute-start.25 = (bf16[2,128,128]{2,1,0:T(8,128)(2,1)S(1)}, bf16[2,128,128]{2,1,0:T(8,128)(2,1)S(1)}, u32[]{:S(2)}, u32[]{:S(2)}) collective-permute-start(bf16[2,128,128]{2,1,0:T(8,128)(2,1)S(1)} %get-tuple-element.58), channel_id=1, source_target_pairs={{0,8},{1,25},{4,12},{5,29},{8,0},{9,17},{12,4},{13,21},{16,24},{17... | collective-permute-start | bytes 196616 | tf_op jit(solution)/shard_map/ppermute | solution.py:39
  62.9 5.7 %collective-permute-start.26 = (bf16[2,128,128]{2,1,0:T(8,128)(2,1)S(1)}, bf16[2,128,128]{2,1,0:T(8,128)(2,1)S(1)}, u32[]{:S(2)}, u32[]{:S(2)}) collective-permute-start(bf16[2,128,128]{2,1,0:T(8,128)(2,1)S(1)} %get-tuple-element.59), channel_id=1, source_target_pairs={{0,16},{1,17},{4,20},{5,21},{8,24},{9,25},{12,28},{13,29},{16,0},{... | collective-permute-start | bytes 196616 | tf_op jit(solution)/shard_map/ppermute | solution.py:39
  63.4 6.2 %collective-permute-start.27 = (bf16[2,128,128]{2,1,0:T(8,128)(2,1)S(1)}, bf16[2,128,128]{2,1,0:T(8,128)(2,1)S(1)}, u32[]{:S(2)}, u32[]{:S(2)}) collective-permute-start(bf16[2,128,128]{2,1,0:T(8,128)(2,1)S(1)} %get-tuple-element.60), channel_id=1, source_target_pairs={{0,24},{1,9},{4,28},{5,13},{8,16},{9,1},{12,20},{13,5},{16,8},{17,... | collective-permute-start | bytes 196616 | tf_op jit(solution)/shard_map/ppermute | solution.py:39
  69.7 6.7 %collective-permute-start.30 = (bf16[256,128]{1,0:T(8,128)(2,1)S(1)}, bf16[256,128]{1,0:T(8,128)(2,1)S(1)}, u32[]{:S(2)}, u32[]{:S(2)}) collective-permute-start(bf16[256,128]{1,0:T(8,128)(2,1)S(1)} %shard_map.74.refs_0_), channel_id=1, source_target_pairs={{0,24},{4,28},{8,16},{12,20},{16,8},{20,12},{24,0},{28,4},{1,25},{... | collective-permute-start | bytes 196616 | tf_op jit(solution)/shard_map/ppermute | solution.py:20
  71.9 5.9 %collective-permute-start.29 = (bf16[256,128]{1,0:T(8,128)(2,1)S(1)}, bf16[256,128]{1,0:T(8,128)(2,1)S(1)}, u32[]{:S(2)}, u32[]{:S(2)}) collective-permute-start(bf16[256,128]{1,0:T(8,128)(2,1)S(1)} %shard_map.74.refs_0_), channel_id=1, source_target_pairs={{0,16},{4,20},{8,24},{12,28},{16,0},{20,4},{24,8},{28,12},{1,17},{... | collective-permute-start | bytes 196616 | tf_op jit(solution)/shard_map/ppermute | solution.py:20
  72.2 6.6 %collective-permute-start.32 = (bf16[256,128]{1,0:T(8,128)(2,1)S(1)}, bf16[256,128]{1,0:T(8,128)(2,1)S(1)}, u32[]{:S(2)}, u32[]{:S(2)}) collective-permute-start(bf16[256,128]{1,0:T(8,128)(2,1)S(1)} %shard_map.74.refs_0_), channel_id=1, source_target_pairs={{0,12},{4,8},{8,4},{12,0},{16,28},{20,24},{24,20},{28,16},{1,13},{... | collective-permute-start | bytes 196616 | tf_op jit(solution)/shard_map/ppermute | solution.py:20
  74.9 4.3 %collective-permute-start.31 = (bf16[256,128]{1,0:T(8,128)(2,1)S(1)}, bf16[256,128]{1,0:T(8,128)(2,1)S(1)}, u32[]{:S(2)}, u32[]{:S(2)}) collective-permute-start(bf16[256,128]{1,0:T(8,128)(2,1)S(1)} %shard_map.74.refs_0_), channel_id=1, source_target_pairs={{0,4},{4,0},{8,12},{12,8},{16,20},{20,16},{24,28},{28,24},{1,5},{5... | collective-permute-start | bytes 196616 | tf_op jit(solution)/shard_map/ppermute | solution.py:20
  75.6 4.3 %collective-permute-start.28 = (bf16[256,128]{1,0:T(8,128)(2,1)S(1)}, bf16[256,128]{1,0:T(8,128)(2,1)S(1)}, u32[]{:S(2)}, u32[]{:S(2)}) collective-permute-start(bf16[256,128]{1,0:T(8,128)(2,1)S(1)} %shard_map.74.refs_0_), channel_id=1, source_target_pairs={{0,8},{4,12},{8,0},{12,4},{16,24},{20,28},{24,16},{28,20},{1,9},{5... | collective-permute-start | bytes 196616 | tf_op jit(solution)/shard_map/ppermute | solution.py:20
  76.4 4.3 %collective-permute-start.34 = (bf16[256,128]{1,0:T(8,128)(2,1)S(1)}, bf16[256,128]{1,0:T(8,128)(2,1)S(1)}, u32[]{:S(2)}, u32[]{:S(2)}) collective-permute-start(bf16[256,128]{1,0:T(8,128)(2,1)S(1)} %collective-permute-done.30.refs_3_), channel_id=1, source_target_pairs={{0,4},{4,0},{8,12},{12,8},{16,20},{20,16},{24,28},{28,24},{1,5},{5... | collective-permute-start | bytes 196616 | tf_op jit(solution)/shard_map/ppermute | solution.py:20
  77.8 4.3 %collective-permute-start.33 = (bf16[256,128]{1,0:T(8,128)(2,1)S(1)}, bf16[256,128]{1,0:T(8,128)(2,1)S(1)}, u32[]{:S(2)}, u32[]{:S(2)}) collective-permute-start(bf16[256,128]{1,0:T(8,128)(2,1)S(1)} %collective-permute-done.29.refs_2_), channel_id=1, source_target_pairs={{0,4},{4,0},{8,12},{12,8},{16,20},{20,16},{24,28},{28,24},{1,5},{5... | collective-permute-start | bytes 196616 | tf_op jit(solution)/shard_map/ppermute | solution.py:20
